TPU v7x, 32 devices: a whole 2x2x4 slice. The times are simulated.
32 devices in a mesh: outer: 8 (over z, x), inner: 4 (over y, core).
Axes of the slice: x: 2, y: 2, z: 4, core: 2. Of those that a mesh axis runs over, the one named last changes fastest.
Arguments:
- queries: bfloat16 [4096, 1024], P(('outer', 'inner')), may hold values from -6 to 6
- keys: bfloat16 [4096, 1024], P(('outer', 'inner')), may hold values from -6 to 6
- values: bfloat16 [4096, 1024], P(('outer', 'inner')), may hold values from -6 to 6
- head_gain: float32 [1024], replicated, may hold values from 0.1 to 1.9
Outputs:
- attended: bfloat16 [4096, 1024], P(('outer', 'inner'))
All inputs are finite; a program needn't handle non-finite values.
Results may differ from a plain program's by a relative error of at most 0.0034.
Values sent between devices are 32-bit elements; how exact they have to be, the bound alone decides.
No kernel may reach another device: no remote copies, remote signals or barrier semaphores. Data moves between devices by JAX's collectives and lax.ppermute only.
A program may use at most 64 MiB of HBM per device.

v0:
```python
import jax
import jax.numpy as jnp
from jax import lax
from jax.sharding import PartitionSpec as P

HEADS = 8
HEAD_DIM = 128


def entering(x, axis, combine, identity):
    length, mine = (lax.axis_size(axis), lax.axis_index(axis))
    everything = lax.all_gather(x, axis)
    start = jnp.broadcast_to(jnp.asarray(identity, x.dtype), x.shape)

    def lap(k, before):
        reached = k < mine
        new = combine(before, everything[k])
        return jnp.where(reached, new, before)

    return lax.fori_loop(0, length, lap, start)


def features(x):
    return (jax.nn.elu(x.astype(jnp.float32)) + 1.0).astype(jnp.bfloat16)


def add_states(earlier, later):
    return earlier + later


def per_device(queries, keys, values, head_gain):
    rows = queries.shape[0]
    fq = features(queries).reshape(rows, HEADS, HEAD_DIM)
    fk = features(keys).reshape(rows, HEADS, HEAD_DIM)
    vals = values.reshape(rows, HEADS, HEAD_DIM)
    own_state = jnp.einsum("thd,the->hde", fk, vals, preferred_element_type=jnp.float32)
    zero_state = jnp.zeros_like(own_state)
    before_group = entering(own_state, "inner", add_states, zero_state)
    share = lax.psum_scatter(own_state, "inner", scatter_dimension=1, tiled=True)
    share_zero = jnp.zeros_like(share)
    share_before = entering(share, "outer", add_states, share_zero)
    before_outer = lax.all_gather(share_before, "inner", axis=1, tiled=True)
    carried = before_outer + before_group
    carried_low = carried.astype(jnp.bfloat16)
    causal = jnp.arange(rows)[:, None] >= jnp.arange(rows)[None, :]
    scores = jnp.einsum("thd,shd->hts", fq, fk, preferred_element_type=jnp.float32)
    weights = jnp.where(causal[None], scores, 0.0).astype(jnp.bfloat16)
    intra = jnp.einsum("hts,she->the", weights, vals, preferred_element_type=jnp.float32)
    inter = jnp.einsum("thd,hde->the", fq, carried_low, preferred_element_type=jnp.float32)
    total = inter + intra
    meansq = jnp.mean(total * total, axis=-1, keepdims=True)
    normed = total * lax.rsqrt(meansq + 1e-06)
    return (normed.reshape(rows, HEADS * HEAD_DIM) * head_gain).astype(jnp.bfloat16)


def solution(mesh):
    return jax.shard_map(
        per_device,
        mesh=mesh,
        in_specs=(
            P(("outer", "inner"), None),
            P(("outer", "inner"), None),
            P(("outer", "inner"), None),
            P(),
        ),
        out_specs=P(("outer", "inner"), None),
        check_vma=False,
    )
```

profile of v0, /device:TPU:0, one launch (start us, length us, event | category | flops | bytes accessed | tf_op | source)
XLA Modules:
  0.0 116.1 jit_solution(12516536101482465656)
XLA Ops:
  6.5 1.2 %fusion.4 = bf16[128,1024]{1,0:T(8,128)(2,1)S(1)} fusion(bf16[128,1024]{1,0:T(8,128)(2,1)} %param.9), kind=kLoop, calls=%fused_computation.13 | loop fusion | flops 786432 | bytes 524288 | tf_op jit(solution)/shard_map/convert_element_type | solution.py:24
  7.9 1.1 copy.19
  9.1 1.1 fusion.18
  10.3 24.5 %reduce-scatter.2.cloned.1.call-done = f32[8,32,128]{2,1,0:T(8,128)} async-done(((f32[8,128,128]{2,1,0:T(8,128)}), f32[8,32,128]{2,1,0:T(8,128)}) %reduce-scatter.2.cloned.1.call-update) | async-done | bytes 131088 | tf_op jit(solution)/shard_map/reduce_scatter | solution.py:39
  34.8 0.7 all-gather.7.cloned.1.call-update
  35.5 0.5 convolution_bitcast_fusion
  36.1 41.2 %all-gather.5.cloned.1.call-done = f32[64,32,128]{2,1,0:T(8,128)} async-done(((f32[8,32,128]{2,1,0:T(8,128)}), f32[64,32,128]{2,1,0:T(8,128)}) %all-gather.5.cloned.1.call-update) | async-done | bytes 1048592 | tf_op jit(solution)/shard_map/all_gather | solution.py:12
  77.2 7.8 %while.28 = (s32[]{:T(128)}, f32[8,32,128]{2,1,0:T(8,128)S(1)}, s32[]{:T(128)}, f32[8,8,32,128]{3,2,1,0:T(8,128)}, s32[]{:T(128)}, /*index=5*/s32[]{:T(128)}) while((s32[]{:T(128)}, f32[8,32,128]{2,1,0:T(8,128)S(1)}, s32[]{:T(128)}, f32[8,8,32,128]{3,2,1,0:T(8,128)}, s32[]{:T(128)}, /*index=5*/s32[]{:T(128)}) %tuple.73), condition=%wide.region_2.3_spmd.clone, body=%wide.region_1.2_spmd.clone.sunk | while | flops 98308 | bytes 393317 | solution.py:20
  77.2 1.0 add_select_fusion.4
  78.2 1.0 add_select_fusion.4
  79.2 1.0 add_select_fusion.4
  80.2 1.0 add_select_fusion.4
  81.2 1.0 add_select_fusion.4
  82.1 1.0 add_select_fusion.4
  83.1 1.0 add_select_fusion.4
  84.1 1.0 add_select_fusion.4
  85.1 10.3 %all_gather.17 = f32[8,128,128]{2,1,0:T(8,128)S(1)} all-gather(f32[8,32,128]{2,1,0:T(8,128)S(1)} %get-tuple-element.163), channel_id=1, replica_groups=mesh['outer'=8,'inner'=4] {'inner'}, dimensions={1}, use_global_device_ids=true | all-gather | bytes 655360 | tf_op jit(solution)/shard_map/all_gather | solution.py:42
  95.4 7.7 %all-gather.7.cloned.1.call-done = f32[32,128,128]{2,1,0:T(8,128)} async-done(((f32[8,128,128]{2,1,0:T(8,128)}), f32[32,128,128]{2,1,0:T(8,128)}) %all-gather.7.cloned.1.call-update) | async-done | bytes 2097168 | tf_op jit(solution)/shard_map/all_gather | solution.py:12
  103.1 5.0 %while.29 = (s32[]{:T(128)}, f32[8,128,128]{2,1,0:T(8,128)S(1)}, s32[]{:T(128)}, f32[4,8,128,128]{3,2,1,0:T(8,128)}, s32[]{:T(128)}, /*index=5*/s32[]{:T(128)}) while((s32[]{:T(128)}, f32[8,128,128]{2,1,0:T(8,128)S(1)}, s32[]{:T(128)}, f32[4,8,128,128]{3,2,1,0:T(8,128)}, s32[]{:T(128)}, /*index=5*/s32[]{:T(128)}) %tuple.72), condition=%wide.region_4.5_spmd.clone, body=%wide.region_3.4_spmd.clone.sunk | while | flops 393220 | bytes 1572965 | solution.py:20
  103.1 1.2 %add_select_fusion.5 = f32[8,128,128]{2,1,0:T(8,128)S(1)} fusion(f32[8,128,128]{2,1,0:T(8,128)S(1)} %get-tuple-element.288, f32[4,8,128,128]{3,2,1,0:T(8,128)} %get-tuple-element.296, s32[]{:T(128)S(6)} %copy.40, pred[]{:T(512)S(6)} %compare.7, pred[]{:T(512)S(6)} %lt.43), kind=kLoop, calls=%fused_computation.1.clone.1 | loop fusion | flops 393216 | bytes 1572870 | tf_op jit(solution)/shard_map/while/body/eval_jaxpr/jit(_where)/select_n | solution.py:18
  104.3 1.2 %add_select_fusion.5 = f32[8,128,128]{2,1,0:T(8,128)S(1)} fusion(f32[8,128,128]{2,1,0:T(8,128)S(1)} %get-tuple-element.288, f32[4,8,128,128]{3,2,1,0:T(8,128)} %get-tuple-element.296, s32[]{:T(128)S(6)} %copy.40, pred[]{:T(512)S(6)} %compare.7, pred[]{:T(512)S(6)} %lt.43), kind=kLoop, calls=%fused_computation.1.clone.1 | loop fusion | flops 393216 | bytes 1572870 | tf_op jit(solution)/shard_map/while/body/eval_jaxpr/jit(_where)/select_n | solution.py:18
  105.6 1.2 %add_select_fusion.5 = f32[8,128,128]{2,1,0:T(8,128)S(1)} fusion(f32[8,128,128]{2,1,0:T(8,128)S(1)} %get-tuple-element.288, f32[4,8,128,128]{3,2,1,0:T(8,128)} %get-tuple-element.296, s32[]{:T(128)S(6)} %copy.40, pred[]{:T(512)S(6)} %compare.7, pred[]{:T(512)S(6)} %lt.43), kind=kLoop, calls=%fused_computation.1.clone.1 | loop fusion | flops 393216 | bytes 1572870 | tf_op jit(solution)/shard_map/while/body/eval_jaxpr/jit(_where)/select_n | solution.py:18
  106.8 1.2 %add_select_fusion.5 = f32[8,128,128]{2,1,0:T(8,128)S(1)} fusion(f32[8,128,128]{2,1,0:T(8,128)S(1)} %get-tuple-element.288, f32[4,8,128,128]{3,2,1,0:T(8,128)} %get-tuple-element.296, s32[]{:T(128)S(6)} %copy.40, pred[]{:T(512)S(6)} %compare.7, pred[]{:T(512)S(6)} %lt.43), kind=kLoop, calls=%fused_computation.1.clone.1 | loop fusion | flops 393216 | bytes 1572870 | tf_op jit(solution)/shard_map/while/body/eval_jaxpr/jit(_where)/select_n | solution.py:18
  108.8 0.7 multiply_convert_fusion
  (17 shorter events, 1.0 us)
Async XLA Ops:
  6.5 29.0 %copy-start = (bf16[128,1024]{1,0:T(8,128)(2,1)S(1)}, bf16[128,1024]{1,0:T(8,128)(2,1)}, u32[]{:S(2)}) copy-start(bf16[128,1024]{1,0:T(8,128)(2,1)} %param.8) | copy-start | bytes 786436
  6.5 28.2 %reduce-scatter.2.cloned.1.call-start = ((), (), s32[]{:S(2)}) async-start(), calls=%async_computation.1 | async-start | bytes 655360 | tf_op jit(solution)/shard_map/reduce_scatter | solution.py:39
  10.2 67.0 %all-gather.5.cloned.1.call-start = ((), (), s32[]{:S(2)}) async-start(), calls=%async_computation.2 | async-start | bytes 1179648 | tf_op jit(solution)/shard_map/all_gather | solution.py:12
  34.7 68.3 %all-gather.7.cloned.1.call-start = ((), (), s32[]{:S(2)}) async-start(), calls=%async_computation.3 | async-start | bytes 2621440 | tf_op jit(solution)/shard_map/all_gather | solution.py:12
  108.1 0.7 copy-start.1
Sparse Core Ops, SparseCore 0:
  10.3 24.3 reduce-scatter.1
  37.1 40.1 all-gather.4
  78.9 24.1 all-gather.6
where the time goes:
time: 117 us; the launch traced here: 116 us
  waiting for transfers between devices  74 us (63%)
  other arithmetic  14.6 us (12%)
  between operations  13.2 us (11%)
  blocking collectives  10.3 us (9%)
  matrix products  2.1 us (2%)
  local copies, waits for them, and re-layouts  1.5 us (1%)
    all_gather x2, waiting for transfers between devices, entering(): everything = lax.all_gather(x, axis)  48.9 us
    reduce_scatter x1, waiting for transfers between devices, per_device(): lax.psum_scatter(own_state, 'inner', scatter_dimension=1, tiled=True)  24.5 us
    select_n x12, other arithmetic, lap(): return jnp.where(reached, new, before)  12.6 us
    all_gather x1, blocking collectives, per_device(): before_outer = lax.all_gather(share_before, 'inner', axis=1, tiled=True)  10.3 us
  transfers between devices with their start and end apart: 3, of which 3 were waited for; matrix products, arithmetic and copies ran while one was open for 7% of the time, Pallas kernels for 0%

commit v1 on v0

v1 whole, which is shorter than its diff:
```python
import functools

import jax
import jax.numpy as jnp
from jax import lax
from jax.experimental import pallas as pl
from jax.experimental.pallas import tpu as pltpu
from jax.sharding import PartitionSpec as P

HEADS = 8
HEAD_DIM = 128
HALF = HEADS // 2
CHUNKS = 2
AXES = ("outer", "inner")


def features(x):
    x = x.astype(jnp.float32)
    return jnp.where(x > 0.0, x + 1.0, jnp.exp(jnp.minimum(x, 0.0))).astype(jnp.bfloat16)


def head_cols(h):
    return pl.ds(pl.multiple_of(h * HEAD_DIM, HEAD_DIM), HEAD_DIM)


def state_kernel(core_ref, k_ref, v_ref, mine_ref, theirs_ref):
    core = core_ref[0]
    for half, out in ((1, theirs_ref), (0, mine_ref)):
        for i in range(HALF):
            h = (core * HALF + half * HALF + i) % HEADS
            fk = features(k_ref[:, head_cols(h)])
            out[i] = lax.dot_general(
                fk, v_ref[:, head_cols(h)], (((0,), (0,)), ((), ())), preferred_element_type=jnp.float32
            )


def intra_kernel(q_ref, k_ref, v_ref, fq_ref, intra_ref):
    rows = q_ref.shape[0]
    causal = lax.broadcasted_iota(jnp.int32, (rows, rows), 0) >= lax.broadcasted_iota(jnp.int32, (rows, rows), 1)
    for h in range(HEADS):
        cols = slice(h * HEAD_DIM, (h + 1) * HEAD_DIM)
        fq = features(q_ref[:, cols])
        fk = features(k_ref[:, cols])
        fq_ref[:, cols] = fq
        scores = lax.dot_general(fq, fk, (((1,), (1,)), ((), ())), preferred_element_type=jnp.float32)
        weights = jnp.where(causal, scores, 0.0).astype(jnp.bfloat16)
        intra_ref[:, cols] = jnp.dot(weights, v_ref[:, cols], preferred_element_type=jnp.float32)


def final_kernel(core_ref, fq_ref, intra_ref, gain_ref, *refs):
    carried, out_ref = refs[:-1], refs[-1]
    core = core_ref[0]
    per = HALF // CHUNKS
    for half in range(2):
        for c in range(CHUNKS):
            for i in range(per):
                h = (core * HALF + half * HALF + c * per + i) % HEADS
                state = carried[half * CHUNKS + c][i].astype(jnp.bfloat16)
                cols = head_cols(h)
                total = intra_ref[:, cols] + jnp.dot(fq_ref[:, cols], state, preferred_element_type=jnp.float32)
                meansq = jnp.mean(total * total, axis=-1, keepdims=True)
                out_ref[:, cols] = (total * lax.rsqrt(meansq + 1e-06) * gain_ref[:, cols]).astype(jnp.bfloat16)


VMEM = pl.BlockSpec(memory_space=pltpu.VMEM)
SMEM = pl.BlockSpec(memory_space=pltpu.SMEM)


def plan(outer, inner):
    assert outer % 2 == 0 and inner % 2 == 0
    y, x, z = (2, inner // 2), (inner, 2), (2 * inner, outer // 2)
    return y, x, z


def steps_of(level, kind):
    stride, radix = level
    if kind == "ring":
        return [("ring", level, s) for s in range(1, radix)]
    if radix <= 4:
        return [("chain", level, k) for k in range(radix - 1)]
    shifts = [1]
    reach = 1
    while reach < radix - 1:
        shifts.append(reach)
        reach *= 2
    return [("scan", level, s) for s in shifts]


def targets(step, i):
    kind, (stride, radix), s = step
    d = i // stride % radix
    if kind == "ring":
        return i + ((d + s) % radix - d) * stride
    if kind == "chain":
        return i + stride if d == s else None
    return i + s * stride if d + s < radix else None


def per_device(outer, inner, queries, keys, values, head_gain):
    rows = queries.shape[0]
    n = outer * inner
    me = lax.axis_index("outer") * inner + lax.axis_index("inner")
    core = me % 2
    upward = core == 0
    core_arr = core.reshape(1).astype(jnp.int32)
    f32 = jnp.float32
    mine, theirs = pl.pallas_call(
        state_kernel,
        out_shape=[jax.ShapeDtypeStruct((HALF, HEAD_DIM, HEAD_DIM), f32)] * 2,
        in_specs=[SMEM, VMEM, VMEM],
        out_specs=[VMEM, VMEM],
        name="own_state",
    )(core_arr, keys, values)
    fq, intra = pl.pallas_call(
        intra_kernel,
        out_shape=[
            jax.ShapeDtypeStruct(queries.shape, jnp.bfloat16),
            jax.ShapeDtypeStruct(queries.shape, f32),
        ],
        in_specs=[VMEM] * 3,
        out_specs=[VMEM] * 2,
        cost_estimate=pl.CostEstimate(
            flops=4 * HEADS * rows * rows * HEAD_DIM, bytes_accessed=6 * queries.size * 2, transcendentals=queries.size * 2
        ),
        name="intra",
    )(queries, keys, values)

    y, x, z = plan(outer, inner)
    up = steps_of(y, "ring") + steps_of(x, "ring") + steps_of(z, "line")
    down = steps_of(z, "line") + steps_of(x, "ring") + steps_of(y, "ring")
    swap = [(i, i ^ 1) for i in range(n)]
    perms = []
    for a, b in zip(up, down, strict=True):
        pairs = [(i, targets((a, b)[i % 2], i)) for i in range(n)]
        perms.append([(i, t) for i, t in pairs if t is not None])

    def digit(level):
        return me // level[0] % level[1]

    per = HALF // CHUNKS
    own_parts, other_parts = [], []
    for c in range(CHUNKS):
        part = slice(c * per, (c + 1) * per)
        mine_c = mine[part]
        partner = lax.ppermute(theirs[part], AXES, swap)
        base = mine_c + partner
        zero = jnp.zeros_like(base)
        before, total, carry = zero, base, zero
        level_total, level_carry = total, carry
        prev_a = prev_b = None
        for j, (a, b) in enumerate(zip(up, down, strict=True)):
            if prev_a != a[:2]:
                level_total, prev_a = total, a[:2]
            if prev_b != b[:2]:
                level_carry, prev_b = carry, b[:2]
            if a[0] == "ring":
                msg_a = level_total
            elif a[0] == "chain" or a[2] == 1 and (j == 0 or up[j - 1][0] != "scan"):
                msg_a = carry + total
            else:
                msg_a = carry
            if b[0] == "ring":
                msg_b = level_carry + jnp.where(digit(b[1]) + b[2] < b[1][1], base, zero)
            elif b[0] == "chain" or b[2] == 1 and (j == 0 or down[j - 1][0] != "scan"):
                msg_b = carry + base
            else:
                msg_b = carry
            got = lax.ppermute(jnp.where(upward, msg_a, msg_b), AXES, perms[j])
            if a[0] == "ring":
                before = before + jnp.where(upward & (digit(a[1]) >= a[2]), got, zero)
                total = total + got
                carry_a = carry
            else:
                carry_a = carry + got
            carry = jnp.where(upward, carry_a, carry + got)
        before_chip = before + carry
        own_parts.append(before_chip + jnp.where(upward, zero, partner))
        other_parts.append(lax.ppermute(before_chip + jnp.where(upward, mine_c, zero), AXES, swap))

    return pl.pallas_call(
        final_kernel,
        out_shape=jax.ShapeDtypeStruct(queries.shape, jnp.bfloat16),
        in_specs=[SMEM] + [VMEM] * (3 + 2 * CHUNKS),
        out_specs=VMEM,
        name="attend",
    )(core_arr, fq, intra, head_gain.reshape(1, -1), *own_parts, *other_parts)


def solution(mesh):
    outer, inner = mesh.shape["outer"], mesh.shape["inner"]
    return jax.shard_map(
        functools.partial(per_device, outer, inner),
        mesh=mesh,
        in_specs=(
            P(AXES, None),
            P(AXES, None),
            P(AXES, None),
            P(),
        ),
        out_specs=P(AXES, None),
        check_vma=False,
    )
```

time: 117 us -> 45.1 us (0.39)
  the two profiles are of different devices: /device:TPU:0 before, /device:TPU:25 now
where the time goes in v1:
time: 45.1 us; the launch traced here: 44.7 us
  starting transfers between devices  23 us (51%)
  waiting for transfers between devices  10.8 us (24%)
  Pallas kernels  7.73 us (17%)
  local copies, waits for them, and re-layouts  1.67 us (4%)
  other arithmetic  1.22 us (3%)
    ppermute x10, starting transfers between devices, per_device(): got = lax.ppermute(jnp.where(upward, msg_a, msg_b), AXES, perms[j])  16.3 us
    ppermute x10, waiting for transfers between devices, per_device(): got = lax.ppermute(jnp.where(upward, msg_a, msg_b), AXES, perms[j])  9.04 us
    ppermute x2, starting transfers between devices, per_device(): lax.ppermute(before_chip + jnp.where(upward, mine_c, zero), AXES, swap)  5.91 us
    pallas_call x1, Pallas kernels, per_device(): pl.pallas_call(intra_kernel, out_shape=[jax.ShapeDtypeStruct(queries.shap...  3.27 us
    pallas_call x1, Pallas kernels, per_device(): pl.pallas_call(final_kernel, out_shape=jax.ShapeDtypeStruct(queries.shape...  2.37 us
    pallas_call x1, Pallas kernels, per_device(): pl.pallas_call(state_kernel, out_shape=[jax.ShapeDtypeStruct((HALF, HEAD_...  2.1 us
    ppermute x2, waiting for transfers between devices, per_device(): partner = lax.ppermute(theirs[part], AXES, swap)  1.27 us
    slice x1, local copies, waits for them, and re-layouts, per_device(): partner = lax.ppermute(theirs[part], AXES, swap)  1.03 us
  transfers between devices with their start and end apart: 14, of which 7 were waited for; matrix products, arithmetic and copies ran while one was open for 2% of the time, Pallas kernels for 7%

profile of v1, /device:TPU:25, one launch (start us, length us, event | category | flops | bytes accessed | tf_op | source)
XLA Modules:
  0.0 44.7 jit_solution(9622475300297604716)
XLA Ops:
  0.0 2.1 %own_state.1 = (f32[4,128,128]{2,1,0:T(8,128)}, f32[4,128,128]{2,1,0:T(8,128)}) custom-call(s32[1]{0:T(128)} %bitcast.core_ref, bf16[128,1024]{1,0:T(8,128)(2,1)} %k_ref.3, bf16[128,1024]{1,0:T(8,128)(2,1)} %v_ref.3), custom_call_target="tpu_custom_call" | custom-call | tf_op jit(solution)/shard_map/own_state/pallas_call | solution.py:107
  2.1 1.0 %fusion.4 = (f32[2,128,128]{2,1,0:T(8,128)S(1)}, f32[2,128,128]{2,1,0:T(8,128)S(1)}) fusion(f32[4,128,128]{2,1,0:T(8,128)} %get-tuple-element.12), kind=kLoop, calls=%fused_computation.22 | loop fusion | bytes 524288 | tf_op jit(solution)/shard_map/slice | solution.py:145
  3.1 0.7 %collective-permute-start.6 = (f32[2,128,128]{2,1,0:T(8,128)S(1)}, f32[2,128,128]{2,1,0:T(8,128)S(1)}, u32[]{:S(2)}, u32[]{:S(2)}) collective-permute-start(f32[2,128,128]{2,1,0:T(8,128)S(1)} %get-tuple-element.29), channel_id=1, source_target_pairs={{0,1},{1,0},{2,3},{3,2},{4,5},{5,4},{6,7},{7,6},{8,9},{9,8},{10,11... | collective-permute-start | bytes 393224 | tf_op jit(solution)/shard_map/ppermute | solution.py:145
  4.0 0.9 %collective-permute-done.6 = f32[2,128,128]{2,1,0:T(8,128)S(1)} collective-permute-done((f32[2,128,128]{2,1,0:T(8,128)S(1)}, f32[2,128,128]{2,1,0:T(8,128)S(1)}, u32[]{:S(2)}, u32[]{:S(2)}) %collective-permute-start.6) | collective-permute-done | bytes 131104 | tf_op jit(solution)/shard_map/ppermute | solution.py:145
  4.9 0.4 collective-permute-done
  5.3 0.7 %collective-permute-start.1 = (f32[2,128,128]{2,1,0:T(8,128)S(1)}, f32[2,128,128]{2,1,0:T(8,128)S(1)}, u32[]{:S(2)}, u32[]{:S(2)}) collective-permute-start(f32[2,128,128]{2,1,0:T(8,128)S(1)} %get-tuple-element.28), channel_id=1, source_target_pairs={{0,2},{1,9},{2,0},{3,11},{4,6},{5,13},{6,4},{7,15},{8,10},{10,8},{... | collective-permute-start | bytes 393224 | tf_op jit(solution)/shard_map/ppermute | solution.py:168
  6.0 0.7 %collective-permute-start.7 = (f32[2,128,128]{2,1,0:T(8,128)S(1)}, f32[2,128,128]{2,1,0:T(8,128)S(1)}, u32[]{:S(2)}, u32[]{:S(2)}) collective-permute-start(f32[2,128,128]{2,1,0:T(8,128)S(1)} %get-tuple-element.27), channel_id=1, source_target_pairs={{0,2},{1,9},{2,0},{3,11},{4,6},{5,13},{6,4},{7,15},{8,10},{10,8},{... | collective-permute-start | bytes 393224 | tf_op jit(solution)/shard_map/ppermute | solution.py:168
  6.7 0.7 %collective-permute-start.2 = (f32[2,128,128]{2,1,0:T(8,128)S(1)}, f32[2,128,128]{2,1,0:T(8,128)S(1)}, u32[]{:S(2)}, u32[]{:S(2)}) collective-permute-start(f32[2,128,128]{2,1,0:T(8,128)S(1)} %get-tuple-element.23), channel_id=1, source_target_pairs={{0,4},{2,6},{4,0},{6,2},{8,12},{9,17},{10,14},{11,19},{12,8},{13,2... | collective-permute-start | bytes 393224 | tf_op jit(solution)/shard_map/ppermute | solution.py:168
  7.4 0.7 %collective-permute-start.8 = (f32[2,128,128]{2,1,0:T(8,128)S(1)}, f32[2,128,128]{2,1,0:T(8,128)S(1)}, u32[]{:S(2)}, u32[]{:S(2)}) collective-permute-start(f32[2,128,128]{2,1,0:T(8,128)S(1)} %get-tuple-element.19), channel_id=1, source_target_pairs={{0,4},{2,6},{4,0},{6,2},{8,12},{9,17},{10,14},{11,19},{12,8},{13,2... | collective-permute-start | bytes 393224 | tf_op jit(solution)/shard_map/ppermute | solution.py:168
  8.2 1.3 %collective-permute-start.3 = (f32[2,128,128]{2,1,0:T(8,128)S(1)}, f32[2,128,128]{2,1,0:T(8,128)S(1)}, u32[]{:S(2)}, u32[]{:S(2)}) collective-permute-start(f32[2,128,128]{2,1,0:T(8,128)S(1)} %get-tuple-element.21), channel_id=1, source_target_pairs={{0,8},{2,10},{4,12},{6,14},{17,25},{19,27},{21,29},{23,31}} | collective-permute-start | bytes 393224 | tf_op jit(solution)/shard_map/ppermute | solution.py:168
  9.5 1.3 %collective-permute-start.9 = (f32[2,128,128]{2,1,0:T(8,128)S(1)}, f32[2,128,128]{2,1,0:T(8,128)S(1)}, u32[]{:S(2)}, u32[]{:S(2)}) collective-permute-start(f32[2,128,128]{2,1,0:T(8,128)S(1)} %get-tuple-element.17), channel_id=1, source_target_pairs={{0,8},{2,10},{4,12},{6,14},{17,25},{19,27},{21,29},{23,31}} | collective-permute-start | bytes 393224 | tf_op jit(solution)/shard_map/ppermute | solution.py:168
  10.8 8.4 %collective-permute-done.3 = f32[2,128,128]{2,1,0:T(8,128)S(1)} collective-permute-done((f32[2,128,128]{2,1,0:T(8,128)S(1)}, f32[2,128,128]{2,1,0:T(8,128)S(1)}, u32[]{:S(2)}, u32[]{:S(2)}) %collective-permute-start.3) | collective-permute-done | bytes 131104 | tf_op jit(solution)/shard_map/ppermute | solution.py:168
  19.3 3.1 %collective-permute-start.4 = (f32[2,128,128]{2,1,0:T(8,128)S(1)}, f32[2,128,128]{2,1,0:T(8,128)S(1)}, u32[]{:S(2)}, u32[]{:S(2)}) collective-permute-start(f32[2,128,128]{2,1,0:T(8,128)S(1)} %add_select_fusion.7), channel_id=1, source_target_pairs={{1,5},{3,7},{5,1},{7,3},{8,16},{9,13},{10,18},{11,15},{12,20},{13,... | collective-permute-start | bytes 393224 | tf_op jit(solution)/shard_map/ppermute | solution.py:168
  22.5 2.2 %collective-permute-start.10 = (f32[2,128,128]{2,1,0:T(8,128)S(1)}, f32[2,128,128]{2,1,0:T(8,128)S(1)}, u32[]{:S(2)}, u32[]{:S(2)}) collective-permute-start(f32[2,128,128]{2,1,0:T(8,128)S(1)} %add_select_fusion.3), channel_id=1, source_target_pairs={{1,5},{3,7},{5,1},{7,3},{8,16},{9,13},{10,18},{11,15},{12,20},{13,... | collective-permute-start | bytes 393224 | tf_op jit(solution)/shard_map/ppermute | solution.py:168
  24.6 0.3 collective-permute-done.4
  25.1 2.9 %collective-permute-start.5 = (f32[2,128,128]{2,1,0:T(8,128)S(1)}, f32[2,128,128]{2,1,0:T(8,128)S(1)}, u32[]{:S(2)}, u32[]{:S(2)}) collective-permute-start(f32[2,128,128]{2,1,0:T(8,128)S(1)} %add_select_fusion.6), channel_id=1, source_target_pairs={{1,3},{3,1},{5,7},{7,5},{9,11},{11,9},{13,15},{15,13},{16,24},{17,... | collective-permute-start | bytes 393224 | tf_op jit(solution)/shard_map/ppermute | solution.py:168
  28.3 2.9 %collective-permute-start.11 = (f32[2,128,128]{2,1,0:T(8,128)S(1)}, f32[2,128,128]{2,1,0:T(8,128)S(1)}, u32[]{:S(2)}, u32[]{:S(2)}) collective-permute-start(f32[2,128,128]{2,1,0:T(8,128)S(1)} %add_select_fusion.2), channel_id=1, source_target_pairs={{1,3},{3,1},{5,7},{7,5},{9,11},{11,9},{13,15},{15,13},{16,24},{17,... | collective-permute-start | bytes 393224 | tf_op jit(solution)/shard_map/ppermute | solution.py:168
  31.1 3.3 %intra.1 = (bf16[128,1024]{1,0:T(8,128)(2,1)}, f32[128,1024]{1,0:T(8,128)}) custom-call(bf16[128,1024]{1,0:T(8,128)(2,1)} %q_ref.1, bf16[128,1024]{1,0:T(8,128)(2,1)} %k_ref.3, bf16[128,1024]{1,0:T(8,128)(2,1)} %v_ref.3), custom_call_target="tpu_custom_call" | custom-call | flops 67108864 | bytes 1572864 | tf_op jit(solution)/shard_map/intra/pallas_call | solution.py:114
  34.5 5.8 %collective-permute-start.13 = (f32[2,128,128]{2,1,0:T(8,128)S(1)}, f32[2,128,128]{2,1,0:T(8,128)S(1)}, u32[]{:S(2)}, u32[]{:S(2)}) collective-permute-start(f32[2,128,128]{2,1,0:T(8,128)S(1)} %get-tuple-element.13), channel_id=1, source_target_pairs={{0,1},{1,0},{2,3},{3,2},{4,5},{5,4},{6,7},{7,6},{8,9},{9,8},{10,11... | collective-permute-start | bytes 393224 | tf_op jit(solution)/shard_map/ppermute | solution.py:178
  40.4 0.7 %select_add_fusion.2 = (f32[2,128,128]{2,1,0:T(8,128)}, f32[2,128,128]{2,1,0:T(8,128)}) fusion(f32[2,128,128]{2,1,0:T(8,128)S(1)} %get-tuple-element.14, f32[2,128,128]{2,1,0:T(8,128)S(1)} %collective-permute-done.6, pred[]{:T(512)S(6)} %eq.13, f32[2,128,128]{2,1,0:T(8,128)S(1)} %get-tuple-element.26, f32[2,128,128]{2,1,0:T(8,128)S(1)} %collective-permute-done), kind=kLoop, calls=%fused_computation.4 | loop fusion | flops 131072 | bytes 786433 | tf_op jit(solution)/shard_map/add | solution.py:177
  41.3 0.4 collective-permute-done.12.refs_2_
  41.7 0.3 copy-done.1
  42.0 0.3 copy-done.2
  42.3 2.4 %attend.1 = bf16[128,1024]{1,0:T(8,128)(2,1)} custom-call(s32[1]{0:T(128)} %bitcast.core_ref, bf16[128,1024]{1,0:T(8,128)(2,1)} %get-tuple-element.9.fq_ref, f32[128,1024]{1,0:T(8,128)} %get-tuple-element.10.intra_ref, f32[1,1024]{1,0:T(1,128)} %bitcast.2, f32[2,128,128]{2,1,0:T(8,128)} %get-tuple-element.32.refs_0_, ...), custom_call_target="tpu_custom_call" | custom-call | tf_op jit(solution)/shard_map/attend/pallas_call | solution.py:180
  (25 shorter events, 1.1 us)
Async XLA Ops:
  2.1 3.1 %copy-start = (f32[4,128,128]{2,1,0:T(8,128)S(1)}, f32[4,128,128]{2,1,0:T(8,128)}, u32[]{:S(2)}) copy-start(f32[4,128,128]{2,1,0:T(8,128)} %get-tuple-element.11) | copy-start | bytes 786436
  3.1 1.7 %collective-permute-start.6 = (f32[2,128,128]{2,1,0:T(8,128)S(1)}, f32[2,128,128]{2,1,0:T(8,128)S(1)}, u32[]{:S(2)}, u32[]{:S(2)}) collective-permute-start(f32[2,128,128]{2,1,0:T(8,128)S(1)} %get-tuple-element.29), channel_id=1, source_target_pairs={{0,1},{1,0},{2,3},{3,2},{4,5},{5,4},{6,7},{7,6},{8,9},{9,8},{10,11... | collective-permute-start | bytes 393224 | tf_op jit(solution)/shard_map/ppermute | solution.py:145
  3.9 1.3 %collective-permute-start = (f32[2,128,128]{2,1,0:T(8,128)S(1)}, f32[2,128,128]{2,1,0:T(8,128)S(1)}, u32[]{:S(2)}, u32[]{:S(2)}) collective-permute-start(f32[2,128,128]{2,1,0:T(8,128)S(1)} %get-tuple-element.30), channel_id=1, source_target_pairs={{0,1},{1,0},{2,3},{3,2},{4,5},{5,4},{6,7},{7,6},{8,9},{9,8},{10,11... | collective-permute-start | bytes 393224 | tf_op jit(solution)/shard_map/ppermute | solution.py:145
  5.3 1.4 %collective-permute-start.1 = (f32[2,128,128]{2,1,0:T(8,128)S(1)}, f32[2,128,128]{2,1,0:T(8,128)S(1)}, u32[]{:S(2)}, u32[]{:S(2)}) collective-permute-start(f32[2,128,128]{2,1,0:T(8,128)S(1)} %get-tuple-element.28), channel_id=1, source_target_pairs={{0,2},{1,9},{2,0},{3,11},{4,6},{5,13},{6,4},{7,15},{8,10},{10,8},{... | collective-permute-start | bytes 393224 | tf_op jit(solution)/shard_map/ppermute | solution.py:168
  6.0 1.4 %collective-permute-start.7 = (f32[2,128,128]{2,1,0:T(8,128)S(1)}, f32[2,128,128]{2,1,0:T(8,128)S(1)}, u32[]{:S(2)}, u32[]{:S(2)}) collective-permute-start(f32[2,128,128]{2,1,0:T(8,128)S(1)} %get-tuple-element.27), channel_id=1, source_target_pairs={{0,2},{1,9},{2,0},{3,11},{4,6},{5,13},{6,4},{7,15},{8,10},{10,8},{... | collective-permute-start | bytes 393224 | tf_op jit(solution)/shard_map/ppermute | solution.py:168
  6.7 1.4 %collective-permute-start.2 = (f32[2,128,128]{2,1,0:T(8,128)S(1)}, f32[2,128,128]{2,1,0:T(8,128)S(1)}, u32[]{:S(2)}, u32[]{:S(2)}) collective-permute-start(f32[2,128,128]{2,1,0:T(8,128)S(1)} %get-tuple-element.23), channel_id=1, source_target_pairs={{0,4},{2,6},{4,0},{6,2},{8,12},{9,17},{10,14},{11,19},{12,8},{13,2... | collective-permute-start | bytes 393224 | tf_op jit(solution)/shard_map/ppermute | solution.py:168
  7.4 2.0 %collective-permute-start.8 = (f32[2,128,128]{2,1,0:T(8,128)S(1)}, f32[2,128,128]{2,1,0:T(8,128)S(1)}, u32[]{:S(2)}, u32[]{:S(2)}) collective-permute-start(f32[2,128,128]{2,1,0:T(8,128)S(1)} %get-tuple-element.19), channel_id=1, source_target_pairs={{0,4},{2,6},{4,0},{6,2},{8,12},{9,17},{10,14},{11,19},{12,8},{13,2... | collective-permute-start | bytes 393224 | tf_op jit(solution)/shard_map/ppermute | solution.py:168
  8.2 11.1 %collective-permute-start.3 = (f32[2,128,128]{2,1,0:T(8,128)S(1)}, f32[2,128,128]{2,1,0:T(8,128)S(1)}, u32[]{:S(2)}, u32[]{:S(2)}) collective-permute-start(f32[2,128,128]{2,1,0:T(8,128)S(1)} %get-tuple-element.21), channel_id=1, source_target_pairs={{0,8},{2,10},{4,12},{6,14},{17,25},{19,27},{21,29},{23,31}} | collective-permute-start | bytes 393224 | tf_op jit(solution)/shard_map/ppermute | solution.py:168
  9.5 12.9 %collective-permute-start.9 = (f32[2,128,128]{2,1,0:T(8,128)S(1)}, f32[2,128,128]{2,1,0:T(8,128)S(1)}, u32[]{:S(2)}, u32[]{:S(2)}) collective-permute-start(f32[2,128,128]{2,1,0:T(8,128)S(1)} %get-tuple-element.17), channel_id=1, source_target_pairs={{0,8},{2,10},{4,12},{6,14},{17,25},{19,27},{21,29},{23,31}} | collective-permute-start | bytes 393224 | tf_op jit(solution)/shard_map/ppermute | solution.py:168
  19.3 5.7 %collective-permute-start.4 = (f32[2,128,128]{2,1,0:T(8,128)S(1)}, f32[2,128,128]{2,1,0:T(8,128)S(1)}, u32[]{:S(2)}, u32[]{:S(2)}) collective-permute-start(f32[2,128,128]{2,1,0:T(8,128)S(1)} %add_select_fusion.7), channel_id=1, source_target_pairs={{1,5},{3,7},{5,1},{7,3},{8,16},{9,13},{10,18},{11,15},{12,20},{13,... | collective-permute-start | bytes 393224 | tf_op jit(solution)/shard_map/ppermute | solution.py:168
  22.5 5.7 %collective-permute-start.10 = (f32[2,128,128]{2,1,0:T(8,128)S(1)}, f32[2,128,128]{2,1,0:T(8,128)S(1)}, u32[]{:S(2)}, u32[]{:S(2)}) collective-permute-start(f32[2,128,128]{2,1,0:T(8,128)S(1)} %add_select_fusion.3), channel_id=1, source_target_pairs={{1,5},{3,7},{5,1},{7,3},{8,16},{9,13},{10,18},{11,15},{12,20},{13,... | collective-permute-start | bytes 393224 | tf_op jit(solution)/shard_map/ppermute | solution.py:168
  25.1 9.3 %collective-permute-start.5 = (f32[2,128,128]{2,1,0:T(8,128)S(1)}, f32[2,128,128]{2,1,0:T(8,128)S(1)}, u32[]{:S(2)}, u32[]{:S(2)}) collective-permute-start(f32[2,128,128]{2,1,0:T(8,128)S(1)} %add_select_fusion.6), channel_id=1, source_target_pairs={{1,3},{3,1},{5,7},{7,5},{9,11},{11,9},{13,15},{15,13},{16,24},{17,... | collective-permute-start | bytes 393224 | tf_op jit(solution)/shard_map/ppermute | solution.py:168
  28.3 6.2 %collective-permute-start.11 = (f32[2,128,128]{2,1,0:T(8,128)S(1)}, f32[2,128,128]{2,1,0:T(8,128)S(1)}, u32[]{:S(2)}, u32[]{:S(2)}) collective-permute-start(f32[2,128,128]{2,1,0:T(8,128)S(1)} %add_select_fusion.2), channel_id=1, source_target_pairs={{1,3},{3,1},{5,7},{7,5},{9,11},{11,9},{13,15},{15,13},{16,24},{17,... | collective-permute-start | bytes 393224 | tf_op jit(solution)/shard_map/ppermute | solution.py:168
  34.5 6.8 %collective-permute-start.13 = (f32[2,128,128]{2,1,0:T(8,128)S(1)}, f32[2,128,128]{2,1,0:T(8,128)S(1)}, u32[]{:S(2)}, u32[]{:S(2)}) collective-permute-start(f32[2,128,128]{2,1,0:T(8,128)S(1)} %get-tuple-element.13), channel_id=1, source_target_pairs={{0,1},{1,0},{2,3},{3,2},{4,5},{5,4},{6,7},{7,6},{8,9},{9,8},{10,11... | collective-permute-start | bytes 393224 | tf_op jit(solution)/shard_map/ppermute | solution.py:178
  40.4 1.3 %collective-permute-start.12 = (f32[2,128,128]{2,1,0:T(8,128)S(1)}, f32[2,128,128]{2,1,0:T(8,128)S(1)}, u32[]{:S(2)}, u32[]{:S(2)}) collective-permute-start(f32[2,128,128]{2,1,0:T(8,128)S(1)} %get-tuple-element.25), channel_id=1, source_target_pairs={{0,1},{1,0},{2,3},{3,2},{4,5},{5,4},{6,7},{7,6},{8,9},{9,8},{10,11... | collective-permute-start | bytes 393224 | tf_op jit(solution)/shard_map/ppermute | solution.py:178
  41.3 0.7 %copy-start.1 = (f32[2,128,128]{2,1,0:T(8,128)}, f32[2,128,128]{2,1,0:T(8,128)S(1)}, u32[]{:S(2)}) copy-start(f32[2,128,128]{2,1,0:T(8,128)S(1)} %collective-permute-done.13.refs_3_) | copy-start | bytes 393220
  41.7 0.6 %copy-start.2 = (f32[2,128,128]{2,1,0:T(8,128)}, f32[2,128,128]{2,1,0:T(8,128)S(1)}, u32[]{:S(2)}) copy-start(f32[2,128,128]{2,1,0:T(8,128)S(1)} %collective-permute-done.12.refs_2_) | copy-start | bytes 393220

commit v2 on v1

v2 whole, which is shorter than its diff:
```python
import functools

import jax
import jax.numpy as jnp
from jax import lax
from jax.experimental import pallas as pl
from jax.experimental.pallas import tpu as pltpu
from jax.sharding import PartitionSpec as P

HEADS = 8
HEAD_DIM = 128
HALF = HEADS // 2
CHUNKS = 2
PER = HALF // CHUNKS
AXES = ("outer", "inner")


def features(x):
    x = x.astype(jnp.float32)
    return jnp.where(x > 0.0, x + 1.0, jnp.exp(jnp.minimum(x, 0.0))).astype(jnp.bfloat16)


def head_cols(h):
    return pl.ds(pl.multiple_of(h * HEAD_DIM, HEAD_DIM), HEAD_DIM)


def state_kernel(core_ref, k_ref, v_ref, *out_refs):
    core = core_ref[0]
    for half in (1, 0):
        for i in range(HALF):
            h = (core * HALF + half * HALF + i) % HEADS
            fk = features(k_ref[:, head_cols(h)])
            out_refs[half * CHUNKS + i // PER][i % PER] = lax.dot_general(
                fk, v_ref[:, head_cols(h)], (((0,), (0,)), ((), ())), preferred_element_type=jnp.float32
            )


def intra_kernel(q_ref, k_ref, v_ref, fq_ref, intra_ref):
    rows = q_ref.shape[0]
    causal = lax.broadcasted_iota(jnp.int32, (rows, rows), 0) >= lax.broadcasted_iota(jnp.int32, (rows, rows), 1)
    for h in range(HEADS):
        cols = slice(h * HEAD_DIM, (h + 1) * HEAD_DIM)
        fq = features(q_ref[:, cols])
        fk = features(k_ref[:, cols])
        fq_ref[:, cols] = fq
        scores = lax.dot_general(fq, fk, (((1,), (1,)), ((), ())), preferred_element_type=jnp.float32)
        weights = jnp.where(causal, scores, 0.0).astype(jnp.bfloat16)
        intra_ref[:, cols] = jnp.dot(weights, v_ref[:, cols], preferred_element_type=jnp.float32)


def final_kernel(core_ref, fq_ref, intra_ref, gain_ref, *refs):
    carried, out_ref = refs[:-1], refs[-1]
    core = core_ref[0]
    for half in range(2):
        for c in range(CHUNKS):
            for i in range(PER):
                h = (core * HALF + half * HALF + c * PER + i) % HEADS
                state = carried[half * CHUNKS + c][i].astype(jnp.bfloat16)
                cols = head_cols(h)
                total = intra_ref[:, cols] + jnp.dot(fq_ref[:, cols], state, preferred_element_type=jnp.float32)
                meansq = jnp.mean(total * total, axis=-1, keepdims=True)
                out_ref[:, cols] = (total * lax.rsqrt(meansq + 1e-06) * gain_ref[:, cols]).astype(jnp.bfloat16)


VMEM = pl.BlockSpec(memory_space=pltpu.VMEM)
SMEM = pl.BlockSpec(memory_space=pltpu.SMEM)
PARAMS = pltpu.CompilerParams(vmem_limit_bytes=8 * 1024 * 1024)


def levels_of(stride, extent):
    levels = []
    while extent > 1:
        radix = next(r for r in range(2, extent + 1) if extent % r == 0)
        levels.append((stride, radix))
        stride, extent = stride * radix, extent // radix
    return levels


def steps_of(levels):
    return [(stride, radix, shift) for stride, radix in levels for shift in range(1, radix)]


def target(step, i):
    stride, radix, shift = step
    digit = i // stride % radix
    return i + ((digit + shift) % radix - digit) * stride


def per_device(outer, inner, queries, keys, values, head_gain):
    rows = queries.shape[0]
    n = outer * inner
    me = lax.axis_index("outer") * inner + lax.axis_index("inner")
    core = me % 2
    even = core == 0
    core_arr = core.reshape(1).astype(jnp.int32)
    f32 = jnp.float32
    part = jax.ShapeDtypeStruct((PER, HEAD_DIM, HEAD_DIM), f32)
    states = pl.pallas_call(
        state_kernel,
        out_shape=[part] * (2 * CHUNKS),
        in_specs=[SMEM, VMEM, VMEM],
        out_specs=[VMEM] * (2 * CHUNKS),
        compiler_params=PARAMS,
        name="own_state",
    )(core_arr, keys, values)
    fq, intra = pl.pallas_call(
        intra_kernel,
        out_shape=[
            jax.ShapeDtypeStruct(queries.shape, jnp.bfloat16),
            jax.ShapeDtypeStruct(queries.shape, f32),
        ],
        in_specs=[VMEM] * 3,
        out_specs=[VMEM] * 2,
        compiler_params=PARAMS,
        cost_estimate=pl.CostEstimate(
            flops=4 * HEADS * rows * rows * HEAD_DIM, bytes_accessed=6 * queries.size * 2, transcendentals=queries.size * 2
        ),
        name="intra",
    )(queries, keys, values)

    up_levels = levels_of(2, inner // 2) + levels_of(inner, outer)
    ups = steps_of(up_levels)
    downs = steps_of(up_levels[::-1])
    swap = [(i, i ^ 1) for i in range(n)]

    def digit(step):
        return me // step[0] % step[1]

    def to_swap(x):
        return lax.ppermute(x, AXES, swap)

    mine, theirs = states[:CHUNKS], states[CHUNKS:]
    partner = [to_swap(x) for x in theirs]
    own_parts, other_parts = [], []
    for c in range(CHUNKS):
        base = mine[c] + partner[c]
        zero = jnp.zeros_like(base)
        before, total = zero, base
        for j, (up, down) in enumerate(zip(ups, downs, strict=True)):
            if up[2] == 1:
                level_total = total
            if down[2] == 1:
                level_before = before
            higher = digit(down) + down[2] < down[1]
            message = jnp.where(even, level_total, level_before + jnp.where(higher, base, zero))
            perm = [(i, target(down if i % 2 else up, i)) for i in range(n)]
            got = lax.ppermute(message, AXES, perm)
            before = before + jnp.where(even & (digit(up) < up[2]), zero, got)
            total = total + got
        own_parts.append(before + jnp.where(even, zero, partner[c]))
        other_parts.append(to_swap(before + jnp.where(even, mine[c], zero)))

    return pl.pallas_call(
        final_kernel,
        out_shape=jax.ShapeDtypeStruct(queries.shape, jnp.bfloat16),
        in_specs=[SMEM] + [VMEM] * (3 + 2 * CHUNKS),
        out_specs=VMEM,
        compiler_params=PARAMS,
        name="attend",
    )(core_arr, fq, intra, head_gain.reshape(1, -1), *own_parts, *other_parts)


def solution(mesh):
    outer, inner = mesh.shape["outer"], mesh.shape["inner"]
    assert inner % 2 == 0
    return jax.shard_map(
        functools.partial(per_device, outer, inner),
        mesh=mesh,
        in_specs=(
            P(AXES, None),
            P(AXES, None),
            P(AXES, None),
            P(),
        ),
        out_specs=P(AXES, None),
        check_vma=False,
    )
```

time: 45.1 us -> 34.7 us (0.77)
  the two profiles are of different devices: /device:TPU:25 before, /device:TPU:0 now
where the time goes in v2:
time: 34.7 us; the launch traced here: 34.5 us
  starting transfers between devices  15.9 us (46%)
  waiting for transfers between devices  12.4 us (36%)
  local copies, waits for them, and re-layouts  2.96 us (9%)
  Pallas kernels  2.77 us (8%)
  other arithmetic  0.38 us (1%)
    ppermute x8, starting transfers between devices, per_device(): got = lax.ppermute(message, AXES, perm)  15.2 us
    ppermute x8, waiting for transfers between devices, per_device(): got = lax.ppermute(message, AXES, perm)  11.1 us
    unnamed x12, local copies, waits for them, and re-layouts  2.96 us
    pallas_call x1, Pallas kernels, per_device(): pl.pallas_call(intra_kernel, out_shape=[jax.ShapeDtypeStruct(queries.shap...  1.35 us
    ppermute x4, waiting for transfers between devices, to_swap(): return lax.ppermute(x, AXES, swap)  1.27 us
    pallas_call x1, Pallas kernels, per_device(): pl.pallas_call(final_kernel, out_shape=jax.ShapeDtypeStruct(queries.shape...  1.09 us
    ppermute x4, starting transfers between devices, to_swap(): return lax.ppermute(x, AXES, swap)  0.74 us
  transfers between devices with their start and end apart: 12, of which 6 were waited for; matrix products, arithmetic and copies ran while one was open for 1% of the time, Pallas kernels for 4%

profile of v2, /device:TPU:0, one launch (start us, length us, event | category | flops | bytes accessed | tf_op | source)
XLA Modules:
  0.0 34.5 jit_solution(5532998661187436357)
XLA Ops:
  0.0 0.9 %copy-done = bf16[128,1024]{1,0:T(8,128)(2,1)S(1)} copy-done((bf16[128,1024]{1,0:T(8,128)(2,1)S(1)}, bf16[128,1024]{1,0:T(8,128)(2,1)}, u32[]{:S(2)}) %copy-start) | copy-done | bytes 262168
  1.0 0.9 %copy-done.2 = bf16[128,1024]{1,0:T(8,128)(2,1)S(1)} copy-done((bf16[128,1024]{1,0:T(8,128)(2,1)S(1)}, bf16[128,1024]{1,0:T(8,128)(2,1)}, u32[]{:S(2)}) %copy-start.2) | copy-done | bytes 262168
  1.9 0.3 own_state.1
  2.2 0.5 %collective-permute-start.5 = (f32[2,128,128]{2,1,0:T(8,128)S(1)}, f32[2,128,128]{2,1,0:T(8,128)S(1)}, u32[]{:S(2)}, u32[]{:S(2)}) collective-permute-start(f32[2,128,128]{2,1,0:T(8,128)S(1)} %get-tuple-element.16), channel_id=1, source_target_pairs={{0,1},{1,0},{2,3},{3,2},{4,5},{5,4},{6,7},{7,6},{8,9},{9,8},{10,11... | collective-permute-start | bytes 393224 | tf_op jit(solution)/shard_map/ppermute | solution.py:130
  2.8 0.1 collective-permute-start
  2.9 0.1 copy-done.3
  2.9 0.9 %copy-done.4 = bf16[128,1024]{1,0:T(8,128)(2,1)S(1)} copy-done((bf16[128,1024]{1,0:T(8,128)(2,1)S(1)}, bf16[128,1024]{1,0:T(8,128)(2,1)}, u32[]{:S(2)}) %copy-start.4) | copy-done | bytes 262168
  3.9 1.4 %intra.1 = (bf16[128,1024]{1,0:T(8,128)(2,1)S(1)}, f32[128,1024]{1,0:T(8,128)S(1)}) custom-call(bf16[128,1024]{1,0:T(8,128)(2,1)S(1)} %copy-done.4, bf16[128,1024]{1,0:T(8,128)(2,1)S(1)} %copy-done.1, bf16[128,1024]{1,0:T(8,128)(2,1)S(1)} %copy-done.3), custom_call_target="tpu_custom_call" | custom-call | flops 67108864 | bytes 1572864 | tf_op jit(solution)/shard_map/intra/pallas_call | solution.py:106
  5.3 3.0 %collective-permute-start.6 = (f32[2,128,128]{2,1,0:T(8,128)S(1)}, f32[2,128,128]{2,1,0:T(8,128)S(1)}, u32[]{:S(2)}, u32[]{:S(2)}) collective-permute-start(f32[2,128,128]{2,1,0:T(8,128)S(1)} %get-tuple-element.26), channel_id=1, source_target_pairs={{0,2},{1,17},{2,0},{3,19},{4,6},{5,21},{6,4},{7,23},{8,10},{9,25},... | collective-permute-start | bytes 393224 | tf_op jit(solution)/shard_map/ppermute | solution.py:147
  8.3 0.1 collective-permute-start.1
  8.4 2.8 %collective-permute-done.6 = f32[2,128,128]{2,1,0:T(8,128)S(1)} collective-permute-done((f32[2,128,128]{2,1,0:T(8,128)S(1)}, f32[2,128,128]{2,1,0:T(8,128)S(1)}, u32[]{:S(2)}, u32[]{:S(2)}) %collective-permute-start.6) | collective-permute-done | bytes 131104 | tf_op jit(solution)/shard_map/ppermute | solution.py:147
  11.3 2.1 %collective-permute-start.7 = (f32[2,128,128]{2,1,0:T(8,128)S(1)}, f32[2,128,128]{2,1,0:T(8,128)S(1)}, u32[]{:S(2)}, u32[]{:S(2)}) collective-permute-start(f32[2,128,128]{2,1,0:T(8,128)S(1)} %get-tuple-element.24), channel_id=1, source_target_pairs={{0,4},{1,9},{2,6},{3,11},{4,0},{5,13},{6,2},{7,15},{8,12},{9,1},{1... | collective-permute-start | bytes 393224 | tf_op jit(solution)/shard_map/ppermute | solution.py:147
  13.4 1.6 %collective-permute-start.2 = (f32[2,128,128]{2,1,0:T(8,128)S(1)}, f32[2,128,128]{2,1,0:T(8,128)S(1)}, u32[]{:S(2)}, u32[]{:S(2)}) collective-permute-start(f32[2,128,128]{2,1,0:T(8,128)S(1)} %get-tuple-element.31), channel_id=1, source_target_pairs={{0,4},{1,9},{2,6},{3,11},{4,0},{5,13},{6,2},{7,15},{8,12},{9,1},{1... | collective-permute-start | bytes 393224 | tf_op jit(solution)/shard_map/ppermute | solution.py:147
  15.0 1.4 %collective-permute-done.7 = f32[2,128,128]{2,1,0:T(8,128)S(1)} collective-permute-done((f32[2,128,128]{2,1,0:T(8,128)S(1)}, f32[2,128,128]{2,1,0:T(8,128)S(1)}, u32[]{:S(2)}, u32[]{:S(2)}) %collective-permute-start.7) | collective-permute-done | bytes 131104 | tf_op jit(solution)/shard_map/ppermute | solution.py:147
  16.4 2.1 %collective-permute-start.8 = (f32[2,128,128]{2,1,0:T(8,128)S(1)}, f32[2,128,128]{2,1,0:T(8,128)S(1)}, u32[]{:S(2)}, u32[]{:S(2)}) collective-permute-start(f32[2,128,128]{2,1,0:T(8,128)S(1)} %get-tuple-element.21), channel_id=1, source_target_pairs={{0,8},{1,5},{2,10},{3,7},{4,12},{5,1},{6,14},{7,3},{8,0},{9,13},{1... | collective-permute-start | bytes 393224 | tf_op jit(solution)/shard_map/ppermute | solution.py:147
  18.6 1.6 %collective-permute-start.3 = (f32[2,128,128]{2,1,0:T(8,128)S(1)}, f32[2,128,128]{2,1,0:T(8,128)S(1)}, u32[]{:S(2)}, u32[]{:S(2)}) collective-permute-start(f32[2,128,128]{2,1,0:T(8,128)S(1)} %get-tuple-element.28), channel_id=1, source_target_pairs={{0,8},{1,5},{2,10},{3,7},{4,12},{5,1},{6,14},{7,3},{8,0},{9,13},{1... | collective-permute-start | bytes 393224 | tf_op jit(solution)/shard_map/ppermute | solution.py:147
  20.1 1.3 %collective-permute-done.8 = f32[2,128,128]{2,1,0:T(8,128)S(1)} collective-permute-done((f32[2,128,128]{2,1,0:T(8,128)S(1)}, f32[2,128,128]{2,1,0:T(8,128)S(1)}, u32[]{:S(2)}, u32[]{:S(2)}) %collective-permute-start.8) | collective-permute-done | bytes 131104 | tf_op jit(solution)/shard_map/ppermute | solution.py:147
  21.5 3.1 %collective-permute-start.9 = (f32[2,128,128]{2,1,0:T(8,128)S(1)}, f32[2,128,128]{2,1,0:T(8,128)S(1)}, u32[]{:S(2)}, u32[]{:S(2)}) collective-permute-start(f32[2,128,128]{2,1,0:T(8,128)S(1)} %add_select_fusion), channel_id=1, source_target_pairs={{0,16},{1,3},{2,18},{3,1},{4,20},{5,7},{6,22},{7,5},{8,24},{9,11},... | collective-permute-start | bytes 393224 | tf_op jit(solution)/shard_map/ppermute | solution.py:147
  24.6 1.6 %collective-permute-start.4 = (f32[2,128,128]{2,1,0:T(8,128)S(1)}, f32[2,128,128]{2,1,0:T(8,128)S(1)}, u32[]{:S(2)}, u32[]{:S(2)}) collective-permute-start(f32[2,128,128]{2,1,0:T(8,128)S(1)} %add_select_fusion.3), channel_id=1, source_target_pairs={{0,16},{1,3},{2,18},{3,1},{4,20},{5,7},{6,22},{7,5},{8,24},{9,11},... | collective-permute-start | bytes 393224 | tf_op jit(solution)/shard_map/ppermute | solution.py:147
  26.3 1.3 %collective-permute-done.9 = f32[2,128,128]{2,1,0:T(8,128)S(1)} collective-permute-done((f32[2,128,128]{2,1,0:T(8,128)S(1)}, f32[2,128,128]{2,1,0:T(8,128)S(1)}, u32[]{:S(2)}, u32[]{:S(2)}) %collective-permute-start.9) | collective-permute-done | bytes 131104 | tf_op jit(solution)/shard_map/ppermute | solution.py:147
  27.6 0.1 collective-permute-start.11
  27.7 4.3 %collective-permute-done.4 = f32[2,128,128]{2,1,0:T(8,128)S(1)} collective-permute-done((f32[2,128,128]{2,1,0:T(8,128)S(1)}, f32[2,128,128]{2,1,0:T(8,128)S(1)}, u32[]{:S(2)}, u32[]{:S(2)}) %collective-permute-start.4) | collective-permute-done | bytes 131104 | tf_op jit(solution)/shard_map/ppermute | solution.py:147
  32.2 1.3 %collective-permute-done.10.refs_2_ = f32[2,128,128]{2,1,0:T(8,128)S(1)} collective-permute-done((f32[2,128,128]{2,1,0:T(8,128)S(1)}, f32[2,128,128]{2,1,0:T(8,128)S(1)}, u32[]{:S(2)}, u32[]{:S(2)}) %collective-permute-start.10) | collective-permute-done | bytes 131104 | tf_op jit(solution)/shard_map/ppermute | solution.py:130
  33.4 1.1 %attend.1 = bf16[128,1024]{1,0:T(8,128)(2,1)} custom-call(s32[1]{0:T(128)} %bitcast.core_ref, bf16[128,1024]{1,0:T(8,128)(2,1)S(1)} %get-tuple-element.11.fq_ref, f32[128,1024]{1,0:T(8,128)S(1)} %get-tuple-element.12.intra_ref, f32[1,1024]{1,0:T(1,128)S(1)} %bitcast.2, f32[2,128,128]{2,1,0:T(8,128)S(1)} %select_add_fusion.6.refs_0_, ...), custom_call_target="tpu_custom_call" | custom-call | tf_op jit(solution)/shard_map/attend/pallas_call | solution.py:153
  (27 shorter events, 0.5 us)
Async XLA Ops:
  0.0 0.9 %copy-start = (bf16[128,1024]{1,0:T(8,128)(2,1)S(1)}, bf16[128,1024]{1,0:T(8,128)(2,1)}, u32[]{:S(2)}) copy-start(bf16[128,1024]{1,0:T(8,128)(2,1)} %k_ref.3) | copy-start | bytes 786436
  1.0 0.9 %copy-start.2 = (bf16[128,1024]{1,0:T(8,128)(2,1)S(1)}, bf16[128,1024]{1,0:T(8,128)(2,1)}, u32[]{:S(2)}) copy-start(bf16[128,1024]{1,0:T(8,128)(2,1)} %v_ref.3) | copy-start | bytes 786436
  1.9 0.9 %copy-start.1 = (bf16[128,1024]{1,0:T(8,128)(2,1)S(1)}, bf16[128,1024]{1,0:T(8,128)(2,1)}, u32[]{:S(2)}) copy-start(bf16[128,1024]{1,0:T(8,128)(2,1)} %k_ref.3) | copy-start | bytes 786436
  1.9 1.0 %copy-start.3 = (bf16[128,1024]{1,0:T(8,128)(2,1)S(1)}, bf16[128,1024]{1,0:T(8,128)(2,1)}, u32[]{:S(2)}) copy-start(bf16[128,1024]{1,0:T(8,128)(2,1)} %v_ref.3) | copy-start | bytes 786436
  2.2 3.0 %collective-permute-start.5 = (f32[2,128,128]{2,1,0:T(8,128)S(1)}, f32[2,128,128]{2,1,0:T(8,128)S(1)}, u32[]{:S(2)}, u32[]{:S(2)}) collective-permute-start(f32[2,128,128]{2,1,0:T(8,128)S(1)} %get-tuple-element.16), channel_id=1, source_target_pairs={{0,1},{1,0},{2,3},{3,2},{4,5},{5,4},{6,7},{7,6},{8,9},{9,8},{10,11... | collective-permute-start | bytes 393224 | tf_op jit(solution)/shard_map/ppermute | solution.py:130
  2.8 5.6 %collective-permute-start = (f32[2,128,128]{2,1,0:T(8,128)S(1)}, f32[2,128,128]{2,1,0:T(8,128)S(1)}, u32[]{:S(2)}, u32[]{:S(2)}) collective-permute-start(f32[2,128,128]{2,1,0:T(8,128)S(1)} %get-tuple-element.14), channel_id=1, source_target_pairs={{0,1},{1,0},{2,3},{3,2},{4,5},{5,4},{6,7},{7,6},{8,9},{9,8},{10,11... | collective-permute-start | bytes 393224 | tf_op jit(solution)/shard_map/ppermute | solution.py:130
  2.9 0.9 %copy-start.4 = (bf16[128,1024]{1,0:T(8,128)(2,1)S(1)}, bf16[128,1024]{1,0:T(8,128)(2,1)}, u32[]{:S(2)}) copy-start(bf16[128,1024]{1,0:T(8,128)(2,1)} %q_ref.1) | copy-start | bytes 786436
  5.3 6.0 %collective-permute-start.6 = (f32[2,128,128]{2,1,0:T(8,128)S(1)}, f32[2,128,128]{2,1,0:T(8,128)S(1)}, u32[]{:S(2)}, u32[]{:S(2)}) collective-permute-start(f32[2,128,128]{2,1,0:T(8,128)S(1)} %get-tuple-element.26), channel_id=1, source_target_pairs={{0,2},{1,17},{2,0},{3,19},{4,6},{5,21},{6,4},{7,23},{8,10},{9,25},... | collective-permute-start | bytes 393224 | tf_op jit(solution)/shard_map/ppermute | solution.py:147
  8.3 5.0 %collective-permute-start.1 = (f32[2,128,128]{2,1,0:T(8,128)S(1)}, f32[2,128,128]{2,1,0:T(8,128)S(1)}, u32[]{:S(2)}, u32[]{:S(2)}) collective-permute-start(f32[2,128,128]{2,1,0:T(8,128)S(1)} %get-tuple-element.33), channel_id=1, source_target_pairs={{0,2},{1,17},{2,0},{3,19},{4,6},{5,21},{6,4},{7,23},{8,10},{9,25},... | collective-permute-start | bytes 393224 | tf_op jit(solution)/shard_map/ppermute | solution.py:147
  11.3 5.0 %collective-permute-start.7 = (f32[2,128,128]{2,1,0:T(8,128)S(1)}, f32[2,128,128]{2,1,0:T(8,128)S(1)}, u32[]{:S(2)}, u32[]{:S(2)}) collective-permute-start(f32[2,128,128]{2,1,0:T(8,128)S(1)} %get-tuple-element.24), channel_id=1, source_target_pairs={{0,4},{1,9},{2,6},{3,11},{4,0},{5,13},{6,2},{7,15},{8,12},{9,1},{1... | collective-permute-start | bytes 393224 | tf_op jit(solution)/shard_map/ppermute | solution.py:147
  13.4 5.1 %collective-permute-start.2 = (f32[2,128,128]{2,1,0:T(8,128)S(1)}, f32[2,128,128]{2,1,0:T(8,128)S(1)}, u32[]{:S(2)}, u32[]{:S(2)}) collective-permute-start(f32[2,128,128]{2,1,0:T(8,128)S(1)} %get-tuple-element.31), channel_id=1, source_target_pairs={{0,4},{1,9},{2,6},{3,11},{4,0},{5,13},{6,2},{7,15},{8,12},{9,1},{1... | collective-permute-start | bytes 393224 | tf_op jit(solution)/shard_map/ppermute | solution.py:147
  16.4 5.1 %collective-permute-start.8 = (f32[2,128,128]{2,1,0:T(8,128)S(1)}, f32[2,128,128]{2,1,0:T(8,128)S(1)}, u32[]{:S(2)}, u32[]{:S(2)}) collective-permute-start(f32[2,128,128]{2,1,0:T(8,128)S(1)} %get-tuple-element.21), channel_id=1, source_target_pairs={{0,8},{1,5},{2,10},{3,7},{4,12},{5,1},{6,14},{7,3},{8,0},{9,13},{1... | collective-permute-start | bytes 393224 | tf_op jit(solution)/shard_map/ppermute | solution.py:147
  18.6 6.0 %collective-permute-start.3 = (f32[2,128,128]{2,1,0:T(8,128)S(1)}, f32[2,128,128]{2,1,0:T(8,128)S(1)}, u32[]{:S(2)}, u32[]{:S(2)}) collective-permute-start(f32[2,128,128]{2,1,0:T(8,128)S(1)} %get-tuple-element.28), channel_id=1, source_target_pairs={{0,8},{1,5},{2,10},{3,7},{4,12},{5,1},{6,14},{7,3},{8,0},{9,13},{1... | collective-permute-start | bytes 393224 | tf_op jit(solution)/shard_map/ppermute | solution.py:147
  21.5 6.1 %collective-permute-start.9 = (f32[2,128,128]{2,1,0:T(8,128)S(1)}, f32[2,128,128]{2,1,0:T(8,128)S(1)}, u32[]{:S(2)}, u32[]{:S(2)}) collective-permute-start(f32[2,128,128]{2,1,0:T(8,128)S(1)} %add_select_fusion), channel_id=1, source_target_pairs={{0,16},{1,3},{2,18},{3,1},{4,20},{5,7},{6,22},{7,5},{8,24},{9,11},... | collective-permute-start | bytes 393224 | tf_op jit(solution)/shard_map/ppermute | solution.py:147
  24.6 7.3 %collective-permute-start.4 = (f32[2,128,128]{2,1,0:T(8,128)S(1)}, f32[2,128,128]{2,1,0:T(8,128)S(1)}, u32[]{:S(2)}, u32[]{:S(2)}) collective-permute-start(f32[2,128,128]{2,1,0:T(8,128)S(1)} %add_select_fusion.3), channel_id=1, source_target_pairs={{0,16},{1,3},{2,18},{3,1},{4,20},{5,7},{6,22},{7,5},{8,24},{9,11},... | collective-permute-start | bytes 393224 | tf_op jit(solution)/shard_map/ppermute | solution.py:147
  27.6 4.6 %collective-permute-start.11 = (f32[2,128,128]{2,1,0:T(8,128)S(1)}, f32[2,128,128]{2,1,0:T(8,128)S(1)}, u32[]{:S(2)}, u32[]{:S(2)}) collective-permute-start(f32[2,128,128]{2,1,0:T(8,128)S(1)} %get-tuple-element.17), channel_id=1, source_target_pairs={{0,1},{1,0},{2,3},{3,2},{4,5},{5,4},{6,7},{7,6},{8,9},{9,8},{10,11... | collective-permute-start | bytes 393224 | tf_op jit(solution)/shard_map/ppermute | solution.py:130
  32.0 1.4 %collective-permute-start.10 = (f32[2,128,128]{2,1,0:T(8,128)S(1)}, f32[2,128,128]{2,1,0:T(8,128)S(1)}, u32[]{:S(2)}, u32[]{:S(2)}) collective-permute-start(f32[2,128,128]{2,1,0:T(8,128)S(1)} %get-tuple-element.19), channel_id=1, source_target_pairs={{0,1},{1,0},{2,3},{3,2},{4,5},{5,4},{6,7},{7,6},{8,9},{9,8},{10,11... | collective-permute-start | bytes 393224 | tf_op jit(solution)/shard_map/ppermute | solution.py:130
  32.1 1.3 %copy-start.5 = (f32[1024]{0:T(1024)S(1)}, f32[1024]{0:T(1024)}, u32[]{:S(2)}) copy-start(f32[1024]{0:T(1024)} %param.7) | copy-start | bytes 12292

commit v3 on v2

--- a/solution.py
+++ b/solution.py
@@ -24,7 +24,16 @@
     return pl.ds(pl.multiple_of(h * HEAD_DIM, HEAD_DIM), HEAD_DIM)
 
 
-def state_kernel(core_ref, k_ref, v_ref, *out_refs):
+def state_kernel(core_ref, k_hbm, v_hbm, *refs):
+    out_refs, (k_ref, v_ref, sems) = refs[: 2 * CHUNKS], refs[2 * CHUNKS :]
+    copies = [
+        pltpu.make_async_copy(k_hbm, k_ref, sems.at[0]),
+        pltpu.make_async_copy(v_hbm, v_ref, sems.at[1]),
+    ]
+    for copy in copies:
+        copy.start()
+    for copy in copies:
+        copy.wait()
     core = core_ref[0]
     for half in (1, 0):
         for i in range(HALF):
@@ -35,7 +44,8 @@
             )
 
 
-def intra_kernel(q_ref, k_ref, v_ref, fq_ref, intra_ref):
+def intra_kernel(q_ref, k_ref, v_ref, late_ref, fq_ref, intra_ref):
+    del late_ref
     rows = q_ref.shape[0]
     causal = lax.broadcasted_iota(jnp.int32, (rows, rows), 0) >= lax.broadcasted_iota(jnp.int32, (rows, rows), 1)
     for h in range(HEADS):
@@ -64,6 +74,8 @@
 
 VMEM = pl.BlockSpec(memory_space=pltpu.VMEM)
 SMEM = pl.BlockSpec(memory_space=pltpu.SMEM)
+HBM = pl.BlockSpec(memory_space=pltpu.HBM)
+ANY = pl.BlockSpec(memory_space=pl.ANY)
 PARAMS = pltpu.CompilerParams(vmem_limit_bytes=8 * 1024 * 1024)
 
 
@@ -76,12 +88,12 @@
     return levels
 
 
-def steps_of(levels):
-    return [(stride, radix, shift) for stride, radix in levels for shift in range(1, radix)]
+def steps_of(order):
+    return [(kind, stride, radix, shift) for kind, (stride, radix) in order for shift in range(1, radix)]
 
 
 def target(step, i):
-    stride, radix, shift = step
+    _, stride, radix, shift = step
     digit = i // stride % radix
     return i + ((digit + shift) % radix - digit) * stride
 
@@ -98,57 +110,83 @@
     states = pl.pallas_call(
         state_kernel,
         out_shape=[part] * (2 * CHUNKS),
-        in_specs=[SMEM, VMEM, VMEM],
+        in_specs=[SMEM, HBM, HBM],
         out_specs=[VMEM] * (2 * CHUNKS),
+        scratch_shapes=[
+            pltpu.VMEM(keys.shape, keys.dtype),
+            pltpu.VMEM(values.shape, values.dtype),
+            pltpu.SemaphoreType.DMA((2,)),
+        ],
         compiler_params=PARAMS,
         name="own_state",
-    )(core_arr, keys, values)
+    )(core_arr, pltpu.with_memory_space_constraint(keys, pltpu.HBM), pltpu.with_memory_space_constraint(values, pltpu.HBM))
+    low = levels_of(2, inner // 2)
+    outer_levels = levels_of(inner, outer)
+    low, high = low + outer_levels[:1], outer_levels[1:]
+    total_low, total_high = [("total", v) for v in low], [("total", v) for v in high]
+    prefix_low, prefix_high = [("prefix", v) for v in low[::-1]], [("prefix", v) for v in high[::-1]]
+    orders = [
+        (total_low + prefix_high, prefix_high + prefix_low),
+        (total_low + total_high, total_high + prefix_low),
+    ]
+    swap = [(i, i ^ 1) for i in range(n)]
+
+    def digit(step):
+        return me // step[1] % step[2]
+
+    def to_swap(x):
+        return lax.ppermute(x, AXES, swap)
+
+    mine, theirs = states[:CHUNKS], states[CHUNKS:]
+    partner = [to_swap(x) for x in theirs]
+    own_parts, other_parts = [], []
+    late = None
+    for c in range(CHUNKS):
+        base = mine[c] + partner[c]
+        zero = jnp.zeros_like(base)
+        evens, odds = (steps_of(order) for order in orders[c % 2])
+        before, apart, total, unit = zero, zero, base, base
+        switched, entered = False, [None, None]
+        for j, (up, down) in enumerate(zip(evens, odds, strict=True)):
+            if up[0] == "prefix" and not switched:
+                switched = True
+                before, apart, unit = jnp.where(even, zero, before), jnp.where(even, before, zero), jnp.where(even, total, base)
+            messages, kept = [], []
+            for q, step in enumerate((up, down)):
+                kind, _, radix, shift = step
+                if shift == 1:
+                    entered[q] = total if kind == "total" else before
+                if kind == "total":
+                    messages.append(entered[q])
+                    kept.append(digit(step) >= shift)
+                else:
+                    messages.append(entered[q] + jnp.where(digit(step) + shift < radix, unit, zero))
+                    kept.append(jnp.bool_(True))
+            perm = [(i, target(down if i % 2 else up, i)) for i in range(n)]
+            message = jnp.where(even, messages[0], messages[1])
+            if c == CHUNKS - 1 and j == len(evens) - 1:
+                late = message
+            got = lax.ppermute(message, AXES, perm)
+            before = before + jnp.where(jnp.where(even, kept[0], kept[1]), got, zero)
+            total = total + got
+        before = before + apart
+        own_parts.append(before + jnp.where(even, zero, partner[c]))
+        other_parts.append(to_swap(before + jnp.where(even, mine[c], zero)))
+
     fq, intra = pl.pallas_call(
         intra_kernel,
         out_shape=[
             jax.ShapeDtypeStruct(queries.shape, jnp.bfloat16),
             jax.ShapeDtypeStruct(queries.shape, f32),
         ],
-        in_specs=[VMEM] * 3,
+        in_specs=[VMEM] * 3 + [ANY],
         out_specs=[VMEM] * 2,
         compiler_params=PARAMS,
         cost_estimate=pl.CostEstimate(
             flops=4 * HEADS * rows * rows * HEAD_DIM, bytes_accessed=6 * queries.size * 2, transcendentals=queries.size * 2
         ),
         name="intra",
-    )(queries, keys, values)
-
-    up_levels = levels_of(2, inner // 2) + levels_of(inner, outer)
-    ups = steps_of(up_levels)
-    downs = steps_of(up_levels[::-1])
-    swap = [(i, i ^ 1) for i in range(n)]
-
-    def digit(step):
-        return me // step[0] % step[1]
-
-    def to_swap(x):
-        return lax.ppermute(x, AXES, swap)
-
-    mine, theirs = states[:CHUNKS], states[CHUNKS:]
-    partner = [to_swap(x) for x in theirs]
-    own_parts, other_parts = [], []
-    for c in range(CHUNKS):
-        base = mine[c] + partner[c]
-        zero = jnp.zeros_like(base)
-        before, total = zero, base
-        for j, (up, down) in enumerate(zip(ups, downs, strict=True)):
-            if up[2] == 1:
-                level_total = total
-            if down[2] == 1:
-                level_before = before
-            higher = digit(down) + down[2] < down[1]
-            message = jnp.where(even, level_total, level_before + jnp.where(higher, base, zero))
-            perm = [(i, target(down if i % 2 else up, i)) for i in range(n)]
-            got = lax.ppermute(message, AXES, perm)
-            before = before + jnp.where(even & (digit(up) < up[2]), zero, got)
-            total = total + got
-        own_parts.append(before + jnp.where(even, zero, partner[c]))
-        other_parts.append(to_swap(before + jnp.where(even, mine[c], zero)))
+    )(queries, keys, values, late)
 
     return pl.pallas_call(
         final_kernel,

time: 34.7 us -> 31.2 us (0.90)
  local copies, waits for them, and re-layouts: 2.96 us -> 0.03 us
  waiting for transfers between devices: 12.4 us -> 10.6 us
  Pallas kernels: 2.77 us -> 3.82 us
    unnamed x12 -> x8, local copies, waits for them, and re-layouts: 2.96 us -> 0.03 us
    ppermute x8, waiting for transfers between devices: 11.1 us -> 8.42 us  [per_device(): got = lax.ppermute(message, AXES, perm)]
    pallas_call x1, Pallas kernels: 0.32 us -> 1.37 us  [per_device(): pl.pallas_call(state_kernel, out_shape=[part] * (2 * CHUNKS), in_specs=[S...]
    ppermute x4, waiting for transfers between devices: 1.27 us -> 2.2 us  [to_swap(): return lax.ppermute(x, AXES, swap)]
  transfers between devices with their start and end apart: 12 -> 12, of which waited for: 6 -> 7; matrix products, arithmetic and copies ran while one was open for 1% -> 1% of each run, Pallas kernels for 4% -> 4%
where the time goes in v3:
time: 31.2 us; the launch traced here: 31.1 us
  starting transfers between devices  16.1 us (52%)
  waiting for transfers between devices  10.6 us (34%)
  Pallas kernels  3.82 us (12%)
  other arithmetic  0.39 us (1%)
    ppermute x8, starting transfers between devices, per_device(): got = lax.ppermute(message, AXES, perm)  15.4 us
    ppermute x8, waiting for transfers between devices, per_device(): got = lax.ppermute(message, AXES, perm)  8.42 us
    ppermute x4, waiting for transfers between devices, to_swap(): return lax.ppermute(x, AXES, swap)  2.2 us
    pallas_call x1, Pallas kernels, per_device(): pl.pallas_call(state_kernel, out_shape=[part] * (2 * CHUNKS), in_specs=[S...  1.37 us
    pallas_call x1, Pallas kernels, per_device(): pl.pallas_call(intra_kernel, out_shape=[jax.ShapeDtypeStruct(queries.shap...  1.36 us
    pallas_call x1, Pallas kernels, per_device(): pl.pallas_call(final_kernel, out_shape=jax.ShapeDtypeStruct(queries.shape...  1.09 us
    ppermute x4, starting transfers between devices, to_swap(): return lax.ppermute(x, AXES, swap)  0.74 us
  transfers between devices with their start and end apart: 12, of which 7 were waited for; matrix products, arithmetic and copies ran while one was open for 1% of the time, Pallas kernels for 4%

profile of v3, /device:TPU:0, one launch (start us, length us, event | category | flops | bytes accessed | tf_op | source)
XLA Modules:
  0.0 31.1 jit_solution(10960833292290717834)
XLA Ops:
  0.0 1.4 %own_state.1 = (f32[2,128,128]{2,1,0:T(8,128)S(1)}, f32[2,128,128]{2,1,0:T(8,128)S(1)}, f32[2,128,128]{2,1,0:T(8,128)S(1)}, f32[2,128,128]{2,1,0:T(8,128)S(1)}) custom-call(s32[1]{0:T(128)} %bitcast.core_ref, bf16[128,1024]{1,0:T(8,128)(2,1)} %k_ref.1, bf16[128,1024]{1,0:T(8,128)(2,1)} %v_ref.1), custom_call_target="tpu_custom_call" | custom-call | tf_op jit(solution)/shard_map/own_state/pallas_call | solution.py:110
  1.4 0.5 %collective-permute-start = (f32[2,128,128]{2,1,0:T(8,128)S(1)}, f32[2,128,128]{2,1,0:T(8,128)S(1)}, u32[]{:S(2)}, u32[]{:S(2)}) collective-permute-start(f32[2,128,128]{2,1,0:T(8,128)S(1)} %get-tuple-element.12), channel_id=1, source_target_pairs={{0,1},{1,0},{2,3},{3,2},{4,5},{5,4},{6,7},{7,6},{8,9},{9,8},{10,11... | collective-permute-start | bytes 393224 | tf_op jit(solution)/shard_map/ppermute | solution.py:138
  1.9 0.1 collective-permute-start.4
  2.0 0.9 %collective-permute-done = f32[2,128,128]{2,1,0:T(8,128)S(1)} collective-permute-done((f32[2,128,128]{2,1,0:T(8,128)S(1)}, f32[2,128,128]{2,1,0:T(8,128)S(1)}, u32[]{:S(2)}, u32[]{:S(2)}) %collective-permute-start) | collective-permute-done | bytes 131104 | tf_op jit(solution)/shard_map/ppermute | solution.py:138
  2.9 2.9 %collective-permute-start.1 = (f32[2,128,128]{2,1,0:T(8,128)S(1)}, f32[2,128,128]{2,1,0:T(8,128)S(1)}, u32[]{:S(2)}, u32[]{:S(2)}) collective-permute-start(f32[2,128,128]{2,1,0:T(8,128)S(1)} %add.128), channel_id=1, source_target_pairs={{0,2},{1,9},{2,0},{3,11},{4,6},{5,13},{6,4},{7,15},{8,10},{9,1},{1... | collective-permute-start | bytes 393224 | tf_op jit(solution)/shard_map/ppermute | solution.py:169
  5.9 0.2 collective-permute-start.5
  6.1 2.7 %collective-permute-done.1 = f32[2,128,128]{2,1,0:T(8,128)S(1)} collective-permute-done((f32[2,128,128]{2,1,0:T(8,128)S(1)}, f32[2,128,128]{2,1,0:T(8,128)S(1)}, u32[]{:S(2)}, u32[]{:S(2)}) %collective-permute-start.1) | collective-permute-done | bytes 131104 | tf_op jit(solution)/shard_map/ppermute | solution.py:169
  8.8 2.1 %collective-permute-start.2 = (f32[2,128,128]{2,1,0:T(8,128)S(1)}, f32[2,128,128]{2,1,0:T(8,128)S(1)}, u32[]{:S(2)}, u32[]{:S(2)}) collective-permute-start(f32[2,128,128]{2,1,0:T(8,128)S(1)} %add.129), channel_id=1, source_target_pairs={{0,4},{1,17},{2,6},{3,19},{4,0},{5,21},{6,2},{7,23},{8,12},{9,25},... | collective-permute-start | bytes 393224 | tf_op jit(solution)/shard_map/ppermute | solution.py:169
  10.9 1.6 %collective-permute-start.6 = (f32[2,128,128]{2,1,0:T(8,128)S(1)}, f32[2,128,128]{2,1,0:T(8,128)S(1)}, u32[]{:S(2)}, u32[]{:S(2)}) collective-permute-start(f32[2,128,128]{2,1,0:T(8,128)S(1)} %get-tuple-element.19), channel_id=1, source_target_pairs={{0,4},{1,9},{2,6},{3,11},{4,0},{5,13},{6,2},{7,15},{8,12},{9,1},{1... | collective-permute-start | bytes 393224 | tf_op jit(solution)/shard_map/ppermute | solution.py:169
  12.5 1.4 %collective-permute-done.2 = f32[2,128,128]{2,1,0:T(8,128)S(1)} collective-permute-done((f32[2,128,128]{2,1,0:T(8,128)S(1)}, f32[2,128,128]{2,1,0:T(8,128)S(1)}, u32[]{:S(2)}, u32[]{:S(2)}) %collective-permute-start.2) | collective-permute-done | bytes 131104 | tf_op jit(solution)/shard_map/ppermute | solution.py:169
  13.9 2.1 %collective-permute-start.3 = (f32[2,128,128]{2,1,0:T(8,128)S(1)}, f32[2,128,128]{2,1,0:T(8,128)S(1)}, u32[]{:S(2)}, u32[]{:S(2)}) collective-permute-start(f32[2,128,128]{2,1,0:T(8,128)S(1)} %get-tuple-element.23), channel_id=1, source_target_pairs={{0,8},{1,5},{2,10},{3,7},{4,12},{5,1},{6,14},{7,3},{8,0},{9,13},{1... | collective-permute-start | bytes 393224 | tf_op jit(solution)/shard_map/ppermute | solution.py:169
  16.1 2.7 %collective-permute-start.7 = (f32[2,128,128]{2,1,0:T(8,128)S(1)}, f32[2,128,128]{2,1,0:T(8,128)S(1)}, u32[]{:S(2)}, u32[]{:S(2)}) collective-permute-start(f32[2,128,128]{2,1,0:T(8,128)S(1)} %add_select_fusion.1), channel_id=1, source_target_pairs={{0,16},{1,5},{2,18},{3,7},{4,20},{5,1},{6,22},{7,3},{8,24},{9,13},... | collective-permute-start | bytes 393224 | tf_op jit(solution)/shard_map/ppermute | solution.py:169
  18.7 0.2 collective-permute-done.3
  19.1 3.1 %collective-permute-start.9 = (f32[2,128,128]{2,1,0:T(8,128)S(1)}, f32[2,128,128]{2,1,0:T(8,128)S(1)}, u32[]{:S(2)}, u32[]{:S(2)}) collective-permute-start(f32[2,128,128]{2,1,0:T(8,128)S(1)} %add_select_fusion.4.late_ref), channel_id=1, source_target_pairs={{0,16},{1,3},{2,18},{3,1},{4,20},{5,7},{6,22},{7,5},{8,24},{9,11},... | collective-permute-start | bytes 393224 | tf_op jit(solution)/shard_map/ppermute | solution.py:169
  22.1 1.3 %collective-permute-done.7 = f32[2,128,128]{2,1,0:T(8,128)S(1)} collective-permute-done((f32[2,128,128]{2,1,0:T(8,128)S(1)}, f32[2,128,128]{2,1,0:T(8,128)S(1)}, u32[]{:S(2)}, u32[]{:S(2)}) %collective-permute-start.7) | collective-permute-done | bytes 131104 | tf_op jit(solution)/shard_map/ppermute | solution.py:169
  23.4 0.1 add_select_fusion
  23.5 0.7 %collective-permute-start.8 = (f32[2,128,128]{2,1,0:T(8,128)S(1)}, f32[2,128,128]{2,1,0:T(8,128)S(1)}, u32[]{:S(2)}, u32[]{:S(2)}) collective-permute-start(f32[2,128,128]{2,1,0:T(8,128)S(1)} %add_select_fusion), channel_id=1, source_target_pairs={{0,8},{1,3},{2,10},{3,1},{4,12},{5,7},{6,14},{7,5},{8,0},{9,11},{1... | collective-permute-start | bytes 393224 | tf_op jit(solution)/shard_map/ppermute | solution.py:169
  24.2 1.4 %intra.1 = (bf16[128,1024]{1,0:T(8,128)(2,1)S(1)}, f32[128,1024]{1,0:T(8,128)S(1)}) custom-call(bf16[128,1024]{1,0:T(8,128)(2,1)S(1)} %copy-done.2, bf16[128,1024]{1,0:T(8,128)(2,1)S(1)} %copy-done, bf16[128,1024]{1,0:T(8,128)(2,1)S(1)} %copy-done.1, f32[2,128,128]{2,1,0:T(8,128)S(1)} %add_select_fusion.4.late_ref), custom_call_target="tpu_custom_call" | custom-call | flops 67108864 | bytes 1572864 | tf_op jit(solution)/shard_map/intra/pallas_call | solution.py:176
  25.7 0.1 collective-permute-start.11
  25.7 2.8 %collective-permute-done.8 = f32[2,128,128]{2,1,0:T(8,128)S(1)} collective-permute-done((f32[2,128,128]{2,1,0:T(8,128)S(1)}, f32[2,128,128]{2,1,0:T(8,128)S(1)}, u32[]{:S(2)}, u32[]{:S(2)}) %collective-permute-start.8) | collective-permute-done | bytes 131104 | tf_op jit(solution)/shard_map/ppermute | solution.py:169
  28.5 0.1 select_add_fusion.1
  28.6 0.1 collective-permute-start.10
  28.7 1.3 %collective-permute-done.10.refs_2_ = f32[2,128,128]{2,1,0:T(8,128)S(1)} collective-permute-done((f32[2,128,128]{2,1,0:T(8,128)S(1)}, f32[2,128,128]{2,1,0:T(8,128)S(1)}, u32[]{:S(2)}, u32[]{:S(2)}) %collective-permute-start.10) | collective-permute-done | bytes 131104 | tf_op jit(solution)/shard_map/ppermute | solution.py:138
  30.0 1.1 %attend.1 = bf16[128,1024]{1,0:T(8,128)(2,1)} custom-call(s32[1]{0:T(128)} %bitcast.core_ref, bf16[128,1024]{1,0:T(8,128)(2,1)S(1)} %get-tuple-element.13.fq_ref, f32[128,1024]{1,0:T(8,128)S(1)} %get-tuple-element.14.intra_ref, f32[1,1024]{1,0:T(1,128)S(1)} %bitcast.2, f32[2,128,128]{2,1,0:T(8,128)S(1)} %get-tuple-element.27.refs_0_, ...), custom_call_target="tpu_custom_call" | custom-call | tf_op jit(solution)/shard_map/attend/pallas_call | solution.py:191
  (22 shorter events, 0.3 us)
Async XLA Ops:
  1.4 1.5 %collective-permute-start = (f32[2,128,128]{2,1,0:T(8,128)S(1)}, f32[2,128,128]{2,1,0:T(8,128)S(1)}, u32[]{:S(2)}, u32[]{:S(2)}) collective-permute-start(f32[2,128,128]{2,1,0:T(8,128)S(1)} %get-tuple-element.12), channel_id=1, source_target_pairs={{0,1},{1,0},{2,3},{3,2},{4,5},{5,4},{6,7},{7,6},{8,9},{9,8},{10,11... | collective-permute-start | bytes 393224 | tf_op jit(solution)/shard_map/ppermute | solution.py:138
  1.9 3.9 %collective-permute-start.4 = (f32[2,128,128]{2,1,0:T(8,128)S(1)}, f32[2,128,128]{2,1,0:T(8,128)S(1)}, u32[]{:S(2)}, u32[]{:S(2)}) collective-permute-start(f32[2,128,128]{2,1,0:T(8,128)S(1)} %get-tuple-element.16), channel_id=1, source_target_pairs={{0,1},{1,0},{2,3},{3,2},{4,5},{5,4},{6,7},{7,6},{8,9},{9,8},{10,11... | collective-permute-start | bytes 393224 | tf_op jit(solution)/shard_map/ppermute | solution.py:138
  2.9 5.9 %collective-permute-start.1 = (f32[2,128,128]{2,1,0:T(8,128)S(1)}, f32[2,128,128]{2,1,0:T(8,128)S(1)}, u32[]{:S(2)}, u32[]{:S(2)}) collective-permute-start(f32[2,128,128]{2,1,0:T(8,128)S(1)} %add.128), channel_id=1, source_target_pairs={{0,2},{1,9},{2,0},{3,11},{4,6},{5,13},{6,4},{7,15},{8,10},{9,1},{1... | collective-permute-start | bytes 393224 | tf_op jit(solution)/shard_map/ppermute | solution.py:169
  5.9 5.0 %collective-permute-start.5 = (f32[2,128,128]{2,1,0:T(8,128)S(1)}, f32[2,128,128]{2,1,0:T(8,128)S(1)}, u32[]{:S(2)}, u32[]{:S(2)}) collective-permute-start(f32[2,128,128]{2,1,0:T(8,128)S(1)} %get-tuple-element.21), channel_id=1, source_target_pairs={{0,2},{1,17},{2,0},{3,19},{4,6},{5,21},{6,4},{7,23},{8,10},{9,25},... | collective-permute-start | bytes 393224 | tf_op jit(solution)/shard_map/ppermute | solution.py:169
  8.8 5.0 %collective-permute-start.2 = (f32[2,128,128]{2,1,0:T(8,128)S(1)}, f32[2,128,128]{2,1,0:T(8,128)S(1)}, u32[]{:S(2)}, u32[]{:S(2)}) collective-permute-start(f32[2,128,128]{2,1,0:T(8,128)S(1)} %add.129), channel_id=1, source_target_pairs={{0,4},{1,17},{2,6},{3,19},{4,0},{5,21},{6,2},{7,23},{8,12},{9,25},... | collective-permute-start | bytes 393224 | tf_op jit(solution)/shard_map/ppermute | solution.py:169
  10.9 5.1 %collective-permute-start.6 = (f32[2,128,128]{2,1,0:T(8,128)S(1)}, f32[2,128,128]{2,1,0:T(8,128)S(1)}, u32[]{:S(2)}, u32[]{:S(2)}) collective-permute-start(f32[2,128,128]{2,1,0:T(8,128)S(1)} %get-tuple-element.19), channel_id=1, source_target_pairs={{0,4},{1,9},{2,6},{3,11},{4,0},{5,13},{6,2},{7,15},{8,12},{9,1},{1... | collective-permute-start | bytes 393224 | tf_op jit(solution)/shard_map/ppermute | solution.py:169
  13.9 5.1 %collective-permute-start.3 = (f32[2,128,128]{2,1,0:T(8,128)S(1)}, f32[2,128,128]{2,1,0:T(8,128)S(1)}, u32[]{:S(2)}, u32[]{:S(2)}) collective-permute-start(f32[2,128,128]{2,1,0:T(8,128)S(1)} %get-tuple-element.23), channel_id=1, source_target_pairs={{0,8},{1,5},{2,10},{3,7},{4,12},{5,1},{6,14},{7,3},{8,0},{9,13},{1... | collective-permute-start | bytes 393224 | tf_op jit(solution)/shard_map/ppermute | solution.py:169
  16.1 7.3 %collective-permute-start.7 = (f32[2,128,128]{2,1,0:T(8,128)S(1)}, f32[2,128,128]{2,1,0:T(8,128)S(1)}, u32[]{:S(2)}, u32[]{:S(2)}) collective-permute-start(f32[2,128,128]{2,1,0:T(8,128)S(1)} %add_select_fusion.1), channel_id=1, source_target_pairs={{0,16},{1,5},{2,18},{3,7},{4,20},{5,1},{6,22},{7,3},{8,24},{9,13},... | collective-permute-start | bytes 393224 | tf_op jit(solution)/shard_map/ppermute | solution.py:169
  19.0 5.2 %copy-start = (bf16[128,1024]{1,0:T(8,128)(2,1)S(1)}, bf16[128,1024]{1,0:T(8,128)(2,1)}, u32[]{:S(2)}) copy-start(bf16[128,1024]{1,0:T(8,128)(2,1)} %k_ref.1) | copy-start | bytes 786436
  19.0 5.2 %copy-start.1 = (bf16[128,1024]{1,0:T(8,128)(2,1)S(1)}, bf16[128,1024]{1,0:T(8,128)(2,1)}, u32[]{:S(2)}) copy-start(bf16[128,1024]{1,0:T(8,128)(2,1)} %v_ref.1) | copy-start | bytes 786436
  19.0 5.2 %copy-start.2 = (bf16[128,1024]{1,0:T(8,128)(2,1)S(1)}, bf16[128,1024]{1,0:T(8,128)(2,1)}, u32[]{:S(2)}) copy-start(bf16[128,1024]{1,0:T(8,128)(2,1)} %q_ref.1) | copy-start | bytes 786436
  19.1 6.6 %collective-permute-start.9 = (f32[2,128,128]{2,1,0:T(8,128)S(1)}, f32[2,128,128]{2,1,0:T(8,128)S(1)}, u32[]{:S(2)}, u32[]{:S(2)}) collective-permute-start(f32[2,128,128]{2,1,0:T(8,128)S(1)} %add_select_fusion.4.late_ref), channel_id=1, source_target_pairs={{0,16},{1,3},{2,18},{3,1},{4,20},{5,7},{6,22},{7,5},{8,24},{9,11},... | collective-permute-start | bytes 393224 | tf_op jit(solution)/shard_map/ppermute | solution.py:169
  23.5 5.0 %collective-permute-start.8 = (f32[2,128,128]{2,1,0:T(8,128)S(1)}, f32[2,128,128]{2,1,0:T(8,128)S(1)}, u32[]{:S(2)}, u32[]{:S(2)}) collective-permute-start(f32[2,128,128]{2,1,0:T(8,128)S(1)} %add_select_fusion), channel_id=1, source_target_pairs={{0,8},{1,3},{2,10},{3,1},{4,12},{5,7},{6,14},{7,5},{8,0},{9,11},{1... | collective-permute-start | bytes 393224 | tf_op jit(solution)/shard_map/ppermute | solution.py:169
  25.7 3.1 %collective-permute-start.11 = (f32[2,128,128]{2,1,0:T(8,128)S(1)}, f32[2,128,128]{2,1,0:T(8,128)S(1)}, u32[]{:S(2)}, u32[]{:S(2)}) collective-permute-start(f32[2,128,128]{2,1,0:T(8,128)S(1)} %get-tuple-element.17), channel_id=1, source_target_pairs={{0,1},{1,0},{2,3},{3,2},{4,5},{5,4},{6,7},{7,6},{8,9},{9,8},{10,11... | collective-permute-start | bytes 393224 | tf_op jit(solution)/shard_map/ppermute | solution.py:138
  28.6 1.4 %collective-permute-start.10 = (f32[2,128,128]{2,1,0:T(8,128)S(1)}, f32[2,128,128]{2,1,0:T(8,128)S(1)}, u32[]{:S(2)}, u32[]{:S(2)}) collective-permute-start(f32[2,128,128]{2,1,0:T(8,128)S(1)} %get-tuple-element.26), channel_id=1, source_target_pairs={{0,1},{1,0},{2,3},{3,2},{4,5},{5,4},{6,7},{7,6},{8,9},{9,8},{10,11... | collective-permute-start | bytes 393224 | tf_op jit(solution)/shard_map/ppermute | solution.py:138
  28.7 1.3 %copy-start.3 = (f32[1024]{0:T(1024)S(1)}, f32[1024]{0:T(1024)}, u32[]{:S(2)}) copy-start(f32[1024]{0:T(1024)} %param.7) | copy-start | bytes 12292

commit v4 on v3

--- a/solution.py
+++ b/solution.py
@@ -58,18 +58,26 @@
         intra_ref[:, cols] = jnp.dot(weights, v_ref[:, cols], preferred_element_type=jnp.float32)
 
 
-def final_kernel(core_ref, fq_ref, intra_ref, gain_ref, *refs):
-    carried, out_ref = refs[:-1], refs[-1]
+def attend_kernel(jobs, core_ref, fq_ref, intra_ref, gain_ref, *refs):
+    carried, (out_hbm, buf_ref, sems) = refs[: len(jobs)], refs[-3:]
     core = core_ref[0]
-    for half in range(2):
-        for c in range(CHUNKS):
-            for i in range(PER):
-                h = (core * HALF + half * HALF + c * PER + i) % HEADS
-                state = carried[half * CHUNKS + c][i].astype(jnp.bfloat16)
-                cols = head_cols(h)
-                total = intra_ref[:, cols] + jnp.dot(fq_ref[:, cols], state, preferred_element_type=jnp.float32)
-                meansq = jnp.mean(total * total, axis=-1, keepdims=True)
-                out_ref[:, cols] = (total * lax.rsqrt(meansq + 1e-06) * gain_ref[:, cols]).astype(jnp.bfloat16)
+    copies = []
+    for slot, (half, c) in enumerate(jobs):
+        first = (core * HALF + half * HALF + c * PER) % HEADS
+        for i in range(PER):
+            cols = head_cols(first + i)
+            state = carried[slot][i].astype(jnp.bfloat16)
+            total = intra_ref[:, cols] + jnp.dot(fq_ref[:, cols], state, preferred_element_type=jnp.float32)
+            meansq = jnp.mean(total * total, axis=-1, keepdims=True)
+            normed = total * lax.rsqrt(meansq + 1e-06) * gain_ref[:, cols]
+            buf_ref[slot, :, i * HEAD_DIM : (i + 1) * HEAD_DIM] = normed.astype(jnp.bfloat16)
+        width = PER * HEAD_DIM
+        place = pl.ds(pl.multiple_of(first * HEAD_DIM, width), width)
+        copy = pltpu.make_async_copy(buf_ref.at[slot], out_hbm.at[:, place], sems.at[slot])
+        copy.start()
+        copies.append(copy)
+    for copy in copies:
+        copy.wait()
 
 
 VMEM = pl.BlockSpec(memory_space=pltpu.VMEM)
@@ -188,14 +196,32 @@
         name="intra",
     )(queries, keys, values, late)
 
-    return pl.pallas_call(
-        final_kernel,
-        out_shape=jax.ShapeDtypeStruct(queries.shape, jnp.bfloat16),
-        in_specs=[SMEM] + [VMEM] * (3 + 2 * CHUNKS),
-        out_specs=VMEM,
-        compiler_params=PARAMS,
-        name="attend",
-    )(core_arr, fq, intra, head_gain.reshape(1, -1), *own_parts, *other_parts)
+    gain = head_gain.reshape(1, -1)
+
+    def attend(jobs, parts, so_far=None):
+        whole = jax.ShapeDtypeStruct(queries.shape, jnp.bfloat16)
+        extra = [] if so_far is None else [so_far]
+        given = [core_arr, fq, intra, gain, *parts, *extra]
+        return pl.pallas_call(
+            functools.partial(attend_kernel, jobs),
+            out_shape=whole,
+            in_specs=[SMEM] + [VMEM] * (3 + len(jobs)) + [HBM] * len(extra),
+            out_specs=HBM,
+            scratch_shapes=[
+                pltpu.VMEM((len(jobs), rows, PER * HEAD_DIM), jnp.bfloat16),
+                pltpu.SemaphoreType.DMA((len(jobs),)),
+            ],
+            input_output_aliases={len(given) - 1: 0} if extra else {},
+            compiler_params=PARAMS,
+            cost_estimate=pl.CostEstimate(
+                flops=2 * len(jobs) * PER * rows * HEAD_DIM * HEAD_DIM, bytes_accessed=len(jobs) * queries.size, transcendentals=0
+            ),
+            name="attend",
+        )(*given)
+
+    early = [(0, c) for c in range(CHUNKS)] + [(1, c) for c in range(1, CHUNKS)]
+    most = attend(early, own_parts + other_parts[1:])
+    return attend([(1, 0)], other_parts[:1], most)
 
 
 def solution(mesh):

time: 31.2 us -> 31.5 us (level)
  waiting for transfers between devices: 10.6 us -> 9.34 us
  Pallas kernels: 3.82 us -> 4.62 us
  local copies, waits for them, and re-layouts: 0.03 us -> 0.69 us
    ppermute x4, waiting for transfers between devices: 2.2 us -> 0.92 us  [to_swap(): return lax.ppermute(x, AXES, swap)]
    pallas_call x1 -> x2, Pallas kernels: 1.09 us -> 1.9 us  [attend(): pl.pallas_call(functools.partial(attend_kernel, jobs), out_shape=whole, i...]
    unnamed x8, local copies, waits for them, and re-layouts: 0.03 us -> 0.69 us
  transfers between devices with their start and end apart: 12 -> 12, of which waited for: 7 -> 6; matrix products, arithmetic and copies ran while one was open for 1% -> 1% of each run, Pallas kernels for 4% -> 8%
where the time goes in v4:
time: 31.5 us; the launch traced here: 31.3 us
  starting transfers between devices  16.1 us (51%)
  waiting for transfers between devices  9.34 us (30%)
  Pallas kernels  4.62 us (15%)
  local copies, waits for them, and re-layouts  0.69 us (2%)
  other arithmetic  0.39 us (1%)
    ppermute x8, starting transfers between devices, per_device(): got = lax.ppermute(message, AXES, perm)  15.4 us
    ppermute x8, waiting for transfers between devices, per_device(): got = lax.ppermute(message, AXES, perm)  8.42 us
    pallas_call x2, Pallas kernels, attend(): pl.pallas_call(functools.partial(attend_kernel, jobs), out_shape=whole, i...  1.9 us
    pallas_call x1, Pallas kernels, per_device(): pl.pallas_call(state_kernel, out_shape=[part] * (2 * CHUNKS), in_specs=[S...  1.37 us
    pallas_call x1, Pallas kernels, per_device(): pl.pallas_call(intra_kernel, out_shape=[jax.ShapeDtypeStruct(queries.shap...  1.36 us
    ppermute x4, waiting for transfers between devices, to_swap(): return lax.ppermute(x, AXES, swap)  0.92 us
    ppermute x4, starting transfers between devices, to_swap(): return lax.ppermute(x, AXES, swap)  0.74 us
    unnamed x8, local copies, waits for them, and re-layouts  0.69 us
  transfers between devices with their start and end apart: 12, of which 6 were waited for; matrix products, arithmetic and copies ran while one was open for 1% of the time, Pallas kernels for 8%

profile of v4, /device:TPU:0, one launch (start us, length us, event | category | flops | bytes accessed | tf_op | source)
XLA Modules:
  0.0 31.3 jit_solution(13074633628123817877)
XLA Ops:
  0.0 1.4 %own_state.1 = (f32[2,128,128]{2,1,0:T(8,128)S(1)}, f32[2,128,128]{2,1,0:T(8,128)S(1)}, f32[2,128,128]{2,1,0:T(8,128)S(1)}, f32[2,128,128]{2,1,0:T(8,128)S(1)}) custom-call(s32[1]{0:T(128)} %bitcast.core_ref, bf16[128,1024]{1,0:T(8,128)(2,1)} %k_ref.1, bf16[128,1024]{1,0:T(8,128)(2,1)} %v_ref.1), custom_call_target="tpu_custom_call" | custom-call | tf_op jit(solution)/shard_map/own_state/pallas_call | solution.py:118
  1.4 0.5 %collective-permute-start = (f32[2,128,128]{2,1,0:T(8,128)S(1)}, f32[2,128,128]{2,1,0:T(8,128)S(1)}, u32[]{:S(2)}, u32[]{:S(2)}) collective-permute-start(f32[2,128,128]{2,1,0:T(8,128)S(1)} %get-tuple-element.12), channel_id=1, source_target_pairs={{0,1},{1,0},{2,3},{3,2},{4,5},{5,4},{6,7},{7,6},{8,9},{9,8},{10,11... | collective-permute-start | bytes 393224 | tf_op jit(solution)/shard_map/ppermute | solution.py:146
  1.9 0.1 collective-permute-start.4
  2.0 0.9 %collective-permute-done = f32[2,128,128]{2,1,0:T(8,128)S(1)} collective-permute-done((f32[2,128,128]{2,1,0:T(8,128)S(1)}, f32[2,128,128]{2,1,0:T(8,128)S(1)}, u32[]{:S(2)}, u32[]{:S(2)}) %collective-permute-start) | collective-permute-done | bytes 131104 | tf_op jit(solution)/shard_map/ppermute | solution.py:146
  2.9 2.9 %collective-permute-start.1 = (f32[2,128,128]{2,1,0:T(8,128)S(1)}, f32[2,128,128]{2,1,0:T(8,128)S(1)}, u32[]{:S(2)}, u32[]{:S(2)}) collective-permute-start(f32[2,128,128]{2,1,0:T(8,128)S(1)} %add.128), channel_id=1, source_target_pairs={{0,2},{1,9},{2,0},{3,11},{4,6},{5,13},{6,4},{7,15},{8,10},{9,1},{1... | collective-permute-start | bytes 393224 | tf_op jit(solution)/shard_map/ppermute | solution.py:177
  5.9 0.2 collective-permute-start.5
  6.1 2.7 %collective-permute-done.1 = f32[2,128,128]{2,1,0:T(8,128)S(1)} collective-permute-done((f32[2,128,128]{2,1,0:T(8,128)S(1)}, f32[2,128,128]{2,1,0:T(8,128)S(1)}, u32[]{:S(2)}, u32[]{:S(2)}) %collective-permute-start.1) | collective-permute-done | bytes 131104 | tf_op jit(solution)/shard_map/ppermute | solution.py:177
  8.8 2.1 %collective-permute-start.2 = (f32[2,128,128]{2,1,0:T(8,128)S(1)}, f32[2,128,128]{2,1,0:T(8,128)S(1)}, u32[]{:S(2)}, u32[]{:S(2)}) collective-permute-start(f32[2,128,128]{2,1,0:T(8,128)S(1)} %add.129), channel_id=1, source_target_pairs={{0,4},{1,17},{2,6},{3,19},{4,0},{5,21},{6,2},{7,23},{8,12},{9,25},... | collective-permute-start | bytes 393224 | tf_op jit(solution)/shard_map/ppermute | solution.py:177
  10.9 1.6 %collective-permute-start.6 = (f32[2,128,128]{2,1,0:T(8,128)S(1)}, f32[2,128,128]{2,1,0:T(8,128)S(1)}, u32[]{:S(2)}, u32[]{:S(2)}) collective-permute-start(f32[2,128,128]{2,1,0:T(8,128)S(1)} %get-tuple-element.19), channel_id=1, source_target_pairs={{0,4},{1,9},{2,6},{3,11},{4,0},{5,13},{6,2},{7,15},{8,12},{9,1},{1... | collective-permute-start | bytes 393224 | tf_op jit(solution)/shard_map/ppermute | solution.py:177
  12.5 1.4 %collective-permute-done.2 = f32[2,128,128]{2,1,0:T(8,128)S(1)} collective-permute-done((f32[2,128,128]{2,1,0:T(8,128)S(1)}, f32[2,128,128]{2,1,0:T(8,128)S(1)}, u32[]{:S(2)}, u32[]{:S(2)}) %collective-permute-start.2) | collective-permute-done | bytes 131104 | tf_op jit(solution)/shard_map/ppermute | solution.py:177
  13.9 2.1 %collective-permute-start.3 = (f32[2,128,128]{2,1,0:T(8,128)S(1)}, f32[2,128,128]{2,1,0:T(8,128)S(1)}, u32[]{:S(2)}, u32[]{:S(2)}) collective-permute-start(f32[2,128,128]{2,1,0:T(8,128)S(1)} %get-tuple-element.23), channel_id=1, source_target_pairs={{0,8},{1,5},{2,10},{3,7},{4,12},{5,1},{6,14},{7,3},{8,0},{9,13},{1... | collective-permute-start | bytes 393224 | tf_op jit(solution)/shard_map/ppermute | solution.py:177
  16.1 2.7 %collective-permute-start.7 = (f32[2,128,128]{2,1,0:T(8,128)S(1)}, f32[2,128,128]{2,1,0:T(8,128)S(1)}, u32[]{:S(2)}, u32[]{:S(2)}) collective-permute-start(f32[2,128,128]{2,1,0:T(8,128)S(1)} %add_select_fusion.1), channel_id=1, source_target_pairs={{0,16},{1,5},{2,18},{3,7},{4,20},{5,1},{6,22},{7,3},{8,24},{9,13},... | collective-permute-start | bytes 393224 | tf_op jit(solution)/shard_map/ppermute | solution.py:177
  18.7 0.2 collective-permute-done.3
  19.1 3.1 %collective-permute-start.10 = (f32[2,128,128]{2,1,0:T(8,128)S(1)}, f32[2,128,128]{2,1,0:T(8,128)S(1)}, u32[]{:S(2)}, u32[]{:S(2)}) collective-permute-start(f32[2,128,128]{2,1,0:T(8,128)S(1)} %add_select_fusion.4.late_ref), channel_id=1, source_target_pairs={{0,16},{1,3},{2,18},{3,1},{4,20},{5,7},{6,22},{7,5},{8,24},{9,11},... | collective-permute-start | bytes 393224 | tf_op jit(solution)/shard_map/ppermute | solution.py:177
  22.1 1.3 %collective-permute-done.7 = f32[2,128,128]{2,1,0:T(8,128)S(1)} collective-permute-done((f32[2,128,128]{2,1,0:T(8,128)S(1)}, f32[2,128,128]{2,1,0:T(8,128)S(1)}, u32[]{:S(2)}, u32[]{:S(2)}) %collective-permute-start.7) | collective-permute-done | bytes 131104 | tf_op jit(solution)/shard_map/ppermute | solution.py:177
  23.4 0.1 add_select_fusion
  23.5 0.7 %collective-permute-start.8 = (f32[2,128,128]{2,1,0:T(8,128)S(1)}, f32[2,128,128]{2,1,0:T(8,128)S(1)}, u32[]{:S(2)}, u32[]{:S(2)}) collective-permute-start(f32[2,128,128]{2,1,0:T(8,128)S(1)} %add_select_fusion), channel_id=1, source_target_pairs={{0,8},{1,3},{2,10},{3,1},{4,12},{5,7},{6,14},{7,5},{8,0},{9,11},{1... | collective-permute-start | bytes 393224 | tf_op jit(solution)/shard_map/ppermute | solution.py:177
  24.2 1.4 %intra.1 = (bf16[128,1024]{1,0:T(8,128)(2,1)S(1)}, f32[128,1024]{1,0:T(8,128)S(1)}) custom-call(bf16[128,1024]{1,0:T(8,128)(2,1)S(1)} %copy-done.2, bf16[128,1024]{1,0:T(8,128)(2,1)S(1)} %copy-done, bf16[128,1024]{1,0:T(8,128)(2,1)S(1)} %copy-done.1, f32[2,128,128]{2,1,0:T(8,128)S(1)} %add_select_fusion.4.late_ref), custom_call_target="tpu_custom_call" | custom-call | flops 67108864 | bytes 1572864 | tf_op jit(solution)/shard_map/intra/pallas_call | solution.py:184
  25.7 0.1 collective-permute-start.11
  25.7 2.8 %collective-permute-done.8 = f32[2,128,128]{2,1,0:T(8,128)S(1)} collective-permute-done((f32[2,128,128]{2,1,0:T(8,128)S(1)}, f32[2,128,128]{2,1,0:T(8,128)S(1)}, u32[]{:S(2)}, u32[]{:S(2)}) %collective-permute-start.8) | collective-permute-done | bytes 131104 | tf_op jit(solution)/shard_map/ppermute | solution.py:177
  28.6 0.1 collective-permute-start.9
  28.7 0.7 %copy-done.3 = f32[1024]{0:T(1024)S(1)} copy-done((f32[1024]{0:T(1024)S(1)}, f32[1024]{0:T(1024)}, u32[]{:S(2)}) %copy-start.3) | copy-done | bytes 4120
  29.4 1.0 %attend.2.refs_1_ = bf16[128,1024]{1,0:T(8,128)(2,1)} custom-call(s32[1]{0:T(128)} %bitcast.core_ref, bf16[128,1024]{1,0:T(8,128)(2,1)S(1)} %get-tuple-element.13.fq_ref, f32[128,1024]{1,0:T(8,128)S(1)} %get-tuple-element.14.intra_ref, f32[1,1024]{1,0:T(1,128)S(1)} %bitcast.2, f32[2,128,128]{2,1,0:T(8,128)S(1)} %get-tuple-element.26.refs_0_, ...), custom_call_target="tpu_custom_call" | custom-call | flops 25165824 | bytes 393216 | tf_op jit(solution)/shard_map/attend/pallas_call | solution.py:205
  30.4 0.9 %attend.3 = bf16[128,1024]{1,0:T(8,128)(2,1)} custom-call(s32[1]{0:T(128)} %bitcast.core_ref, bf16[128,1024]{1,0:T(8,128)(2,1)S(1)} %get-tuple-element.13.fq_ref, f32[128,1024]{1,0:T(8,128)S(1)} %get-tuple-element.14.intra_ref, f32[1,1024]{1,0:T(1,128)S(1)} %bitcast.3, ...), custom_call_target="tpu_custom_call", output_to_operand_aliasing={{}: (5, {})} | custom-call | flops 8388608 | bytes 131072 | tf_op jit(solution)/shard_map/attend/pallas_call | solution.py:205
  (23 shorter events, 0.4 us)
Async XLA Ops:
  1.4 1.5 %collective-permute-start = (f32[2,128,128]{2,1,0:T(8,128)S(1)}, f32[2,128,128]{2,1,0:T(8,128)S(1)}, u32[]{:S(2)}, u32[]{:S(2)}) collective-permute-start(f32[2,128,128]{2,1,0:T(8,128)S(1)} %get-tuple-element.12), channel_id=1, source_target_pairs={{0,1},{1,0},{2,3},{3,2},{4,5},{5,4},{6,7},{7,6},{8,9},{9,8},{10,11... | collective-permute-start | bytes 393224 | tf_op jit(solution)/shard_map/ppermute | solution.py:146
  1.9 3.9 %collective-permute-start.4 = (f32[2,128,128]{2,1,0:T(8,128)S(1)}, f32[2,128,128]{2,1,0:T(8,128)S(1)}, u32[]{:S(2)}, u32[]{:S(2)}) collective-permute-start(f32[2,128,128]{2,1,0:T(8,128)S(1)} %get-tuple-element.16), channel_id=1, source_target_pairs={{0,1},{1,0},{2,3},{3,2},{4,5},{5,4},{6,7},{7,6},{8,9},{9,8},{10,11... | collective-permute-start | bytes 393224 | tf_op jit(solution)/shard_map/ppermute | solution.py:146
  2.9 5.9 %collective-permute-start.1 = (f32[2,128,128]{2,1,0:T(8,128)S(1)}, f32[2,128,128]{2,1,0:T(8,128)S(1)}, u32[]{:S(2)}, u32[]{:S(2)}) collective-permute-start(f32[2,128,128]{2,1,0:T(8,128)S(1)} %add.128), channel_id=1, source_target_pairs={{0,2},{1,9},{2,0},{3,11},{4,6},{5,13},{6,4},{7,15},{8,10},{9,1},{1... | collective-permute-start | bytes 393224 | tf_op jit(solution)/shard_map/ppermute | solution.py:177
  5.9 5.0 %collective-permute-start.5 = (f32[2,128,128]{2,1,0:T(8,128)S(1)}, f32[2,128,128]{2,1,0:T(8,128)S(1)}, u32[]{:S(2)}, u32[]{:S(2)}) collective-permute-start(f32[2,128,128]{2,1,0:T(8,128)S(1)} %get-tuple-element.21), channel_id=1, source_target_pairs={{0,2},{1,17},{2,0},{3,19},{4,6},{5,21},{6,4},{7,23},{8,10},{9,25},... | collective-permute-start | bytes 393224 | tf_op jit(solution)/shard_map/ppermute | solution.py:177
  8.8 5.0 %collective-permute-start.2 = (f32[2,128,128]{2,1,0:T(8,128)S(1)}, f32[2,128,128]{2,1,0:T(8,128)S(1)}, u32[]{:S(2)}, u32[]{:S(2)}) collective-permute-start(f32[2,128,128]{2,1,0:T(8,128)S(1)} %add.129), channel_id=1, source_target_pairs={{0,4},{1,17},{2,6},{3,19},{4,0},{5,21},{6,2},{7,23},{8,12},{9,25},... | collective-permute-start | bytes 393224 | tf_op jit(solution)/shard_map/ppermute | solution.py:177
  10.9 5.1 %collective-permute-start.6 = (f32[2,128,128]{2,1,0:T(8,128)S(1)}, f32[2,128,128]{2,1,0:T(8,128)S(1)}, u32[]{:S(2)}, u32[]{:S(2)}) collective-permute-start(f32[2,128,128]{2,1,0:T(8,128)S(1)} %get-tuple-element.19), channel_id=1, source_target_pairs={{0,4},{1,9},{2,6},{3,11},{4,0},{5,13},{6,2},{7,15},{8,12},{9,1},{1... | collective-permute-start | bytes 393224 | tf_op jit(solution)/shard_map/ppermute | solution.py:177
  13.9 5.1 %collective-permute-start.3 = (f32[2,128,128]{2,1,0:T(8,128)S(1)}, f32[2,128,128]{2,1,0:T(8,128)S(1)}, u32[]{:S(2)}, u32[]{:S(2)}) collective-permute-start(f32[2,128,128]{2,1,0:T(8,128)S(1)} %get-tuple-element.23), channel_id=1, source_target_pairs={{0,8},{1,5},{2,10},{3,7},{4,12},{5,1},{6,14},{7,3},{8,0},{9,13},{1... | collective-permute-start | bytes 393224 | tf_op jit(solution)/shard_map/ppermute | solution.py:177
  16.1 7.3 %collective-permute-start.7 = (f32[2,128,128]{2,1,0:T(8,128)S(1)}, f32[2,128,128]{2,1,0:T(8,128)S(1)}, u32[]{:S(2)}, u32[]{:S(2)}) collective-permute-start(f32[2,128,128]{2,1,0:T(8,128)S(1)} %add_select_fusion.1), channel_id=1, source_target_pairs={{0,16},{1,5},{2,18},{3,7},{4,20},{5,1},{6,22},{7,3},{8,24},{9,13},... | collective-permute-start | bytes 393224 | tf_op jit(solution)/shard_map/ppermute | solution.py:177
  19.0 5.2 %copy-start = (bf16[128,1024]{1,0:T(8,128)(2,1)S(1)}, bf16[128,1024]{1,0:T(8,128)(2,1)}, u32[]{:S(2)}) copy-start(bf16[128,1024]{1,0:T(8,128)(2,1)} %k_ref.1) | copy-start | bytes 786436
  19.0 5.2 %copy-start.1 = (bf16[128,1024]{1,0:T(8,128)(2,1)S(1)}, bf16[128,1024]{1,0:T(8,128)(2,1)}, u32[]{:S(2)}) copy-start(bf16[128,1024]{1,0:T(8,128)(2,1)} %v_ref.1) | copy-start | bytes 786436
  19.0 5.2 %copy-start.2 = (bf16[128,1024]{1,0:T(8,128)(2,1)S(1)}, bf16[128,1024]{1,0:T(8,128)(2,1)}, u32[]{:S(2)}) copy-start(bf16[128,1024]{1,0:T(8,128)(2,1)} %q_ref.1) | copy-start | bytes 786436
  19.1 6.6 %collective-permute-start.10 = (f32[2,128,128]{2,1,0:T(8,128)S(1)}, f32[2,128,128]{2,1,0:T(8,128)S(1)}, u32[]{:S(2)}, u32[]{:S(2)}) collective-permute-start(f32[2,128,128]{2,1,0:T(8,128)S(1)} %add_select_fusion.4.late_ref), channel_id=1, source_target_pairs={{0,16},{1,3},{2,18},{3,1},{4,20},{5,7},{6,22},{7,5},{8,24},{9,11},... | collective-permute-start | bytes 393224 | tf_op jit(solution)/shard_map/ppermute | solution.py:177
  23.5 5.0 %collective-permute-start.8 = (f32[2,128,128]{2,1,0:T(8,128)S(1)}, f32[2,128,128]{2,1,0:T(8,128)S(1)}, u32[]{:S(2)}, u32[]{:S(2)}) collective-permute-start(f32[2,128,128]{2,1,0:T(8,128)S(1)} %add_select_fusion), channel_id=1, source_target_pairs={{0,8},{1,3},{2,10},{3,1},{4,12},{5,7},{6,14},{7,5},{8,0},{9,11},{1... | collective-permute-start | bytes 393224 | tf_op jit(solution)/shard_map/ppermute | solution.py:177
  25.7 3.1 %collective-permute-start.11 = (f32[2,128,128]{2,1,0:T(8,128)S(1)}, f32[2,128,128]{2,1,0:T(8,128)S(1)}, u32[]{:S(2)}, u32[]{:S(2)}) collective-permute-start(f32[2,128,128]{2,1,0:T(8,128)S(1)} %get-tuple-element.17), channel_id=1, source_target_pairs={{0,1},{1,0},{2,3},{3,2},{4,5},{5,4},{6,7},{7,6},{8,9},{9,8},{10,11... | collective-permute-start | bytes 393224 | tf_op jit(solution)/shard_map/ppermute | solution.py:146
  28.6 1.8 %collective-permute-start.9 = (f32[2,128,128]{2,1,0:T(8,128)S(1)}, f32[2,128,128]{2,1,0:T(8,128)S(1)}, u32[]{:S(2)}, u32[]{:S(2)}) collective-permute-start(f32[2,128,128]{2,1,0:T(8,128)S(1)} %get-tuple-element.27), channel_id=1, source_target_pairs={{0,1},{1,0},{2,3},{3,2},{4,5},{5,4},{6,7},{7,6},{8,9},{9,8},{10,11... | collective-permute-start | bytes 393224 | tf_op jit(solution)/shard_map/ppermute | solution.py:146
  28.7 0.7 %copy-start.3 = (f32[1024]{0:T(1024)S(1)}, f32[1024]{0:T(1024)}, u32[]{:S(2)}) copy-start(f32[1024]{0:T(1024)} %param.7) | copy-start | bytes 12292

commit v5 on v4

--- a/solution.py
+++ b/solution.py
@@ -26,26 +26,31 @@
 
 def state_kernel(core_ref, k_hbm, v_hbm, *refs):
     out_refs, (k_ref, v_ref, sems) = refs[: 2 * CHUNKS], refs[2 * CHUNKS :]
-    copies = [
-        pltpu.make_async_copy(k_hbm, k_ref, sems.at[0]),
-        pltpu.make_async_copy(v_hbm, v_ref, sems.at[1]),
-    ]
-    for copy in copies:
-        copy.start()
-    for copy in copies:
-        copy.wait()
     core = core_ref[0]
+    width = HALF * HEAD_DIM
+    copies = {}
     for half in (1, 0):
+        cols = pl.ds(pl.multiple_of((core + half) % 2 * width, width), width)
+        copies[half] = [
+            pltpu.make_async_copy(k_hbm.at[:, cols], k_ref.at[half], sems.at[half, 0]),
+            pltpu.make_async_copy(v_hbm.at[:, cols], v_ref.at[half], sems.at[half, 1]),
+        ]
+        for copy in copies[half]:
+            copy.start()
+    for half in (1, 0):
+        for copy in copies[half]:
+            copy.wait()
         for i in range(HALF):
-            h = (core * HALF + half * HALF + i) % HEADS
-            fk = features(k_ref[:, head_cols(h)])
+            cols = slice(i * HEAD_DIM, (i + 1) * HEAD_DIM)
+            fk = features(k_ref[half, :, cols])
             out_refs[half * CHUNKS + i // PER][i % PER] = lax.dot_general(
-                fk, v_ref[:, head_cols(h)], (((0,), (0,)), ((), ())), preferred_element_type=jnp.float32
+                fk, v_ref[half, :, cols], (((0,), (0,)), ((), ())), preferred_element_type=jnp.float32
             )
 
 
-def intra_kernel(q_ref, k_ref, v_ref, late_ref, fq_ref, intra_ref):
+def intra_kernel(q_ref, k_ref, v_ref, gain_ref, late_ref, fq_ref, intra_ref, near_gain_ref):
     del late_ref
+    near_gain_ref[...] = gain_ref[...]
     rows = q_ref.shape[0]
     causal = lax.broadcasted_iota(jnp.int32, (rows, rows), 0) >= lax.broadcasted_iota(jnp.int32, (rows, rows), 1)
     for h in range(HEADS):
@@ -121,9 +126,9 @@
         in_specs=[SMEM, HBM, HBM],
         out_specs=[VMEM] * (2 * CHUNKS),
         scratch_shapes=[
-            pltpu.VMEM(keys.shape, keys.dtype),
-            pltpu.VMEM(values.shape, values.dtype),
-            pltpu.SemaphoreType.DMA((2,)),
+            pltpu.VMEM((2, rows, HALF * HEAD_DIM), keys.dtype),
+            pltpu.VMEM((2, rows, HALF * HEAD_DIM), values.dtype),
+            pltpu.SemaphoreType.DMA((2, 2)),
         ],
         compiler_params=PARAMS,
         name="own_state",
@@ -181,22 +186,21 @@
         own_parts.append(before + jnp.where(even, zero, partner[c]))
         other_parts.append(to_swap(before + jnp.where(even, mine[c], zero)))
 
-    fq, intra = pl.pallas_call(
+    fq, intra, gain = pl.pallas_call(
         intra_kernel,
         out_shape=[
             jax.ShapeDtypeStruct(queries.shape, jnp.bfloat16),
             jax.ShapeDtypeStruct(queries.shape, f32),
+            jax.ShapeDtypeStruct((1, queries.shape[1]), f32),
         ],
-        in_specs=[VMEM] * 3 + [ANY],
-        out_specs=[VMEM] * 2,
+        in_specs=[VMEM] * 4 + [ANY],
+        out_specs=[VMEM] * 3,
         compiler_params=PARAMS,
         cost_estimate=pl.CostEstimate(
             flops=4 * HEADS * rows * rows * HEAD_DIM, bytes_accessed=6 * queries.size * 2, transcendentals=queries.size * 2
         ),
         name="intra",
-    )(queries, keys, values, late)
-
-    gain = head_gain.reshape(1, -1)
+    )(queries, keys, values, head_gain.reshape(1, -1), late)
 
     def attend(jobs, parts, so_far=None):
         whole = jax.ShapeDtypeStruct(queries.shape, jnp.bfloat16)

time: 31.5 us -> 31.2 us (level)
  local copies, waits for them, and re-layouts: 0.69 us -> 0.02 us
    unnamed x8, local copies, waits for them, and re-layouts: 0.69 us -> 0.02 us
  transfers between devices with their start and end apart: 12 -> 12, of which waited for: 6 -> 7; matrix products, arithmetic and copies ran while one was open for 1% -> 1% of each run, Pallas kernels for 8% -> 8%
where the time goes in v5:
time: 31.2 us; the launch traced here: 31 us
  starting transfers between devices  16.1 us (52%)
  waiting for transfers between devices  9.61 us (31%)
  Pallas kernels  4.74 us (15%)
  other arithmetic  0.4 us (1%)
    ppermute x8, starting transfers between devices, per_device(): got = lax.ppermute(message, AXES, perm)  15.3 us
    ppermute x8, waiting for transfers between devices, per_device(): got = lax.ppermute(message, AXES, perm)  8.41 us
    pallas_call x2, Pallas kernels, attend(): pl.pallas_call(functools.partial(attend_kernel, jobs), out_shape=whole, i...  1.9 us
    pallas_call x1, Pallas kernels, per_device(): pl.pallas_call(state_kernel, out_shape=[part] * (2 * CHUNKS), in_specs=[S...  1.48 us
    pallas_call x1, Pallas kernels, per_device(): pl.pallas_call(intra_kernel, out_shape=[jax.ShapeDtypeStruct(queries.shap...  1.36 us
    ppermute x4, waiting for transfers between devices, to_swap(): return lax.ppermute(x, AXES, swap)  1.2 us
    ppermute x4, starting transfers between devices, to_swap(): return lax.ppermute(x, AXES, swap)  0.74 us
  transfers between devices with their start and end apart: 12, of which 7 were waited for; matrix products, arithmetic and copies ran while one was open for 1% of the time, Pallas kernels for 8%

profile of v5, /device:TPU:0, one launch (start us, length us, event | category | flops | bytes accessed | tf_op | source)
XLA Modules:
  0.0 31.0 jit_solution(17394515317592119696)
XLA Ops:
  0.0 1.5 %own_state.1 = (f32[2,128,128]{2,1,0:T(8,128)S(1)}, f32[2,128,128]{2,1,0:T(8,128)S(1)}, f32[2,128,128]{2,1,0:T(8,128)S(1)}, f32[2,128,128]{2,1,0:T(8,128)S(1)}) custom-call(s32[1]{0:T(128)} %bitcast.core_ref, bf16[128,1024]{1,0:T(8,128)(2,1)} %k_ref.1, bf16[128,1024]{1,0:T(8,128)(2,1)} %v_ref.1), custom_call_target="tpu_custom_call" | custom-call | tf_op jit(solution)/shard_map/own_state/pallas_call | solution.py:123
  1.5 0.5 %collective-permute-start = (f32[2,128,128]{2,1,0:T(8,128)S(1)}, f32[2,128,128]{2,1,0:T(8,128)S(1)}, u32[]{:S(2)}, u32[]{:S(2)}) collective-permute-start(f32[2,128,128]{2,1,0:T(8,128)S(1)} %get-tuple-element.13), channel_id=1, source_target_pairs={{0,1},{1,0},{2,3},{3,2},{4,5},{5,4},{6,7},{7,6},{8,9},{9,8},{10,11... | collective-permute-start | bytes 393224 | tf_op jit(solution)/shard_map/ppermute | solution.py:151
  2.0 0.1 collective-permute-start.4
  2.1 0.9 %collective-permute-done = f32[2,128,128]{2,1,0:T(8,128)S(1)} collective-permute-done((f32[2,128,128]{2,1,0:T(8,128)S(1)}, f32[2,128,128]{2,1,0:T(8,128)S(1)}, u32[]{:S(2)}, u32[]{:S(2)}) %collective-permute-start) | collective-permute-done | bytes 131104 | tf_op jit(solution)/shard_map/ppermute | solution.py:151
  3.0 2.9 %collective-permute-start.1 = (f32[2,128,128]{2,1,0:T(8,128)S(1)}, f32[2,128,128]{2,1,0:T(8,128)S(1)}, u32[]{:S(2)}, u32[]{:S(2)}) collective-permute-start(f32[2,128,128]{2,1,0:T(8,128)S(1)} %add.128), channel_id=1, source_target_pairs={{0,2},{1,9},{2,0},{3,11},{4,6},{5,13},{6,4},{7,15},{8,10},{9,1},{1... | collective-permute-start | bytes 393224 | tf_op jit(solution)/shard_map/ppermute | solution.py:182
  6.0 0.2 collective-permute-start.5
  6.2 2.7 %collective-permute-done.1 = f32[2,128,128]{2,1,0:T(8,128)S(1)} collective-permute-done((f32[2,128,128]{2,1,0:T(8,128)S(1)}, f32[2,128,128]{2,1,0:T(8,128)S(1)}, u32[]{:S(2)}, u32[]{:S(2)}) %collective-permute-start.1) | collective-permute-done | bytes 131104 | tf_op jit(solution)/shard_map/ppermute | solution.py:182
  8.9 2.1 %collective-permute-start.2 = (f32[2,128,128]{2,1,0:T(8,128)S(1)}, f32[2,128,128]{2,1,0:T(8,128)S(1)}, u32[]{:S(2)}, u32[]{:S(2)}) collective-permute-start(f32[2,128,128]{2,1,0:T(8,128)S(1)} %add.129), channel_id=1, source_target_pairs={{0,4},{1,17},{2,6},{3,19},{4,0},{5,21},{6,2},{7,23},{8,12},{9,25},... | collective-permute-start | bytes 393224 | tf_op jit(solution)/shard_map/ppermute | solution.py:182
  11.0 1.6 %collective-permute-start.6 = (f32[2,128,128]{2,1,0:T(8,128)S(1)}, f32[2,128,128]{2,1,0:T(8,128)S(1)}, u32[]{:S(2)}, u32[]{:S(2)}) collective-permute-start(f32[2,128,128]{2,1,0:T(8,128)S(1)} %get-tuple-element.21), channel_id=1, source_target_pairs={{0,4},{1,9},{2,6},{3,11},{4,0},{5,13},{6,2},{7,15},{8,12},{9,1},{1... | collective-permute-start | bytes 393224 | tf_op jit(solution)/shard_map/ppermute | solution.py:182
  12.6 1.4 %collective-permute-done.2 = f32[2,128,128]{2,1,0:T(8,128)S(1)} collective-permute-done((f32[2,128,128]{2,1,0:T(8,128)S(1)}, f32[2,128,128]{2,1,0:T(8,128)S(1)}, u32[]{:S(2)}, u32[]{:S(2)}) %collective-permute-start.2) | collective-permute-done | bytes 131104 | tf_op jit(solution)/shard_map/ppermute | solution.py:182
  14.0 2.1 %collective-permute-start.3 = (f32[2,128,128]{2,1,0:T(8,128)S(1)}, f32[2,128,128]{2,1,0:T(8,128)S(1)}, u32[]{:S(2)}, u32[]{:S(2)}) collective-permute-start(f32[2,128,128]{2,1,0:T(8,128)S(1)} %get-tuple-element.25), channel_id=1, source_target_pairs={{0,8},{1,5},{2,10},{3,7},{4,12},{5,1},{6,14},{7,3},{8,0},{9,13},{1... | collective-permute-start | bytes 393224 | tf_op jit(solution)/shard_map/ppermute | solution.py:182
  16.2 2.7 %collective-permute-start.7 = (f32[2,128,128]{2,1,0:T(8,128)S(1)}, f32[2,128,128]{2,1,0:T(8,128)S(1)}, u32[]{:S(2)}, u32[]{:S(2)}) collective-permute-start(f32[2,128,128]{2,1,0:T(8,128)S(1)} %add_select_fusion.1), channel_id=1, source_target_pairs={{0,16},{1,5},{2,18},{3,7},{4,20},{5,1},{6,22},{7,3},{8,24},{9,13},... | collective-permute-start | bytes 393224 | tf_op jit(solution)/shard_map/ppermute | solution.py:182
  18.9 0.2 collective-permute-done.3
  19.2 3.1 %collective-permute-start.10 = (f32[2,128,128]{2,1,0:T(8,128)S(1)}, f32[2,128,128]{2,1,0:T(8,128)S(1)}, u32[]{:S(2)}, u32[]{:S(2)}) collective-permute-start(f32[2,128,128]{2,1,0:T(8,128)S(1)} %add_select_fusion.4.late_ref), channel_id=1, source_target_pairs={{0,16},{1,3},{2,18},{3,1},{4,20},{5,7},{6,22},{7,5},{8,24},{9,11},... | collective-permute-start | bytes 393224 | tf_op jit(solution)/shard_map/ppermute | solution.py:182
  22.3 1.3 %collective-permute-done.7 = f32[2,128,128]{2,1,0:T(8,128)S(1)} collective-permute-done((f32[2,128,128]{2,1,0:T(8,128)S(1)}, f32[2,128,128]{2,1,0:T(8,128)S(1)}, u32[]{:S(2)}, u32[]{:S(2)}) %collective-permute-start.7) | collective-permute-done | bytes 131104 | tf_op jit(solution)/shard_map/ppermute | solution.py:182
  23.6 0.7 %collective-permute-start.8 = (f32[2,128,128]{2,1,0:T(8,128)S(1)}, f32[2,128,128]{2,1,0:T(8,128)S(1)}, u32[]{:S(2)}, u32[]{:S(2)}) collective-permute-start(f32[2,128,128]{2,1,0:T(8,128)S(1)} %add_select_fusion), channel_id=1, source_target_pairs={{0,8},{1,3},{2,10},{3,1},{4,12},{5,7},{6,14},{7,5},{8,0},{9,11},{1... | collective-permute-start | bytes 393224 | tf_op jit(solution)/shard_map/ppermute | solution.py:182
  24.4 1.4 %intra.1 = (bf16[128,1024]{1,0:T(8,128)(2,1)S(1)}, f32[128,1024]{1,0:T(8,128)S(1)}, f32[1,1024]{1,0:T(1,128)S(1)}) custom-call(bf16[128,1024]{1,0:T(8,128)(2,1)S(1)} %copy-done.2, bf16[128,1024]{1,0:T(8,128)(2,1)S(1)} %copy-done, bf16[128,1024]{1,0:T(8,128)(2,1)S(1)} %copy-done.1, f32[1,1024]{1,0:T(1,128)S(1)} %bitcast.2, ...), custom_call_target="tpu_custom_call" | custom-call | flops 67108864 | bytes 1572864 | tf_op jit(solution)/shard_map/intra/pallas_call | solution.py:189
  25.8 0.1 collective-permute-start.11
  25.9 2.8 %collective-permute-done.8 = f32[2,128,128]{2,1,0:T(8,128)S(1)} collective-permute-done((f32[2,128,128]{2,1,0:T(8,128)S(1)}, f32[2,128,128]{2,1,0:T(8,128)S(1)}, u32[]{:S(2)}, u32[]{:S(2)}) %collective-permute-start.8) | collective-permute-done | bytes 131104 | tf_op jit(solution)/shard_map/ppermute | solution.py:182
  28.6 0.1 select_add_fusion.3
  28.7 0.1 collective-permute-start.9
  28.8 1.0 %attend.2.refs_1_ = bf16[128,1024]{1,0:T(8,128)(2,1)} custom-call(s32[1]{0:T(128)} %bitcast.core_ref, bf16[128,1024]{1,0:T(8,128)(2,1)S(1)} %get-tuple-element.14.fq_ref, f32[128,1024]{1,0:T(8,128)S(1)} %get-tuple-element.15.intra_ref, f32[1,1024]{1,0:T(1,128)S(1)} %get-tuple-element.16.gain_ref, f32[2,128,128]{2,1,0:T(8,128)S(1)} %get-tuple-element.28.refs_0_, ...), custom_call_target="tpu_custom_call" | custom-call | flops 25165824 | bytes 393216 | tf_op jit(solution)/shard_map/attend/pallas_call | solution.py:209
  29.8 0.3 collective-permute-done.9.refs_0_
  30.1 0.9 %attend.3 = bf16[128,1024]{1,0:T(8,128)(2,1)} custom-call(s32[1]{0:T(128)} %bitcast.core_ref, bf16[128,1024]{1,0:T(8,128)(2,1)S(1)} %get-tuple-element.14.fq_ref, f32[128,1024]{1,0:T(8,128)S(1)} %get-tuple-element.15.intra_ref, f32[1,1024]{1,0:T(1,128)S(1)} %get-tuple-element.16.gain_ref, ...), custom_call_target="tpu_custom_call", output_to_operand_aliasing={{}: (5, {})} | custom-call | flops 8388608 | bytes 131072 | tf_op jit(solution)/shard_map/attend/pallas_call | solution.py:209
  (23 shorter events, 0.4 us)
Async XLA Ops:
  1.5 1.5 %collective-permute-start = (f32[2,128,128]{2,1,0:T(8,128)S(1)}, f32[2,128,128]{2,1,0:T(8,128)S(1)}, u32[]{:S(2)}, u32[]{:S(2)}) collective-permute-start(f32[2,128,128]{2,1,0:T(8,128)S(1)} %get-tuple-element.13), channel_id=1, source_target_pairs={{0,1},{1,0},{2,3},{3,2},{4,5},{5,4},{6,7},{7,6},{8,9},{9,8},{10,11... | collective-permute-start | bytes 393224 | tf_op jit(solution)/shard_map/ppermute | solution.py:151
  2.0 4.0 %collective-permute-start.4 = (f32[2,128,128]{2,1,0:T(8,128)S(1)}, f32[2,128,128]{2,1,0:T(8,128)S(1)}, u32[]{:S(2)}, u32[]{:S(2)}) collective-permute-start(f32[2,128,128]{2,1,0:T(8,128)S(1)} %get-tuple-element.18), channel_id=1, source_target_pairs={{0,1},{1,0},{2,3},{3,2},{4,5},{5,4},{6,7},{7,6},{8,9},{9,8},{10,11... | collective-permute-start | bytes 393224 | tf_op jit(solution)/shard_map/ppermute | solution.py:151
  3.0 5.9 %collective-permute-start.1 = (f32[2,128,128]{2,1,0:T(8,128)S(1)}, f32[2,128,128]{2,1,0:T(8,128)S(1)}, u32[]{:S(2)}, u32[]{:S(2)}) collective-permute-start(f32[2,128,128]{2,1,0:T(8,128)S(1)} %add.128), channel_id=1, source_target_pairs={{0,2},{1,9},{2,0},{3,11},{4,6},{5,13},{6,4},{7,15},{8,10},{9,1},{1... | collective-permute-start | bytes 393224 | tf_op jit(solution)/shard_map/ppermute | solution.py:182
  6.0 5.0 %collective-permute-start.5 = (f32[2,128,128]{2,1,0:T(8,128)S(1)}, f32[2,128,128]{2,1,0:T(8,128)S(1)}, u32[]{:S(2)}, u32[]{:S(2)}) collective-permute-start(f32[2,128,128]{2,1,0:T(8,128)S(1)} %get-tuple-element.23), channel_id=1, source_target_pairs={{0,2},{1,17},{2,0},{3,19},{4,6},{5,21},{6,4},{7,23},{8,10},{9,25},... | collective-permute-start | bytes 393224 | tf_op jit(solution)/shard_map/ppermute | solution.py:182
  8.9 5.0 %collective-permute-start.2 = (f32[2,128,128]{2,1,0:T(8,128)S(1)}, f32[2,128,128]{2,1,0:T(8,128)S(1)}, u32[]{:S(2)}, u32[]{:S(2)}) collective-permute-start(f32[2,128,128]{2,1,0:T(8,128)S(1)} %add.129), channel_id=1, source_target_pairs={{0,4},{1,17},{2,6},{3,19},{4,0},{5,21},{6,2},{7,23},{8,12},{9,25},... | collective-permute-start | bytes 393224 | tf_op jit(solution)/shard_map/ppermute | solution.py:182
  11.0 5.1 %collective-permute-start.6 = (f32[2,128,128]{2,1,0:T(8,128)S(1)}, f32[2,128,128]{2,1,0:T(8,128)S(1)}, u32[]{:S(2)}, u32[]{:S(2)}) collective-permute-start(f32[2,128,128]{2,1,0:T(8,128)S(1)} %get-tuple-element.21), channel_id=1, source_target_pairs={{0,4},{1,9},{2,6},{3,11},{4,0},{5,13},{6,2},{7,15},{8,12},{9,1},{1... | collective-permute-start | bytes 393224 | tf_op jit(solution)/shard_map/ppermute | solution.py:182
  14.0 5.1 %collective-permute-start.3 = (f32[2,128,128]{2,1,0:T(8,128)S(1)}, f32[2,128,128]{2,1,0:T(8,128)S(1)}, u32[]{:S(2)}, u32[]{:S(2)}) collective-permute-start(f32[2,128,128]{2,1,0:T(8,128)S(1)} %get-tuple-element.25), channel_id=1, source_target_pairs={{0,8},{1,5},{2,10},{3,7},{4,12},{5,1},{6,14},{7,3},{8,0},{9,13},{1... | collective-permute-start | bytes 393224 | tf_op jit(solution)/shard_map/ppermute | solution.py:182
  16.2 7.3 %collective-permute-start.7 = (f32[2,128,128]{2,1,0:T(8,128)S(1)}, f32[2,128,128]{2,1,0:T(8,128)S(1)}, u32[]{:S(2)}, u32[]{:S(2)}) collective-permute-start(f32[2,128,128]{2,1,0:T(8,128)S(1)} %add_select_fusion.1), channel_id=1, source_target_pairs={{0,16},{1,5},{2,18},{3,7},{4,20},{5,1},{6,22},{7,3},{8,24},{9,13},... | collective-permute-start | bytes 393224 | tf_op jit(solution)/shard_map/ppermute | solution.py:182
  19.1 5.2 %copy-start = (bf16[128,1024]{1,0:T(8,128)(2,1)S(1)}, bf16[128,1024]{1,0:T(8,128)(2,1)}, u32[]{:S(2)}) copy-start(bf16[128,1024]{1,0:T(8,128)(2,1)} %k_ref.1) | copy-start | bytes 786436
  19.1 5.2 %copy-start.1 = (bf16[128,1024]{1,0:T(8,128)(2,1)S(1)}, bf16[128,1024]{1,0:T(8,128)(2,1)}, u32[]{:S(2)}) copy-start(bf16[128,1024]{1,0:T(8,128)(2,1)} %v_ref.1) | copy-start | bytes 786436
  19.2 5.2 %copy-start.2 = (bf16[128,1024]{1,0:T(8,128)(2,1)S(1)}, bf16[128,1024]{1,0:T(8,128)(2,1)}, u32[]{:S(2)}) copy-start(bf16[128,1024]{1,0:T(8,128)(2,1)} %q_ref.1) | copy-start | bytes 786436
  19.2 6.5 %collective-permute-start.10 = (f32[2,128,128]{2,1,0:T(8,128)S(1)}, f32[2,128,128]{2,1,0:T(8,128)S(1)}, u32[]{:S(2)}, u32[]{:S(2)}) collective-permute-start(f32[2,128,128]{2,1,0:T(8,128)S(1)} %add_select_fusion.4.late_ref), channel_id=1, source_target_pairs={{0,16},{1,3},{2,18},{3,1},{4,20},{5,7},{6,22},{7,5},{8,24},{9,11},... | collective-permute-start | bytes 393224 | tf_op jit(solution)/shard_map/ppermute | solution.py:182
  23.5 0.8 %copy-start.3 = (f32[1024]{0:T(1024)S(1)}, f32[1024]{0:T(1024)}, u32[]{:S(2)}) copy-start(f32[1024]{0:T(1024)} %param.7) | copy-start | bytes 12292
  23.6 5.0 %collective-permute-start.8 = (f32[2,128,128]{2,1,0:T(8,128)S(1)}, f32[2,128,128]{2,1,0:T(8,128)S(1)}, u32[]{:S(2)}, u32[]{:S(2)}) collective-permute-start(f32[2,128,128]{2,1,0:T(8,128)S(1)} %add_select_fusion), channel_id=1, source_target_pairs={{0,8},{1,3},{2,10},{3,1},{4,12},{5,7},{6,14},{7,5},{8,0},{9,11},{1... | collective-permute-start | bytes 393224 | tf_op jit(solution)/shard_map/ppermute | solution.py:182
  25.8 3.0 %collective-permute-start.11 = (f32[2,128,128]{2,1,0:T(8,128)S(1)}, f32[2,128,128]{2,1,0:T(8,128)S(1)}, u32[]{:S(2)}, u32[]{:S(2)}) collective-permute-start(f32[2,128,128]{2,1,0:T(8,128)S(1)} %get-tuple-element.19), channel_id=1, source_target_pairs={{0,1},{1,0},{2,3},{3,2},{4,5},{5,4},{6,7},{7,6},{8,9},{9,8},{10,11... | collective-permute-start | bytes 393224 | tf_op jit(solution)/shard_map/ppermute | solution.py:151
  28.7 1.4 %collective-permute-start.9 = (f32[2,128,128]{2,1,0:T(8,128)S(1)}, f32[2,128,128]{2,1,0:T(8,128)S(1)}, u32[]{:S(2)}, u32[]{:S(2)}) collective-permute-start(f32[2,128,128]{2,1,0:T(8,128)S(1)} %get-tuple-element.29), channel_id=1, source_target_pairs={{0,1},{1,0},{2,3},{3,2},{4,5},{5,4},{6,7},{7,6},{8,9},{9,8},{10,11... | collective-permute-start | bytes 393224 | tf_op jit(solution)/shard_map/ppermute | solution.py:151

commit v6 on v4

--- a/solution.py
+++ b/solution.py
@@ -24,8 +24,17 @@
     return pl.ds(pl.multiple_of(h * HEAD_DIM, HEAD_DIM), HEAD_DIM)
 
 
-def state_kernel(core_ref, k_hbm, v_hbm, *refs):
-    out_refs, (k_ref, v_ref, sems) = refs[: 2 * CHUNKS], refs[2 * CHUNKS :]
+def states_of(half, core, k_ref, v_ref, out_refs):
+    for i in range(HALF):
+        cols = head_cols((core * HALF + half * HALF + i) % HEADS)
+        fk = features(k_ref[:, cols])
+        out_refs[i // PER][i % PER] = lax.dot_general(
+            fk, v_ref[:, cols], (((0,), (0,)), ((), ())), preferred_element_type=jnp.float32
+        )
+
+
+def theirs_kernel(core_ref, k_hbm, v_hbm, *refs):
+    out_refs, (k_ref, v_ref, sems) = refs[:CHUNKS], refs[CHUNKS:]
     copies = [
         pltpu.make_async_copy(k_hbm, k_ref, sems.at[0]),
         pltpu.make_async_copy(v_hbm, v_ref, sems.at[1]),
@@ -34,18 +43,16 @@
         copy.start()
     for copy in copies:
         copy.wait()
-    core = core_ref[0]
-    for half in (1, 0):
-        for i in range(HALF):
-            h = (core * HALF + half * HALF + i) % HEADS
-            fk = features(k_ref[:, head_cols(h)])
-            out_refs[half * CHUNKS + i // PER][i % PER] = lax.dot_general(
-                fk, v_ref[:, head_cols(h)], (((0,), (0,)), ((), ())), preferred_element_type=jnp.float32
-            )
-
-
-def intra_kernel(q_ref, k_ref, v_ref, late_ref, fq_ref, intra_ref):
+    states_of(1, core_ref[0], k_ref, v_ref, out_refs)
+
+
+def mine_kernel(core_ref, k_ref, v_ref, *out_refs):
+    states_of(0, core_ref[0], k_ref, v_ref, out_refs)
+
+
+def intra_kernel(q_ref, k_ref, v_ref, gain_ref, late_ref, fq_ref, intra_ref, near_gain_ref):
     del late_ref
+    near_gain_ref[...] = gain_ref[...]
     rows = q_ref.shape[0]
     causal = lax.broadcasted_iota(jnp.int32, (rows, rows), 0) >= lax.broadcasted_iota(jnp.int32, (rows, rows), 1)
     for h in range(HEADS):
@@ -115,19 +122,31 @@
     core_arr = core.reshape(1).astype(jnp.int32)
     f32 = jnp.float32
     part = jax.ShapeDtypeStruct((PER, HEAD_DIM, HEAD_DIM), f32)
-    states = pl.pallas_call(
-        state_kernel,
-        out_shape=[part] * (2 * CHUNKS),
+    *theirs, near_keys, near_values = pl.pallas_call(
+        theirs_kernel,
+        out_shape=[part] * CHUNKS + [jax.ShapeDtypeStruct(x.shape, x.dtype) for x in (keys, values)],
         in_specs=[SMEM, HBM, HBM],
-        out_specs=[VMEM] * (2 * CHUNKS),
-        scratch_shapes=[
-            pltpu.VMEM(keys.shape, keys.dtype),
-            pltpu.VMEM(values.shape, values.dtype),
-            pltpu.SemaphoreType.DMA((2,)),
-        ],
+        out_specs=[VMEM] * (CHUNKS + 2),
+        scratch_shapes=[pltpu.SemaphoreType.DMA((2,))],
         compiler_params=PARAMS,
-        name="own_state",
-    )(core_arr, pltpu.with_memory_space_constraint(keys, pltpu.HBM), pltpu.with_memory_space_constraint(values, pltpu.HBM))
+        name="theirs",
+    )(
+        core_arr,
+        pltpu.with_memory_space_constraint(keys, pltpu.HBM),
+        pltpu.with_memory_space_constraint(values, pltpu.HBM),
+    )
+    mine = pl.pallas_call(
+        mine_kernel,
+        out_shape=[part] * CHUNKS,
+        in_specs=[SMEM, VMEM, VMEM],
+        out_specs=[VMEM] * CHUNKS,
+        compiler_params=PARAMS,
+        cost_estimate=pl.CostEstimate(
+            flops=2 * HALF * rows * HEAD_DIM * HEAD_DIM, bytes_accessed=4 * keys.size, transcendentals=keys.size // 2
+        ),
+        name="mine",
+    )(core_arr, near_keys, near_values)
+
     low = levels_of(2, inner // 2)
     outer_levels = levels_of(inner, outer)
     low, high = low + outer_levels[:1], outer_levels[1:]
@@ -145,7 +164,6 @@
     def to_swap(x):
         return lax.ppermute(x, AXES, swap)
 
-    mine, theirs = states[:CHUNKS], states[CHUNKS:]
     partner = [to_swap(x) for x in theirs]
     own_parts, other_parts = [], []
     late = None
@@ -181,22 +199,21 @@
         own_parts.append(before + jnp.where(even, zero, partner[c]))
         other_parts.append(to_swap(before + jnp.where(even, mine[c], zero)))
 
-    fq, intra = pl.pallas_call(
+    fq, intra, gain = pl.pallas_call(
         intra_kernel,
         out_shape=[
             jax.ShapeDtypeStruct(queries.shape, jnp.bfloat16),
             jax.ShapeDtypeStruct(queries.shape, f32),
+            jax.ShapeDtypeStruct((1, queries.shape[1]), f32),
         ],
-        in_specs=[VMEM] * 3 + [ANY],
-        out_specs=[VMEM] * 2,
+        in_specs=[VMEM] * 4 + [ANY],
+        out_specs=[VMEM] * 3,
         compiler_params=PARAMS,
         cost_estimate=pl.CostEstimate(
             flops=4 * HEADS * rows * rows * HEAD_DIM, bytes_accessed=6 * queries.size * 2, transcendentals=queries.size * 2
         ),
         name="intra",
-    )(queries, keys, values, late)
-
-    gain = head_gain.reshape(1, -1)
+    )(queries, near_keys, near_values, head_gain.reshape(1, -1), late)
 
     def attend(jobs, parts, so_far=None):
         whole = jax.ShapeDtypeStruct(queries.shape, jnp.bfloat16)

time: 31.5 us -> 31 us (0.984)
  local copies, waits for them, and re-layouts: 0.69 us -> 0.01 us
    unnamed x8 -> x4, local copies, waits for them, and re-layouts: 0.69 us -> 0.01 us
    pallas_call x1 -> x2, Pallas kernels: 1.37 us -> 1.52 us  [the longest x1 1.28 us: per_device(): pl.pallas_call(theirs_kernel, out_shape=[part] * CHUNKS + [jax.ShapeDtype...]
  transfers between devices with their start and end apart: 12 -> 12, of which waited for: 6 -> 7; matrix products, arithmetic and copies ran while one was open for 1% -> 1% of each run, Pallas kernels for 8% -> 8%
where the time goes in v6:
time: 31 us; the launch traced here: 30.8 us
  starting transfers between devices  16.1 us (52%)
  waiting for transfers between devices  9.4 us (30%)
  Pallas kernels  4.78 us (15%)
  other arithmetic  0.4 us (1%)
    ppermute x8, starting transfers between devices, per_device(): got = lax.ppermute(message, AXES, perm)  15.4 us
    ppermute x8, waiting for transfers between devices, per_device(): got = lax.ppermute(message, AXES, perm)  8.44 us
    pallas_call x2, Pallas kernels, attend(): pl.pallas_call(functools.partial(attend_kernel, jobs), out_shape=whole, i...  1.9 us
    pallas_call x1, Pallas kernels, per_device(): pl.pallas_call(intra_kernel, out_shape=[jax.ShapeDtypeStruct(queries.shap...  1.36 us
    pallas_call x1, Pallas kernels, per_device(): pl.pallas_call(theirs_kernel, out_shape=[part] * CHUNKS + [jax.ShapeDtype...  1.28 us
    ppermute x4, waiting for transfers between devices, to_swap(): return lax.ppermute(x, AXES, swap)  0.96 us
    ppermute x4, starting transfers between devices, to_swap(): return lax.ppermute(x, AXES, swap)  0.74 us
  transfers between devices with their start and end apart: 12, of which 7 were waited for; matrix products, arithmetic and copies ran while one was open for 1% of the time, Pallas kernels for 8%

profile of v6, /device:TPU:0, one launch (start us, length us, event | category | flops | bytes accessed | tf_op | source)
XLA Modules:
  0.0 30.8 jit_solution(12093917940065446062)
XLA Ops:
  0.0 1.3 %theirs.1 = (f32[2,128,128]{2,1,0:T(8,128)S(1)}, f32[2,128,128]{2,1,0:T(8,128)S(1)}, bf16[128,1024]{1,0:T(8,128)(2,1)S(1)}, bf16[128,1024]{1,0:T(8,128)(2,1)S(1)}) custom-call(s32[1]{0:T(128)} %bitcast.core_ref, bf16[128,1024]{1,0:T(8,128)(2,1)} %k_hbm.1, bf16[128,1024]{1,0:T(8,128)(2,1)} %v_hbm.1), custom_call_target="tpu_custom_call" | custom-call | tf_op jit(solution)/shard_map/theirs/pallas_call | solution.py:125
  1.3 0.5 %collective-permute-start = (f32[2,128,128]{2,1,0:T(8,128)S(1)}, f32[2,128,128]{2,1,0:T(8,128)S(1)}, u32[]{:S(2)}, u32[]{:S(2)}) collective-permute-start(f32[2,128,128]{2,1,0:T(8,128)S(1)} %get-tuple-element.17), channel_id=1, source_target_pairs={{0,1},{1,0},{2,3},{3,2},{4,5},{5,4},{6,7},{7,6},{8,9},{9,8},{10,11... | collective-permute-start | bytes 393224 | tf_op jit(solution)/shard_map/ppermute | solution.py:165
  1.8 0.1 collective-permute-start.4
  1.9 0.2 mine.1
  2.1 0.7 %collective-permute-done = f32[2,128,128]{2,1,0:T(8,128)S(1)} collective-permute-done((f32[2,128,128]{2,1,0:T(8,128)S(1)}, f32[2,128,128]{2,1,0:T(8,128)S(1)}, u32[]{:S(2)}, u32[]{:S(2)}) %collective-permute-start) | collective-permute-done | bytes 131104 | tf_op jit(solution)/shard_map/ppermute | solution.py:165
  2.8 2.9 %collective-permute-start.1 = (f32[2,128,128]{2,1,0:T(8,128)S(1)}, f32[2,128,128]{2,1,0:T(8,128)S(1)}, u32[]{:S(2)}, u32[]{:S(2)}) collective-permute-start(f32[2,128,128]{2,1,0:T(8,128)S(1)} %add.128), channel_id=1, source_target_pairs={{0,2},{1,9},{2,0},{3,11},{4,6},{5,13},{6,4},{7,15},{8,10},{9,1},{1... | collective-permute-start | bytes 393224 | tf_op jit(solution)/shard_map/ppermute | solution.py:195
  5.8 0.2 collective-permute-start.5
  6.0 2.7 %collective-permute-done.1 = f32[2,128,128]{2,1,0:T(8,128)S(1)} collective-permute-done((f32[2,128,128]{2,1,0:T(8,128)S(1)}, f32[2,128,128]{2,1,0:T(8,128)S(1)}, u32[]{:S(2)}, u32[]{:S(2)}) %collective-permute-start.1) | collective-permute-done | bytes 131104 | tf_op jit(solution)/shard_map/ppermute | solution.py:195
  8.7 2.1 %collective-permute-start.2 = (f32[2,128,128]{2,1,0:T(8,128)S(1)}, f32[2,128,128]{2,1,0:T(8,128)S(1)}, u32[]{:S(2)}, u32[]{:S(2)}) collective-permute-start(f32[2,128,128]{2,1,0:T(8,128)S(1)} %add.129), channel_id=1, source_target_pairs={{0,4},{1,17},{2,6},{3,19},{4,0},{5,21},{6,2},{7,23},{8,12},{9,25},... | collective-permute-start | bytes 393224 | tf_op jit(solution)/shard_map/ppermute | solution.py:195
  10.8 1.6 %collective-permute-start.6 = (f32[2,128,128]{2,1,0:T(8,128)S(1)}, f32[2,128,128]{2,1,0:T(8,128)S(1)}, u32[]{:S(2)}, u32[]{:S(2)}) collective-permute-start(f32[2,128,128]{2,1,0:T(8,128)S(1)} %get-tuple-element.25), channel_id=1, source_target_pairs={{0,4},{1,9},{2,6},{3,11},{4,0},{5,13},{6,2},{7,15},{8,12},{9,1},{1... | collective-permute-start | bytes 393224 | tf_op jit(solution)/shard_map/ppermute | solution.py:195
  12.4 1.4 %collective-permute-done.2 = f32[2,128,128]{2,1,0:T(8,128)S(1)} collective-permute-done((f32[2,128,128]{2,1,0:T(8,128)S(1)}, f32[2,128,128]{2,1,0:T(8,128)S(1)}, u32[]{:S(2)}, u32[]{:S(2)}) %collective-permute-start.2) | collective-permute-done | bytes 131104 | tf_op jit(solution)/shard_map/ppermute | solution.py:195
  13.8 2.1 %collective-permute-start.3 = (f32[2,128,128]{2,1,0:T(8,128)S(1)}, f32[2,128,128]{2,1,0:T(8,128)S(1)}, u32[]{:S(2)}, u32[]{:S(2)}) collective-permute-start(f32[2,128,128]{2,1,0:T(8,128)S(1)} %get-tuple-element.29), channel_id=1, source_target_pairs={{0,8},{1,5},{2,10},{3,7},{4,12},{5,1},{6,14},{7,3},{8,0},{9,13},{1... | collective-permute-start | bytes 393224 | tf_op jit(solution)/shard_map/ppermute | solution.py:195
  16.0 2.7 %collective-permute-start.7 = (f32[2,128,128]{2,1,0:T(8,128)S(1)}, f32[2,128,128]{2,1,0:T(8,128)S(1)}, u32[]{:S(2)}, u32[]{:S(2)}) collective-permute-start(f32[2,128,128]{2,1,0:T(8,128)S(1)} %add_select_fusion.1), channel_id=1, source_target_pairs={{0,16},{1,5},{2,18},{3,7},{4,20},{5,1},{6,22},{7,3},{8,24},{9,13},... | collective-permute-start | bytes 393224 | tf_op jit(solution)/shard_map/ppermute | solution.py:195
  18.7 0.2 collective-permute-done.3
  19.0 3.1 %collective-permute-start.10 = (f32[2,128,128]{2,1,0:T(8,128)S(1)}, f32[2,128,128]{2,1,0:T(8,128)S(1)}, u32[]{:S(2)}, u32[]{:S(2)}) collective-permute-start(f32[2,128,128]{2,1,0:T(8,128)S(1)} %add_select_fusion.4.late_ref), channel_id=1, source_target_pairs={{0,16},{1,3},{2,18},{3,1},{4,20},{5,7},{6,22},{7,5},{8,24},{9,11},... | collective-permute-start | bytes 393224 | tf_op jit(solution)/shard_map/ppermute | solution.py:195
  22.0 1.3 %collective-permute-done.7 = f32[2,128,128]{2,1,0:T(8,128)S(1)} collective-permute-done((f32[2,128,128]{2,1,0:T(8,128)S(1)}, f32[2,128,128]{2,1,0:T(8,128)S(1)}, u32[]{:S(2)}, u32[]{:S(2)}) %collective-permute-start.7) | collective-permute-done | bytes 131104 | tf_op jit(solution)/shard_map/ppermute | solution.py:195
  23.4 0.7 %collective-permute-start.8 = (f32[2,128,128]{2,1,0:T(8,128)S(1)}, f32[2,128,128]{2,1,0:T(8,128)S(1)}, u32[]{:S(2)}, u32[]{:S(2)}) collective-permute-start(f32[2,128,128]{2,1,0:T(8,128)S(1)} %add_select_fusion), channel_id=1, source_target_pairs={{0,8},{1,3},{2,10},{3,1},{4,12},{5,7},{6,14},{7,5},{8,0},{9,11},{1... | collective-permute-start | bytes 393224 | tf_op jit(solution)/shard_map/ppermute | solution.py:195
  24.2 1.4 %intra.1 = (bf16[128,1024]{1,0:T(8,128)(2,1)S(1)}, f32[128,1024]{1,0:T(8,128)S(1)}, f32[1,1024]{1,0:T(1,128)S(1)}) custom-call(bf16[128,1024]{1,0:T(8,128)(2,1)S(1)} %copy-done, bf16[128,1024]{1,0:T(8,128)(2,1)S(1)} %get-tuple-element.14.k_ref, bf16[128,1024]{1,0:T(8,128)(2,1)S(1)} %get-tuple-element.15.v_ref, f32[1,1024]{1,0:T(1,128)S(1)} %bitcast.2, ...), custom_call_target="tpu_custom_call" | custom-call | flops 67108864 | bytes 1572864 | tf_op jit(solution)/shard_map/intra/pallas_call | solution.py:202
  25.6 0.1 collective-permute-start.11
  25.6 2.8 %collective-permute-done.8 = f32[2,128,128]{2,1,0:T(8,128)S(1)} collective-permute-done((f32[2,128,128]{2,1,0:T(8,128)S(1)}, f32[2,128,128]{2,1,0:T(8,128)S(1)}, u32[]{:S(2)}, u32[]{:S(2)}) %collective-permute-start.8) | collective-permute-done | bytes 131104 | tf_op jit(solution)/shard_map/ppermute | solution.py:195
  28.5 0.1 collective-permute-start.9
  28.6 1.0 %attend.2.refs_1_ = bf16[128,1024]{1,0:T(8,128)(2,1)} custom-call(s32[1]{0:T(128)} %bitcast.core_ref, bf16[128,1024]{1,0:T(8,128)(2,1)S(1)} %get-tuple-element.18.fq_ref, f32[128,1024]{1,0:T(8,128)S(1)} %get-tuple-element.19.intra_ref, f32[1,1024]{1,0:T(1,128)S(1)} %get-tuple-element.20.gain_ref, f32[2,128,128]{2,1,0:T(8,128)S(1)} %get-tuple-element.32.refs_0_, ...), custom_call_target="tpu_custom_call" | custom-call | flops 25165824 | bytes 393216 | tf_op jit(solution)/shard_map/attend/pallas_call | solution.py:222
  29.6 0.3 collective-permute-done.9.refs_0_
  29.9 0.9 %attend.3 = bf16[128,1024]{1,0:T(8,128)(2,1)} custom-call(s32[1]{0:T(128)} %bitcast.core_ref, bf16[128,1024]{1,0:T(8,128)(2,1)S(1)} %get-tuple-element.18.fq_ref, f32[128,1024]{1,0:T(8,128)S(1)} %get-tuple-element.19.intra_ref, f32[1,1024]{1,0:T(1,128)S(1)} %get-tuple-element.20.gain_ref, ...), custom_call_target="tpu_custom_call", output_to_operand_aliasing={{}: (5, {})} | custom-call | flops 8388608 | bytes 131072 | tf_op jit(solution)/shard_map/attend/pallas_call | solution.py:222
  (20 shorter events, 0.5 us)
Async XLA Ops:
  1.3 1.5 %collective-permute-start = (f32[2,128,128]{2,1,0:T(8,128)S(1)}, f32[2,128,128]{2,1,0:T(8,128)S(1)}, u32[]{:S(2)}, u32[]{:S(2)}) collective-permute-start(f32[2,128,128]{2,1,0:T(8,128)S(1)} %get-tuple-element.17), channel_id=1, source_target_pairs={{0,1},{1,0},{2,3},{3,2},{4,5},{5,4},{6,7},{7,6},{8,9},{9,8},{10,11... | collective-permute-start | bytes 393224 | tf_op jit(solution)/shard_map/ppermute | solution.py:165
  1.8 4.0 %collective-permute-start.4 = (f32[2,128,128]{2,1,0:T(8,128)S(1)}, f32[2,128,128]{2,1,0:T(8,128)S(1)}, u32[]{:S(2)}, u32[]{:S(2)}) collective-permute-start(f32[2,128,128]{2,1,0:T(8,128)S(1)} %get-tuple-element.22), channel_id=1, source_target_pairs={{0,1},{1,0},{2,3},{3,2},{4,5},{5,4},{6,7},{7,6},{8,9},{9,8},{10,11... | collective-permute-start | bytes 393224 | tf_op jit(solution)/shard_map/ppermute | solution.py:165
  2.8 5.9 %collective-permute-start.1 = (f32[2,128,128]{2,1,0:T(8,128)S(1)}, f32[2,128,128]{2,1,0:T(8,128)S(1)}, u32[]{:S(2)}, u32[]{:S(2)}) collective-permute-start(f32[2,128,128]{2,1,0:T(8,128)S(1)} %add.128), channel_id=1, source_target_pairs={{0,2},{1,9},{2,0},{3,11},{4,6},{5,13},{6,4},{7,15},{8,10},{9,1},{1... | collective-permute-start | bytes 393224 | tf_op jit(solution)/shard_map/ppermute | solution.py:195
  5.8 5.0 %collective-permute-start.5 = (f32[2,128,128]{2,1,0:T(8,128)S(1)}, f32[2,128,128]{2,1,0:T(8,128)S(1)}, u32[]{:S(2)}, u32[]{:S(2)}) collective-permute-start(f32[2,128,128]{2,1,0:T(8,128)S(1)} %get-tuple-element.27), channel_id=1, source_target_pairs={{0,2},{1,17},{2,0},{3,19},{4,6},{5,21},{6,4},{7,23},{8,10},{9,25},... | collective-permute-start | bytes 393224 | tf_op jit(solution)/shard_map/ppermute | solution.py:195
  8.7 5.0 %collective-permute-start.2 = (f32[2,128,128]{2,1,0:T(8,128)S(1)}, f32[2,128,128]{2,1,0:T(8,128)S(1)}, u32[]{:S(2)}, u32[]{:S(2)}) collective-permute-start(f32[2,128,128]{2,1,0:T(8,128)S(1)} %add.129), channel_id=1, source_target_pairs={{0,4},{1,17},{2,6},{3,19},{4,0},{5,21},{6,2},{7,23},{8,12},{9,25},... | collective-permute-start | bytes 393224 | tf_op jit(solution)/shard_map/ppermute | solution.py:195
  10.8 5.1 %collective-permute-start.6 = (f32[2,128,128]{2,1,0:T(8,128)S(1)}, f32[2,128,128]{2,1,0:T(8,128)S(1)}, u32[]{:S(2)}, u32[]{:S(2)}) collective-permute-start(f32[2,128,128]{2,1,0:T(8,128)S(1)} %get-tuple-element.25), channel_id=1, source_target_pairs={{0,4},{1,9},{2,6},{3,11},{4,0},{5,13},{6,2},{7,15},{8,12},{9,1},{1... | collective-permute-start | bytes 393224 | tf_op jit(solution)/shard_map/ppermute | solution.py:195
  13.8 5.1 %collective-permute-start.3 = (f32[2,128,128]{2,1,0:T(8,128)S(1)}, f32[2,128,128]{2,1,0:T(8,128)S(1)}, u32[]{:S(2)}, u32[]{:S(2)}) collective-permute-start(f32[2,128,128]{2,1,0:T(8,128)S(1)} %get-tuple-element.29), channel_id=1, source_target_pairs={{0,8},{1,5},{2,10},{3,7},{4,12},{5,1},{6,14},{7,3},{8,0},{9,13},{1... | collective-permute-start | bytes 393224 | tf_op jit(solution)/shard_map/ppermute | solution.py:195
  16.0 7.3 %collective-permute-start.7 = (f32[2,128,128]{2,1,0:T(8,128)S(1)}, f32[2,128,128]{2,1,0:T(8,128)S(1)}, u32[]{:S(2)}, u32[]{:S(2)}) collective-permute-start(f32[2,128,128]{2,1,0:T(8,128)S(1)} %add_select_fusion.1), channel_id=1, source_target_pairs={{0,16},{1,5},{2,18},{3,7},{4,20},{5,1},{6,22},{7,3},{8,24},{9,13},... | collective-permute-start | bytes 393224 | tf_op jit(solution)/shard_map/ppermute | solution.py:195
  18.9 5.2 %copy-start = (bf16[128,1024]{1,0:T(8,128)(2,1)S(1)}, bf16[128,1024]{1,0:T(8,128)(2,1)}, u32[]{:S(2)}) copy-start(bf16[128,1024]{1,0:T(8,128)(2,1)} %q_ref.1) | copy-start | bytes 786436
  19.0 6.6 %collective-permute-start.10 = (f32[2,128,128]{2,1,0:T(8,128)S(1)}, f32[2,128,128]{2,1,0:T(8,128)S(1)}, u32[]{:S(2)}, u32[]{:S(2)}) collective-permute-start(f32[2,128,128]{2,1,0:T(8,128)S(1)} %add_select_fusion.4.late_ref), channel_id=1, source_target_pairs={{0,16},{1,3},{2,18},{3,1},{4,20},{5,7},{6,22},{7,5},{8,24},{9,11},... | collective-permute-start | bytes 393224 | tf_op jit(solution)/shard_map/ppermute | solution.py:195
  23.3 0.8 %copy-start.1 = (f32[1024]{0:T(1024)S(1)}, f32[1024]{0:T(1024)}, u32[]{:S(2)}) copy-start(f32[1024]{0:T(1024)} %param.7) | copy-start | bytes 12292
  23.4 5.0 %collective-permute-start.8 = (f32[2,128,128]{2,1,0:T(8,128)S(1)}, f32[2,128,128]{2,1,0:T(8,128)S(1)}, u32[]{:S(2)}, u32[]{:S(2)}) collective-permute-start(f32[2,128,128]{2,1,0:T(8,128)S(1)} %add_select_fusion), channel_id=1, source_target_pairs={{0,8},{1,3},{2,10},{3,1},{4,12},{5,7},{6,14},{7,5},{8,0},{9,11},{1... | collective-permute-start | bytes 393224 | tf_op jit(solution)/shard_map/ppermute | solution.py:195
  25.6 3.0 %collective-permute-start.11 = (f32[2,128,128]{2,1,0:T(8,128)S(1)}, f32[2,128,128]{2,1,0:T(8,128)S(1)}, u32[]{:S(2)}, u32[]{:S(2)}) collective-permute-start(f32[2,128,128]{2,1,0:T(8,128)S(1)} %get-tuple-element.23), channel_id=1, source_target_pairs={{0,1},{1,0},{2,3},{3,2},{4,5},{5,4},{6,7},{7,6},{8,9},{9,8},{10,11... | collective-permute-start | bytes 393224 | tf_op jit(solution)/shard_map/ppermute | solution.py:165
  28.5 1.4 %collective-permute-start.9 = (f32[2,128,128]{2,1,0:T(8,128)S(1)}, f32[2,128,128]{2,1,0:T(8,128)S(1)}, u32[]{:S(2)}, u32[]{:S(2)}) collective-permute-start(f32[2,128,128]{2,1,0:T(8,128)S(1)} %get-tuple-element.33), channel_id=1, source_target_pairs={{0,1},{1,0},{2,3},{3,2},{4,5},{5,4},{6,7},{7,6},{8,9},{9,8},{10,11... | collective-permute-start | bytes 393224 | tf_op jit(solution)/shard_map/ppermute | solution.py:165

commit v7 on v6

--- a/solution.py
+++ b/solution.py
@@ -1,4 +1,5 @@
 import functools
+import itertools
 
 import jax
 import jax.numpy as jnp
@@ -12,6 +13,9 @@
 HALF = HEADS // 2
 CHUNKS = 2
 PER = HALF // CHUNKS
+LAST_CHUNK = 1
+LATE_CHUNK = 1
+LATE_STEP = -1
 AXES = ("outer", "inner")
 
 
@@ -152,10 +156,7 @@
     low, high = low + outer_levels[:1], outer_levels[1:]
     total_low, total_high = [("total", v) for v in low], [("total", v) for v in high]
     prefix_low, prefix_high = [("prefix", v) for v in low[::-1]], [("prefix", v) for v in high[::-1]]
-    orders = [
-        (total_low + prefix_high, prefix_high + prefix_low),
-        (total_low + total_high, total_high + prefix_low),
-    ]
+    orders = [(total_high, total_high), (prefix_high, prefix_high)]
     swap = [(i, i ^ 1) for i in range(n)]
 
     def digit(step):
@@ -164,21 +165,15 @@
     def to_swap(x):
         return lax.ppermute(x, AXES, swap)
 
-    partner = [to_swap(x) for x in theirs]
-    own_parts, other_parts = [], []
-    late = None
-    for c in range(CHUNKS):
-        base = mine[c] + partner[c]
-        zero = jnp.zeros_like(base)
-        evens, odds = (steps_of(order) for order in orders[c % 2])
-        before, apart, total, unit = zero, zero, base, base
-        switched, entered = False, [None, None]
-        for j, (up, down) in enumerate(zip(evens, odds, strict=True)):
-            if up[0] == "prefix" and not switched:
-                switched = True
-                before, apart, unit = jnp.where(even, zero, before), jnp.where(even, before, zero), jnp.where(even, total, base)
+    def scan(evens, odds, before, unit):
+        zero, total, entered, sent = jnp.zeros_like(unit), unit, [None, None], []
+        for steps in itertools.zip_longest(steps_of(evens), steps_of(odds)):
             messages, kept = [], []
-            for q, step in enumerate((up, down)):
+            for q, step in enumerate(steps):
+                if step is None:
+                    messages.append(zero)
+                    kept.append(jnp.bool_(True))
+                    continue
                 kind, _, radix, shift = step
                 if shift == 1:
                     entered[q] = total if kind == "total" else before
@@ -188,16 +183,31 @@
                 else:
                     messages.append(entered[q] + jnp.where(digit(step) + shift < radix, unit, zero))
                     kept.append(jnp.bool_(True))
-            perm = [(i, target(down if i % 2 else up, i)) for i in range(n)]
-            message = jnp.where(even, messages[0], messages[1])
-            if c == CHUNKS - 1 and j == len(evens) - 1:
-                late = message
-            got = lax.ppermute(message, AXES, perm)
+            perm = [(i, target(steps[i % 2], i)) for i in range(n) if steps[i % 2] is not None]
+            sent.append(jnp.where(even, messages[0], messages[1]))
+            got = lax.ppermute(sent[-1], AXES, perm)
             before = before + jnp.where(jnp.where(even, kept[0], kept[1]), got, zero)
             total = total + got
-        before = before + apart
-        own_parts.append(before + jnp.where(even, zero, partner[c]))
-        other_parts.append(to_swap(before + jnp.where(even, mine[c], zero)))
+        return before, total, sent
+
+    partner = [to_swap(x) for x in theirs]
+    mine_parts, their_parts = [], []
+    late = None
+    for c in range(CHUNKS):
+        first, second = orders[c % 2]
+        zero = jnp.zeros_like(mine[c])
+        before, total, _ = scan(total_low, first, zero, mine[c] + partner[c])
+        swapped = to_swap(
+            jnp.concatenate([jnp.where(even, total, before), mine[c] + jnp.where(even, before, zero)])
+        )
+        got, more = swapped[:PER], swapped[PER:]
+        after, _, sent = scan(
+            prefix_low, second, jnp.where(even, got, zero), jnp.where(even, theirs[c] + more, got)
+        )
+        if c == LATE_CHUNK:
+            late = sent[LATE_STEP]
+        mine_parts.append(to_swap(after) + jnp.where(even, before, partner[c]))
+        their_parts.append(after + jnp.where(even, zero, more))
 
     fq, intra, gain = pl.pallas_call(
         intra_kernel,
@@ -236,9 +246,9 @@
             name="attend",
         )(*given)
 
-    early = [(0, c) for c in range(CHUNKS)] + [(1, c) for c in range(1, CHUNKS)]
-    most = attend(early, own_parts + other_parts[1:])
-    return attend([(1, 0)], other_parts[:1], most)
+    early = [(1, c) for c in range(CHUNKS)] + [(0, c) for c in range(CHUNKS) if c != LAST_CHUNK]
+    most = attend(early, their_parts + [x for c, x in enumerate(mine_parts) if c != LAST_CHUNK])
+    return attend([(0, LAST_CHUNK)], [mine_parts[LAST_CHUNK]], most)
 
 
 def solution(mesh):

time: 31 us -> 30.6 us (0.987)
  starting transfers between devices: 16.1 us -> 14.9 us
  waiting for transfers between devices: 9.4 us -> 10.2 us
    ppermute x8, starting transfers between devices: 15.4 us -> 12.6 us  [scan(): got = lax.ppermute(sent[-1], AXES, perm)]
    ppermute x4 -> x6, starting transfers between devices: 0.74 us -> 2.26 us  [to_swap(): return lax.ppermute(x, AXES, swap)]
    ppermute x8, waiting for transfers between devices: 8.44 us -> 9.53 us  [scan(): got = lax.ppermute(sent[-1], AXES, perm)]
    ppermute x4 -> x6, waiting for transfers between devices: 0.96 us -> 0.68 us  [to_swap(): return lax.ppermute(x, AXES, swap)]
  transfers between devices with their start and end apart: 12 -> 14, of which waited for: 7 -> 7; matrix products, arithmetic and copies ran while one was open for 1% -> 1% of each run, Pallas kernels for 8% -> 9%
where the time goes in v7:
time: 30.6 us; the launch traced here: 30.5 us
  starting transfers between devices  14.9 us (49%)
  waiting for transfers between devices  10.2 us (33%)
  Pallas kernels  4.79 us (16%)
  other arithmetic  0.47 us (2%)
    ppermute x8, starting transfers between devices, scan(): got = lax.ppermute(sent[-1], AXES, perm)  12.6 us
    ppermute x8, waiting for transfers between devices, scan(): got = lax.ppermute(sent[-1], AXES, perm)  9.53 us
    ppermute x6, starting transfers between devices, to_swap(): return lax.ppermute(x, AXES, swap)  2.26 us
    pallas_call x2, Pallas kernels, attend(): pl.pallas_call(functools.partial(attend_kernel, jobs), out_shape=whole, i...  1.91 us
    pallas_call x1, Pallas kernels, per_device(): pl.pallas_call(intra_kernel, out_shape=[jax.ShapeDtypeStruct(queries.shap...  1.36 us
    pallas_call x1, Pallas kernels, per_device(): pl.pallas_call(theirs_kernel, out_shape=[part] * CHUNKS + [jax.ShapeDtype...  1.28 us
    ppermute x6, waiting for transfers between devices, to_swap(): return lax.ppermute(x, AXES, swap)  0.68 us
  transfers between devices with their start and end apart: 14, of which 7 were waited for; matrix products, arithmetic and copies ran while one was open for 1% of the time, Pallas kernels for 9%

profile of v7, /device:TPU:0, one launch (start us, length us, event | category | flops | bytes accessed | tf_op | source)
XLA Modules:
  0.0 30.5 jit_solution(15625550213518904822)
XLA Ops:
  0.0 1.3 %theirs.1 = (f32[2,128,128]{2,1,0:T(8,128)S(1)}, f32[2,128,128]{2,1,0:T(8,128)S(1)}, bf16[128,1024]{1,0:T(8,128)(2,1)S(1)}, bf16[128,1024]{1,0:T(8,128)(2,1)S(1)}) custom-call(s32[1]{0:T(128)} %bitcast.core_ref, bf16[128,1024]{1,0:T(8,128)(2,1)} %k_hbm.1, bf16[128,1024]{1,0:T(8,128)(2,1)} %v_hbm.1), custom_call_target="tpu_custom_call" | custom-call | tf_op jit(solution)/shard_map/theirs/pallas_call | solution.py:129
  1.3 0.5 %collective-permute-start.7 = (f32[2,128,128]{2,1,0:T(8,128)S(1)}, f32[2,128,128]{2,1,0:T(8,128)S(1)}, u32[]{:S(2)}, u32[]{:S(2)}) collective-permute-start(f32[2,128,128]{2,1,0:T(8,128)S(1)} %get-tuple-element.22), channel_id=1, source_target_pairs={{0,1},{1,0},{2,3},{3,2},{4,5},{5,4},{6,7},{7,6},{8,9},{9,8},{10,11... | collective-permute-start | bytes 393224 | tf_op jit(solution)/shard_map/ppermute | solution.py:166
  1.9 0.2 mine.1
  2.1 0.7 %collective-permute-done.7 = f32[2,128,128]{2,1,0:T(8,128)S(1)} collective-permute-done((f32[2,128,128]{2,1,0:T(8,128)S(1)}, f32[2,128,128]{2,1,0:T(8,128)S(1)}, u32[]{:S(2)}, u32[]{:S(2)}) %collective-permute-start.7) | collective-permute-done | bytes 131104 | tf_op jit(solution)/shard_map/ppermute | solution.py:166
  2.8 2.9 %collective-permute-start.8 = (f32[2,128,128]{2,1,0:T(8,128)S(1)}, f32[2,128,128]{2,1,0:T(8,128)S(1)}, u32[]{:S(2)}, u32[]{:S(2)}) collective-permute-start(f32[2,128,128]{2,1,0:T(8,128)S(1)} %add.159), channel_id=1, source_target_pairs={{0,2},{1,9},{2,0},{3,11},{4,6},{5,13},{6,4},{7,15},{8,10},{9,1},{1... | collective-permute-start | bytes 393224 | tf_op jit(solution)/shard_map/ppermute | solution.py:188
  5.8 0.2 collective-permute-start.1
  6.0 2.7 %collective-permute-done.8 = f32[2,128,128]{2,1,0:T(8,128)S(1)} collective-permute-done((f32[2,128,128]{2,1,0:T(8,128)S(1)}, f32[2,128,128]{2,1,0:T(8,128)S(1)}, u32[]{:S(2)}, u32[]{:S(2)}) %collective-permute-start.8) | collective-permute-done | bytes 131104 | tf_op jit(solution)/shard_map/ppermute | solution.py:188
  8.7 2.1 %collective-permute-start.9 = (f32[2,128,128]{2,1,0:T(8,128)S(1)}, f32[2,128,128]{2,1,0:T(8,128)S(1)}, u32[]{:S(2)}, u32[]{:S(2)}) collective-permute-start(f32[2,128,128]{2,1,0:T(8,128)S(1)} %add.160), channel_id=1, source_target_pairs={{0,4},{1,17},{2,6},{3,19},{4,0},{5,21},{6,2},{7,23},{8,12},{9,25},... | collective-permute-start | bytes 393224 | tf_op jit(solution)/shard_map/ppermute | solution.py:188
  10.8 1.6 %collective-permute-start.2 = (f32[2,128,128]{2,1,0:T(8,128)S(1)}, f32[2,128,128]{2,1,0:T(8,128)S(1)}, u32[]{:S(2)}, u32[]{:S(2)}) collective-permute-start(f32[2,128,128]{2,1,0:T(8,128)S(1)} %get-tuple-element.27), channel_id=1, source_target_pairs={{0,4},{1,9},{2,6},{3,11},{4,0},{5,13},{6,2},{7,15},{8,12},{9,1},{1... | collective-permute-start | bytes 393224 | tf_op jit(solution)/shard_map/ppermute | solution.py:188
  12.4 1.4 %collective-permute-done.9 = f32[2,128,128]{2,1,0:T(8,128)S(1)} collective-permute-done((f32[2,128,128]{2,1,0:T(8,128)S(1)}, f32[2,128,128]{2,1,0:T(8,128)S(1)}, u32[]{:S(2)}, u32[]{:S(2)}) %collective-permute-start.9) | collective-permute-done | bytes 131104 | tf_op jit(solution)/shard_map/ppermute | solution.py:188
  13.9 2.0 %collective-permute-done.2 = f32[2,128,128]{2,1,0:T(8,128)S(1)} collective-permute-done((f32[2,128,128]{2,1,0:T(8,128)S(1)}, f32[2,128,128]{2,1,0:T(8,128)S(1)}, u32[]{:S(2)}, u32[]{:S(2)}) %collective-permute-start.2) | collective-permute-done | bytes 131104 | tf_op jit(solution)/shard_map/ppermute | solution.py:188
  15.9 0.2 collective-permute-start.3
  16.2 1.6 %collective-permute-start.11 = (f32[2,128,128]{2,1,0:T(8,128)S(1)}, f32[2,128,128]{2,1,0:T(8,128)S(1)}, u32[]{:S(2)}, u32[]{:S(2)}) collective-permute-start(f32[2,128,128]{2,1,0:T(8,128)S(1)} %add_select_fusion.1), channel_id=1, source_target_pairs={{0,4},{1,9},{2,6},{3,11},{4,0},{5,13},{6,2},{7,15},{8,12},{9,1},{1... | collective-permute-start | bytes 393224 | tf_op jit(solution)/shard_map/ppermute | solution.py:188
  17.8 1.4 %collective-permute-start.4 = (f32[2,128,128]{2,1,0:T(8,128)S(1)}, f32[2,128,128]{2,1,0:T(8,128)S(1)}, u32[]{:S(2)}, u32[]{:S(2)}) collective-permute-start(f32[2,128,128]{2,1,0:T(8,128)S(1)} %add_select_fusion.5), channel_id=1, source_target_pairs={{0,4},{1,17},{2,6},{3,19},{4,0},{5,21},{6,2},{7,23},{8,12},{9,25},... | collective-permute-start | bytes 393224 | tf_op jit(solution)/shard_map/ppermute | solution.py:188
  19.1 2.1 %collective-permute-done.11 = f32[2,128,128]{2,1,0:T(8,128)S(1)} collective-permute-done((f32[2,128,128]{2,1,0:T(8,128)S(1)}, f32[2,128,128]{2,1,0:T(8,128)S(1)}, u32[]{:S(2)}, u32[]{:S(2)}) %collective-permute-start.11) | collective-permute-done | bytes 131104 | tf_op jit(solution)/shard_map/ppermute | solution.py:188
  21.3 1.6 %collective-permute-start.12 = (f32[2,128,128]{2,1,0:T(8,128)S(1)}, f32[2,128,128]{2,1,0:T(8,128)S(1)}, u32[]{:S(2)}, u32[]{:S(2)}) collective-permute-start(f32[2,128,128]{2,1,0:T(8,128)S(1)} %add_select_fusion), channel_id=1, source_target_pairs={{0,2},{1,17},{2,0},{3,19},{4,6},{5,21},{6,4},{7,23},{8,10},{9,25},... | collective-permute-start | bytes 393224 | tf_op jit(solution)/shard_map/ppermute | solution.py:188
  22.9 1.4 %collective-permute-start.5 = (f32[2,128,128]{2,1,0:T(8,128)S(1)}, f32[2,128,128]{2,1,0:T(8,128)S(1)}, u32[]{:S(2)}, u32[]{:S(2)}) collective-permute-start(f32[2,128,128]{2,1,0:T(8,128)S(1)} %add_select_fusion.4.late_ref), channel_id=1, source_target_pairs={{0,2},{1,9},{2,0},{3,11},{4,6},{5,13},{6,4},{7,15},{8,10},{9,1},{1... | collective-permute-start | bytes 393224 | tf_op jit(solution)/shard_map/ppermute | solution.py:188
  24.3 1.4 %intra.1 = (bf16[128,1024]{1,0:T(8,128)(2,1)S(1)}, f32[128,1024]{1,0:T(8,128)S(1)}, f32[1,1024]{1,0:T(1,128)S(1)}) custom-call(bf16[128,1024]{1,0:T(8,128)(2,1)S(1)} %copy-done, bf16[128,1024]{1,0:T(8,128)(2,1)S(1)} %get-tuple-element.14.k_ref, bf16[128,1024]{1,0:T(8,128)(2,1)S(1)} %get-tuple-element.15.v_ref, f32[1,1024]{1,0:T(1,128)S(1)} %bitcast.2, ...), custom_call_target="tpu_custom_call" | custom-call | flops 67108864 | bytes 1572864 | tf_op jit(solution)/shard_map/intra/pallas_call | solution.py:212
  25.6 0.7 %collective-permute-done.12 = f32[2,128,128]{2,1,0:T(8,128)S(1)} collective-permute-done((f32[2,128,128]{2,1,0:T(8,128)S(1)}, f32[2,128,128]{2,1,0:T(8,128)S(1)}, u32[]{:S(2)}, u32[]{:S(2)}) %collective-permute-start.12) | collective-permute-done | bytes 131104 | tf_op jit(solution)/shard_map/ppermute | solution.py:188
  26.3 0.9 %collective-permute-start.13 = (f32[2,128,128]{2,1,0:T(8,128)S(1)}, f32[2,128,128]{2,1,0:T(8,128)S(1)}, u32[]{:S(2)}, u32[]{:S(2)}) collective-permute-start(f32[2,128,128]{2,1,0:T(8,128)S(1)} %get-tuple-element.26), channel_id=1, source_target_pairs={{0,1},{1,0},{2,3},{3,2},{4,5},{5,4},{6,7},{7,6},{8,9},{9,8},{10,11... | collective-permute-start | bytes 393224 | tf_op jit(solution)/shard_map/ppermute | solution.py:166
  27.2 0.7 %collective-permute-done.5 = f32[2,128,128]{2,1,0:T(8,128)S(1)} collective-permute-done((f32[2,128,128]{2,1,0:T(8,128)S(1)}, f32[2,128,128]{2,1,0:T(8,128)S(1)}, u32[]{:S(2)}, u32[]{:S(2)}) %collective-permute-start.5) | collective-permute-done | bytes 131104 | tf_op jit(solution)/shard_map/ppermute | solution.py:188
  27.9 0.5 %collective-permute-start.6 = (f32[2,128,128]{2,1,0:T(8,128)S(1)}, f32[2,128,128]{2,1,0:T(8,128)S(1)}, u32[]{:S(2)}, u32[]{:S(2)}) collective-permute-start(f32[2,128,128]{2,1,0:T(8,128)S(1)} %get-tuple-element.24), channel_id=1, source_target_pairs={{0,1},{1,0},{2,3},{3,2},{4,5},{5,4},{6,7},{7,6},{8,9},{9,8},{10,11... | collective-permute-start | bytes 393224 | tf_op jit(solution)/shard_map/ppermute | solution.py:166
  28.5 1.0 %attend.2.refs_1_ = bf16[128,1024]{1,0:T(8,128)(2,1)} custom-call(s32[1]{0:T(128)} %bitcast.core_ref, bf16[128,1024]{1,0:T(8,128)(2,1)S(1)} %get-tuple-element.18.fq_ref, f32[128,1024]{1,0:T(8,128)S(1)} %get-tuple-element.19.intra_ref, f32[1,1024]{1,0:T(1,128)S(1)} %get-tuple-element.20.gain_ref, f32[2,128,128]{2,1,0:T(8,128)S(1)} %get-tuple-element.25.refs_0_, ...), custom_call_target="tpu_custom_call" | custom-call | flops 25165824 | bytes 393216 | tf_op jit(solution)/shard_map/attend/pallas_call | solution.py:232
  29.6 0.9 %attend.3 = bf16[128,1024]{1,0:T(8,128)(2,1)} custom-call(s32[1]{0:T(128)} %bitcast.core_ref, bf16[128,1024]{1,0:T(8,128)(2,1)S(1)} %get-tuple-element.18.fq_ref, f32[128,1024]{1,0:T(8,128)S(1)} %get-tuple-element.19.intra_ref, f32[1,1024]{1,0:T(1,128)S(1)} %get-tuple-element.20.gain_ref, ...), custom_call_target="tpu_custom_call", output_to_operand_aliasing={{}: (5, {})} | custom-call | flops 8388608 | bytes 131072 | tf_op jit(solution)/shard_map/attend/pallas_call | solution.py:232
  (29 shorter events, 0.7 us)
Async XLA Ops:
  1.3 1.5 %collective-permute-start.7 = (f32[2,128,128]{2,1,0:T(8,128)S(1)}, f32[2,128,128]{2,1,0:T(8,128)S(1)}, u32[]{:S(2)}, u32[]{:S(2)}) collective-permute-start(f32[2,128,128]{2,1,0:T(8,128)S(1)} %get-tuple-element.22), channel_id=1, source_target_pairs={{0,1},{1,0},{2,3},{3,2},{4,5},{5,4},{6,7},{7,6},{8,9},{9,8},{10,11... | collective-permute-start | bytes 393224 | tf_op jit(solution)/shard_map/ppermute | solution.py:166
  1.8 4.0 %collective-permute-start = (f32[2,128,128]{2,1,0:T(8,128)S(1)}, f32[2,128,128]{2,1,0:T(8,128)S(1)}, u32[]{:S(2)}, u32[]{:S(2)}) collective-permute-start(f32[2,128,128]{2,1,0:T(8,128)S(1)} %get-tuple-element.17), channel_id=1, source_target_pairs={{0,1},{1,0},{2,3},{3,2},{4,5},{5,4},{6,7},{7,6},{8,9},{9,8},{10,11... | collective-permute-start | bytes 393224 | tf_op jit(solution)/shard_map/ppermute | solution.py:166
  2.8 5.9 %collective-permute-start.8 = (f32[2,128,128]{2,1,0:T(8,128)S(1)}, f32[2,128,128]{2,1,0:T(8,128)S(1)}, u32[]{:S(2)}, u32[]{:S(2)}) collective-permute-start(f32[2,128,128]{2,1,0:T(8,128)S(1)} %add.159), channel_id=1, source_target_pairs={{0,2},{1,9},{2,0},{3,11},{4,6},{5,13},{6,4},{7,15},{8,10},{9,1},{1... | collective-permute-start | bytes 393224 | tf_op jit(solution)/shard_map/ppermute | solution.py:188
  5.8 5.0 %collective-permute-start.1 = (f32[2,128,128]{2,1,0:T(8,128)S(1)}, f32[2,128,128]{2,1,0:T(8,128)S(1)}, u32[]{:S(2)}, u32[]{:S(2)}) collective-permute-start(f32[2,128,128]{2,1,0:T(8,128)S(1)} %get-tuple-element.29), channel_id=1, source_target_pairs={{0,2},{1,17},{2,0},{3,19},{4,6},{5,21},{6,4},{7,23},{8,10},{9,25},... | collective-permute-start | bytes 393224 | tf_op jit(solution)/shard_map/ppermute | solution.py:188
  8.7 5.0 %collective-permute-start.9 = (f32[2,128,128]{2,1,0:T(8,128)S(1)}, f32[2,128,128]{2,1,0:T(8,128)S(1)}, u32[]{:S(2)}, u32[]{:S(2)}) collective-permute-start(f32[2,128,128]{2,1,0:T(8,128)S(1)} %add.160), channel_id=1, source_target_pairs={{0,4},{1,17},{2,6},{3,19},{4,0},{5,21},{6,2},{7,23},{8,12},{9,25},... | collective-permute-start | bytes 393224 | tf_op jit(solution)/shard_map/ppermute | solution.py:188
  10.8 5.0 %collective-permute-start.2 = (f32[2,128,128]{2,1,0:T(8,128)S(1)}, f32[2,128,128]{2,1,0:T(8,128)S(1)}, u32[]{:S(2)}, u32[]{:S(2)}) collective-permute-start(f32[2,128,128]{2,1,0:T(8,128)S(1)} %get-tuple-element.27), channel_id=1, source_target_pairs={{0,4},{1,9},{2,6},{3,11},{4,0},{5,13},{6,2},{7,15},{8,12},{9,1},{1... | collective-permute-start | bytes 393224 | tf_op jit(solution)/shard_map/ppermute | solution.py:188
  13.8 2.3 %collective-permute-start.10 = (f32[4,128,128]{2,1,0:T(8,128)S(1)}, f32[4,128,128]{2,1,0:T(8,128)S(1)}, u32[]{:S(2)}, u32[]{:S(2)}) collective-permute-start(f32[4,128,128]{2,1,0:T(8,128)S(1)} %pad_maximum_fusion.1), channel_id=1, source_target_pairs={{0,1},{1,0},{2,3},{3,2},{4,5},{5,4},{6,7},{7,6},{8,9},{9,8},{10,11... | collective-permute-start | bytes 786440 | tf_op jit(solution)/shard_map/ppermute | solution.py:166
  15.9 1.8 %collective-permute-start.3 = (f32[4,128,128]{2,1,0:T(8,128)S(1)}, f32[4,128,128]{2,1,0:T(8,128)S(1)}, u32[]{:S(2)}, u32[]{:S(2)}) collective-permute-start(f32[4,128,128]{2,1,0:T(8,128)S(1)} %pad_maximum_fusion), channel_id=1, source_target_pairs={{0,1},{1,0},{2,3},{3,2},{4,5},{5,4},{6,7},{7,6},{8,9},{9,8},{10,11... | collective-permute-start | bytes 786440 | tf_op jit(solution)/shard_map/ppermute | solution.py:166
  16.2 5.0 %collective-permute-start.11 = (f32[2,128,128]{2,1,0:T(8,128)S(1)}, f32[2,128,128]{2,1,0:T(8,128)S(1)}, u32[]{:S(2)}, u32[]{:S(2)}) collective-permute-start(f32[2,128,128]{2,1,0:T(8,128)S(1)} %add_select_fusion.1), channel_id=1, source_target_pairs={{0,4},{1,9},{2,6},{3,11},{4,0},{5,13},{6,2},{7,15},{8,12},{9,1},{1... | collective-permute-start | bytes 393224 | tf_op jit(solution)/shard_map/ppermute | solution.py:188
  17.8 5.0 %collective-permute-start.4 = (f32[2,128,128]{2,1,0:T(8,128)S(1)}, f32[2,128,128]{2,1,0:T(8,128)S(1)}, u32[]{:S(2)}, u32[]{:S(2)}) collective-permute-start(f32[2,128,128]{2,1,0:T(8,128)S(1)} %add_select_fusion.5), channel_id=1, source_target_pairs={{0,4},{1,17},{2,6},{3,19},{4,0},{5,21},{6,2},{7,23},{8,12},{9,25},... | collective-permute-start | bytes 393224 | tf_op jit(solution)/shard_map/ppermute | solution.py:188
  21.2 3.0 %copy-start = (bf16[128,1024]{1,0:T(8,128)(2,1)S(1)}, bf16[128,1024]{1,0:T(8,128)(2,1)}, u32[]{:S(2)}) copy-start(bf16[128,1024]{1,0:T(8,128)(2,1)} %q_ref.1) | copy-start | bytes 786436
  21.3 5.0 %collective-permute-start.12 = (f32[2,128,128]{2,1,0:T(8,128)S(1)}, f32[2,128,128]{2,1,0:T(8,128)S(1)}, u32[]{:S(2)}, u32[]{:S(2)}) collective-permute-start(f32[2,128,128]{2,1,0:T(8,128)S(1)} %add_select_fusion), channel_id=1, source_target_pairs={{0,2},{1,17},{2,0},{3,19},{4,6},{5,21},{6,4},{7,23},{8,10},{9,25},... | collective-permute-start | bytes 393224 | tf_op jit(solution)/shard_map/ppermute | solution.py:188
  22.8 1.4 %copy-start.1 = (f32[1024]{0:T(1024)S(1)}, f32[1024]{0:T(1024)}, u32[]{:S(2)}) copy-start(f32[1024]{0:T(1024)} %param.7) | copy-start | bytes 12292
  22.9 5.0 %collective-permute-start.5 = (f32[2,128,128]{2,1,0:T(8,128)S(1)}, f32[2,128,128]{2,1,0:T(8,128)S(1)}, u32[]{:S(2)}, u32[]{:S(2)}) collective-permute-start(f32[2,128,128]{2,1,0:T(8,128)S(1)} %add_select_fusion.4.late_ref), channel_id=1, source_target_pairs={{0,2},{1,9},{2,0},{3,11},{4,6},{5,13},{6,4},{7,15},{8,10},{9,1},{1... | collective-permute-start | bytes 393224 | tf_op jit(solution)/shard_map/ppermute | solution.py:188
  26.3 2.1 %collective-permute-start.13 = (f32[2,128,128]{2,1,0:T(8,128)S(1)}, f32[2,128,128]{2,1,0:T(8,128)S(1)}, u32[]{:S(2)}, u32[]{:S(2)}) collective-permute-start(f32[2,128,128]{2,1,0:T(8,128)S(1)} %get-tuple-element.26), channel_id=1, source_target_pairs={{0,1},{1,0},{2,3},{3,2},{4,5},{5,4},{6,7},{7,6},{8,9},{9,8},{10,11... | collective-permute-start | bytes 393224 | tf_op jit(solution)/shard_map/ppermute | solution.py:166
  27.9 1.6 %collective-permute-start.6 = (f32[2,128,128]{2,1,0:T(8,128)S(1)}, f32[2,128,128]{2,1,0:T(8,128)S(1)}, u32[]{:S(2)}, u32[]{:S(2)}) collective-permute-start(f32[2,128,128]{2,1,0:T(8,128)S(1)} %get-tuple-element.24), channel_id=1, source_target_pairs={{0,1},{1,0},{2,3},{3,2},{4,5},{5,4},{6,7},{7,6},{8,9},{9,8},{10,11... | collective-permute-start | bytes 393224 | tf_op jit(solution)/shard_map/ppermute | solution.py:166

commit v8 on v7

--- a/solution.py
+++ b/solution.py
@@ -69,24 +69,37 @@
         intra_ref[:, cols] = jnp.dot(weights, v_ref[:, cols], preferred_element_type=jnp.float32)
 
 
-def attend_kernel(jobs, core_ref, fq_ref, intra_ref, gain_ref, *refs):
-    carried, (out_hbm, buf_ref, sems) = refs[: len(jobs)], refs[-3:]
-    core = core_ref[0]
-    copies = []
+def attend_heads(jobs, core, fq_ref, intra_ref, gain_ref, carried, buf_ref):
     for slot, (half, c) in enumerate(jobs):
-        first = (core * HALF + half * HALF + c * PER) % HEADS
         for i in range(PER):
-            cols = head_cols(first + i)
+            cols = head_cols((core * HALF + half * HALF + c * PER + i) % HEADS)
             state = carried[slot][i].astype(jnp.bfloat16)
             total = intra_ref[:, cols] + jnp.dot(fq_ref[:, cols], state, preferred_element_type=jnp.float32)
             meansq = jnp.mean(total * total, axis=-1, keepdims=True)
             normed = total * lax.rsqrt(meansq + 1e-06) * gain_ref[:, cols]
             buf_ref[slot, :, i * HEAD_DIM : (i + 1) * HEAD_DIM] = normed.astype(jnp.bfloat16)
-        width = PER * HEAD_DIM
+
+
+def early_kernel(jobs, core_ref, fq_ref, intra_ref, gain_ref, *refs):
+    attend_heads(jobs, core_ref[0], fq_ref, intra_ref, gain_ref, refs[:-1], refs[-1])
+
+
+def last_kernel(jobs, early, core_ref, fq_ref, intra_ref, gain_ref, *refs):
+    carried, (early_ref, out_hbm, buf_ref, sems) = refs[: len(jobs)], refs[len(jobs) :]
+    core = core_ref[0]
+    width = PER * HEAD_DIM
+
+    def copy_out(job, source, sem):
+        half, c = job
+        first = (core * HALF + half * HALF + c * PER) % HEADS
         place = pl.ds(pl.multiple_of(first * HEAD_DIM, width), width)
-        copy = pltpu.make_async_copy(buf_ref.at[slot], out_hbm.at[:, place], sems.at[slot])
+        copy = pltpu.make_async_copy(source, out_hbm.at[:, place], sems.at[sem])
         copy.start()
-        copies.append(copy)
+        return copy
+
+    copies = [copy_out(job, early_ref.at[slot], slot) for slot, job in enumerate(early)]
+    attend_heads(jobs, core, fq_ref, intra_ref, gain_ref, carried, buf_ref)
+    copies += [copy_out(job, buf_ref.at[slot], len(early) + slot) for slot, job in enumerate(jobs)]
     for copy in copies:
         copy.wait()
 
@@ -225,30 +238,37 @@
         name="intra",
     )(queries, near_keys, near_values, head_gain.reshape(1, -1), late)
 
-    def attend(jobs, parts, so_far=None):
-        whole = jax.ShapeDtypeStruct(queries.shape, jnp.bfloat16)
-        extra = [] if so_far is None else [so_far]
-        given = [core_arr, fq, intra, gain, *parts, *extra]
-        return pl.pallas_call(
-            functools.partial(attend_kernel, jobs),
-            out_shape=whole,
-            in_specs=[SMEM] + [VMEM] * (3 + len(jobs)) + [HBM] * len(extra),
-            out_specs=HBM,
-            scratch_shapes=[
-                pltpu.VMEM((len(jobs), rows, PER * HEAD_DIM), jnp.bfloat16),
-                pltpu.SemaphoreType.DMA((len(jobs),)),
-            ],
-            input_output_aliases={len(given) - 1: 0} if extra else {},
-            compiler_params=PARAMS,
-            cost_estimate=pl.CostEstimate(
-                flops=2 * len(jobs) * PER * rows * HEAD_DIM * HEAD_DIM, bytes_accessed=len(jobs) * queries.size, transcendentals=0
-            ),
-            name="attend",
-        )(*given)
-
     early = [(1, c) for c in range(CHUNKS)] + [(0, c) for c in range(CHUNKS) if c != LAST_CHUNK]
-    most = attend(early, their_parts + [x for c, x in enumerate(mine_parts) if c != LAST_CHUNK])
-    return attend([(0, LAST_CHUNK)], [mine_parts[LAST_CHUNK]], most)
+    jobs = [(0, LAST_CHUNK)]
+    early_parts = their_parts + [x for c, x in enumerate(mine_parts) if c != LAST_CHUNK]
+
+    def cost(n_jobs):
+        return pl.CostEstimate(
+            flops=2 * n_jobs * PER * rows * HEAD_DIM * HEAD_DIM, bytes_accessed=n_jobs * queries.size, transcendentals=0
+        )
+
+    done = pl.pallas_call(
+        functools.partial(early_kernel, early),
+        out_shape=jax.ShapeDtypeStruct((len(early), rows, PER * HEAD_DIM), jnp.bfloat16),
+        in_specs=[SMEM] + [VMEM] * (3 + len(early)),
+        out_specs=VMEM,
+        compiler_params=PARAMS,
+        cost_estimate=cost(len(early)),
+        name="attend_early",
+    )(core_arr, fq, intra, gain, *early_parts)
+    return pl.pallas_call(
+        functools.partial(last_kernel, jobs, early),
+        out_shape=jax.ShapeDtypeStruct(queries.shape, jnp.bfloat16),
+        in_specs=[SMEM] + [VMEM] * (3 + len(jobs) + 1),
+        out_specs=HBM,
+        scratch_shapes=[
+            pltpu.VMEM((len(jobs), rows, PER * HEAD_DIM), jnp.bfloat16),
+            pltpu.SemaphoreType.DMA((len(early) + len(jobs),)),
+        ],
+        compiler_params=PARAMS,
+        cost_estimate=cost(len(jobs)),
+        name="attend_last",
+    )(core_arr, fq, intra, gain, mine_parts[LAST_CHUNK], done)
 
 
 def solution(mesh):

time: 30.6 us -> 30.6 us (level)
  Pallas kernels: 4.79 us -> 4.15 us
  waiting for transfers between devices: 10.2 us -> 10.8 us
    pallas_call x2, Pallas kernels: 1.91 us -> 1.28 us  [the longest x1 0.93 us: per_device(): pl.pallas_call(functools.partial(last_kernel, jobs, early), out_shape=jax...]
    ppermute x6, waiting for transfers between devices: 0.68 us -> 1.27 us  [to_swap(): return lax.ppermute(x, AXES, swap)]
  transfers between devices with their start and end apart: 14 -> 14, of which waited for: 7 -> 8; matrix products, arithmetic and copies ran while one was open for 1% -> 1% of each run, Pallas kernels for 9% -> 6%
where the time goes in v8:
time: 30.6 us; the launch traced here: 30.4 us
  starting transfers between devices  14.9 us (49%)
  waiting for transfers between devices  10.8 us (35%)
  Pallas kernels  4.15 us (14%)
  other arithmetic  0.48 us (2%)
    ppermute x8, starting transfers between devices, scan(): got = lax.ppermute(sent[-1], AXES, perm)  12.6 us
    ppermute x8, waiting for transfers between devices, scan(): got = lax.ppermute(sent[-1], AXES, perm)  9.54 us
    ppermute x6, starting transfers between devices, to_swap(): return lax.ppermute(x, AXES, swap)  2.26 us
    pallas_call x1, Pallas kernels, per_device(): pl.pallas_call(intra_kernel, out_shape=[jax.ShapeDtypeStruct(queries.shap...  1.36 us
    pallas_call x1, Pallas kernels, per_device(): pl.pallas_call(theirs_kernel, out_shape=[part] * CHUNKS + [jax.ShapeDtype...  1.28 us
    ppermute x6, waiting for transfers between devices, to_swap(): return lax.ppermute(x, AXES, swap)  1.27 us
    pallas_call x1, Pallas kernels, per_device(): pl.pallas_call(functools.partial(last_kernel, jobs, early), out_shape=jax...  0.93 us
  transfers between devices with their start and end apart: 14, of which 8 were waited for; matrix products, arithmetic and copies ran while one was open for 1% of the time, Pallas kernels for 6%

profile of v8, /device:TPU:0, one launch (start us, length us, event | category | flops | bytes accessed | tf_op | source)
XLA Modules:
  0.0 30.4 jit_solution(5476519066860387963)
XLA Ops:
  0.0 1.3 %theirs.1 = (f32[2,128,128]{2,1,0:T(8,128)S(1)}, f32[2,128,128]{2,1,0:T(8,128)S(1)}, bf16[128,1024]{1,0:T(8,128)(2,1)S(1)}, bf16[128,1024]{1,0:T(8,128)(2,1)S(1)}) custom-call(s32[1]{0:T(128)} %bitcast.core_ref, bf16[128,1024]{1,0:T(8,128)(2,1)} %k_hbm.1, bf16[128,1024]{1,0:T(8,128)(2,1)} %v_hbm.1), custom_call_target="tpu_custom_call" | custom-call | tf_op jit(solution)/shard_map/theirs/pallas_call | solution.py:142
  1.3 0.5 %collective-permute-start.7 = (f32[2,128,128]{2,1,0:T(8,128)S(1)}, f32[2,128,128]{2,1,0:T(8,128)S(1)}, u32[]{:S(2)}, u32[]{:S(2)}) collective-permute-start(f32[2,128,128]{2,1,0:T(8,128)S(1)} %get-tuple-element.22), channel_id=1, source_target_pairs={{0,1},{1,0},{2,3},{3,2},{4,5},{5,4},{6,7},{7,6},{8,9},{9,8},{10,11... | collective-permute-start | bytes 393224 | tf_op jit(solution)/shard_map/ppermute | solution.py:179
  1.9 0.2 mine.1
  2.1 0.7 %collective-permute-done.7 = f32[2,128,128]{2,1,0:T(8,128)S(1)} collective-permute-done((f32[2,128,128]{2,1,0:T(8,128)S(1)}, f32[2,128,128]{2,1,0:T(8,128)S(1)}, u32[]{:S(2)}, u32[]{:S(2)}) %collective-permute-start.7) | collective-permute-done | bytes 131104 | tf_op jit(solution)/shard_map/ppermute | solution.py:179
  2.8 2.9 %collective-permute-start.8 = (f32[2,128,128]{2,1,0:T(8,128)S(1)}, f32[2,128,128]{2,1,0:T(8,128)S(1)}, u32[]{:S(2)}, u32[]{:S(2)}) collective-permute-start(f32[2,128,128]{2,1,0:T(8,128)S(1)} %add.159), channel_id=1, source_target_pairs={{0,2},{1,9},{2,0},{3,11},{4,6},{5,13},{6,4},{7,15},{8,10},{9,1},{1... | collective-permute-start | bytes 393224 | tf_op jit(solution)/shard_map/ppermute | solution.py:201
  6.0 2.7 %collective-permute-done.8 = f32[2,128,128]{2,1,0:T(8,128)S(1)} collective-permute-done((f32[2,128,128]{2,1,0:T(8,128)S(1)}, f32[2,128,128]{2,1,0:T(8,128)S(1)}, u32[]{:S(2)}, u32[]{:S(2)}) %collective-permute-start.8) | collective-permute-done | bytes 131104 | tf_op jit(solution)/shard_map/ppermute | solution.py:201
  8.7 2.1 %collective-permute-start.9 = (f32[2,128,128]{2,1,0:T(8,128)S(1)}, f32[2,128,128]{2,1,0:T(8,128)S(1)}, u32[]{:S(2)}, u32[]{:S(2)}) collective-permute-start(f32[2,128,128]{2,1,0:T(8,128)S(1)} %add.160), channel_id=1, source_target_pairs={{0,4},{1,17},{2,6},{3,19},{4,0},{5,21},{6,2},{7,23},{8,12},{9,25},... | collective-permute-start | bytes 393224 | tf_op jit(solution)/shard_map/ppermute | solution.py:201
  10.8 1.6 %collective-permute-start.2 = (f32[2,128,128]{2,1,0:T(8,128)S(1)}, f32[2,128,128]{2,1,0:T(8,128)S(1)}, u32[]{:S(2)}, u32[]{:S(2)}) collective-permute-start(f32[2,128,128]{2,1,0:T(8,128)S(1)} %get-tuple-element.27), channel_id=1, source_target_pairs={{0,4},{1,9},{2,6},{3,11},{4,0},{5,13},{6,2},{7,15},{8,12},{9,1},{1... | collective-permute-start | bytes 393224 | tf_op jit(solution)/shard_map/ppermute | solution.py:201
  12.4 1.4 %collective-permute-done.9 = f32[2,128,128]{2,1,0:T(8,128)S(1)} collective-permute-done((f32[2,128,128]{2,1,0:T(8,128)S(1)}, f32[2,128,128]{2,1,0:T(8,128)S(1)}, u32[]{:S(2)}, u32[]{:S(2)}) %collective-permute-start.9) | collective-permute-done | bytes 131104 | tf_op jit(solution)/shard_map/ppermute | solution.py:201
  13.9 2.0 %collective-permute-done.2 = f32[2,128,128]{2,1,0:T(8,128)S(1)} collective-permute-done((f32[2,128,128]{2,1,0:T(8,128)S(1)}, f32[2,128,128]{2,1,0:T(8,128)S(1)}, u32[]{:S(2)}, u32[]{:S(2)}) %collective-permute-start.2) | collective-permute-done | bytes 131104 | tf_op jit(solution)/shard_map/ppermute | solution.py:201
  15.9 0.2 collective-permute-start.3
  16.2 1.6 %collective-permute-start.11 = (f32[2,128,128]{2,1,0:T(8,128)S(1)}, f32[2,128,128]{2,1,0:T(8,128)S(1)}, u32[]{:S(2)}, u32[]{:S(2)}) collective-permute-start(f32[2,128,128]{2,1,0:T(8,128)S(1)} %add_select_fusion.1), channel_id=1, source_target_pairs={{0,4},{1,9},{2,6},{3,11},{4,0},{5,13},{6,2},{7,15},{8,12},{9,1},{1... | collective-permute-start | bytes 393224 | tf_op jit(solution)/shard_map/ppermute | solution.py:201
  17.8 1.4 %collective-permute-start.4 = (f32[2,128,128]{2,1,0:T(8,128)S(1)}, f32[2,128,128]{2,1,0:T(8,128)S(1)}, u32[]{:S(2)}, u32[]{:S(2)}) collective-permute-start(f32[2,128,128]{2,1,0:T(8,128)S(1)} %add_select_fusion.5), channel_id=1, source_target_pairs={{0,4},{1,17},{2,6},{3,19},{4,0},{5,21},{6,2},{7,23},{8,12},{9,25},... | collective-permute-start | bytes 393224 | tf_op jit(solution)/shard_map/ppermute | solution.py:201
  19.1 2.1 %collective-permute-done.11 = f32[2,128,128]{2,1,0:T(8,128)S(1)} collective-permute-done((f32[2,128,128]{2,1,0:T(8,128)S(1)}, f32[2,128,128]{2,1,0:T(8,128)S(1)}, u32[]{:S(2)}, u32[]{:S(2)}) %collective-permute-start.11) | collective-permute-done | bytes 131104 | tf_op jit(solution)/shard_map/ppermute | solution.py:201
  21.3 1.6 %collective-permute-start.12 = (f32[2,128,128]{2,1,0:T(8,128)S(1)}, f32[2,128,128]{2,1,0:T(8,128)S(1)}, u32[]{:S(2)}, u32[]{:S(2)}) collective-permute-start(f32[2,128,128]{2,1,0:T(8,128)S(1)} %add_select_fusion), channel_id=1, source_target_pairs={{0,2},{1,17},{2,0},{3,19},{4,6},{5,21},{6,4},{7,23},{8,10},{9,25},... | collective-permute-start | bytes 393224 | tf_op jit(solution)/shard_map/ppermute | solution.py:201
  22.9 1.4 %collective-permute-start.5 = (f32[2,128,128]{2,1,0:T(8,128)S(1)}, f32[2,128,128]{2,1,0:T(8,128)S(1)}, u32[]{:S(2)}, u32[]{:S(2)}) collective-permute-start(f32[2,128,128]{2,1,0:T(8,128)S(1)} %add_select_fusion.4.late_ref), channel_id=1, source_target_pairs={{0,2},{1,9},{2,0},{3,11},{4,6},{5,13},{6,4},{7,15},{8,10},{9,1},{1... | collective-permute-start | bytes 393224 | tf_op jit(solution)/shard_map/ppermute | solution.py:201
  24.3 1.4 %intra.1 = (bf16[128,1024]{1,0:T(8,128)(2,1)S(1)}, f32[128,1024]{1,0:T(8,128)S(1)}, f32[1,1024]{1,0:T(1,128)S(1)}) custom-call(bf16[128,1024]{1,0:T(8,128)(2,1)S(1)} %copy-done, bf16[128,1024]{1,0:T(8,128)(2,1)S(1)} %get-tuple-element.14.k_ref, bf16[128,1024]{1,0:T(8,128)(2,1)S(1)} %get-tuple-element.15.v_ref, f32[1,1024]{1,0:T(1,128)S(1)} %bitcast.2, ...), custom_call_target="tpu_custom_call" | custom-call | flops 67108864 | bytes 1572864 | tf_op jit(solution)/shard_map/intra/pallas_call | solution.py:225
  25.6 0.7 %collective-permute-done.12 = f32[2,128,128]{2,1,0:T(8,128)S(1)} collective-permute-done((f32[2,128,128]{2,1,0:T(8,128)S(1)}, f32[2,128,128]{2,1,0:T(8,128)S(1)}, u32[]{:S(2)}, u32[]{:S(2)}) %collective-permute-start.12) | collective-permute-done | bytes 131104 | tf_op jit(solution)/shard_map/ppermute | solution.py:201
  26.3 0.9 %collective-permute-start.13 = (f32[2,128,128]{2,1,0:T(8,128)S(1)}, f32[2,128,128]{2,1,0:T(8,128)S(1)}, u32[]{:S(2)}, u32[]{:S(2)}) collective-permute-start(f32[2,128,128]{2,1,0:T(8,128)S(1)} %get-tuple-element.26), channel_id=1, source_target_pairs={{0,1},{1,0},{2,3},{3,2},{4,5},{5,4},{6,7},{7,6},{8,9},{9,8},{10,11... | collective-permute-start | bytes 393224 | tf_op jit(solution)/shard_map/ppermute | solution.py:179
  27.2 0.7 %collective-permute-done.5 = f32[2,128,128]{2,1,0:T(8,128)S(1)} collective-permute-done((f32[2,128,128]{2,1,0:T(8,128)S(1)}, f32[2,128,128]{2,1,0:T(8,128)S(1)}, u32[]{:S(2)}, u32[]{:S(2)}) %collective-permute-start.5) | collective-permute-done | bytes 131104 | tf_op jit(solution)/shard_map/ppermute | solution.py:201
  27.9 0.5 %collective-permute-start.6 = (f32[2,128,128]{2,1,0:T(8,128)S(1)}, f32[2,128,128]{2,1,0:T(8,128)S(1)}, u32[]{:S(2)}, u32[]{:S(2)}) collective-permute-start(f32[2,128,128]{2,1,0:T(8,128)S(1)} %get-tuple-element.24), channel_id=1, source_target_pairs={{0,1},{1,0},{2,3},{3,2},{4,5},{5,4},{6,7},{7,6},{8,9},{9,8},{10,11... | collective-permute-start | bytes 393224 | tf_op jit(solution)/shard_map/ppermute | solution.py:179
  28.5 0.3 %attend_early.1.refs_1_ = bf16[3,128,256]{2,1,0:T(8,128)(2,1)S(1)} custom-call(s32[1]{0:T(128)} %bitcast.core_ref, bf16[128,1024]{1,0:T(8,128)(2,1)S(1)} %get-tuple-element.18.fq_ref, f32[128,1024]{1,0:T(8,128)S(1)} %get-tuple-element.19.intra_ref, f32[1,1024]{1,0:T(1,128)S(1)} %get-tuple-element.20.gain_ref, f32[2,128,128]{2,1,0:T(8,128)S(1)} %get-tuple-element.25.refs_0_, ...), custom_call_target="tpu_custom_call" | custom-call | flops 25165824 | bytes 393216 | tf_op jit(solution)/shard_map/attend_early/pallas_call | solution.py:250
  28.9 0.6 %collective-permute-done.6 = f32[2,128,128]{2,1,0:T(8,128)S(1)} collective-permute-done((f32[2,128,128]{2,1,0:T(8,128)S(1)}, f32[2,128,128]{2,1,0:T(8,128)S(1)}, u32[]{:S(2)}, u32[]{:S(2)}) %collective-permute-start.6) | collective-permute-done | bytes 131104 | tf_op jit(solution)/shard_map/ppermute | solution.py:179
  29.5 0.9 %attend_last.1 = bf16[128,1024]{1,0:T(8,128)(2,1)} custom-call(s32[1]{0:T(128)} %bitcast.core_ref, bf16[128,1024]{1,0:T(8,128)(2,1)S(1)} %get-tuple-element.18.fq_ref, f32[128,1024]{1,0:T(8,128)S(1)} %get-tuple-element.19.intra_ref, f32[1,1024]{1,0:T(1,128)S(1)} %get-tuple-element.20.gain_ref, f32[2,128,128]{2,1,0:T(8,128)S(1)} %select_add_fusion.7.refs_0_, ...), custom_call_target="tpu_custom_call" | custom-call | flops 8388608 | bytes 131072 | tf_op jit(solution)/shard_map/attend_last/pallas_call | solution.py:259
  (29 shorter events, 0.9 us)
Async XLA Ops:
  1.3 1.5 %collective-permute-start.7 = (f32[2,128,128]{2,1,0:T(8,128)S(1)}, f32[2,128,128]{2,1,0:T(8,128)S(1)}, u32[]{:S(2)}, u32[]{:S(2)}) collective-permute-start(f32[2,128,128]{2,1,0:T(8,128)S(1)} %get-tuple-element.22), channel_id=1, source_target_pairs={{0,1},{1,0},{2,3},{3,2},{4,5},{5,4},{6,7},{7,6},{8,9},{9,8},{10,11... | collective-permute-start | bytes 393224 | tf_op jit(solution)/shard_map/ppermute | solution.py:179
  1.8 4.0 %collective-permute-start = (f32[2,128,128]{2,1,0:T(8,128)S(1)}, f32[2,128,128]{2,1,0:T(8,128)S(1)}, u32[]{:S(2)}, u32[]{:S(2)}) collective-permute-start(f32[2,128,128]{2,1,0:T(8,128)S(1)} %get-tuple-element.17), channel_id=1, source_target_pairs={{0,1},{1,0},{2,3},{3,2},{4,5},{5,4},{6,7},{7,6},{8,9},{9,8},{10,11... | collective-permute-start | bytes 393224 | tf_op jit(solution)/shard_map/ppermute | solution.py:179
  2.8 5.9 %collective-permute-start.8 = (f32[2,128,128]{2,1,0:T(8,128)S(1)}, f32[2,128,128]{2,1,0:T(8,128)S(1)}, u32[]{:S(2)}, u32[]{:S(2)}) collective-permute-start(f32[2,128,128]{2,1,0:T(8,128)S(1)} %add.159), channel_id=1, source_target_pairs={{0,2},{1,9},{2,0},{3,11},{4,6},{5,13},{6,4},{7,15},{8,10},{9,1},{1... | collective-permute-start | bytes 393224 | tf_op jit(solution)/shard_map/ppermute | solution.py:201
  5.8 5.0 %collective-permute-start.1 = (f32[2,128,128]{2,1,0:T(8,128)S(1)}, f32[2,128,128]{2,1,0:T(8,128)S(1)}, u32[]{:S(2)}, u32[]{:S(2)}) collective-permute-start(f32[2,128,128]{2,1,0:T(8,128)S(1)} %get-tuple-element.29), channel_id=1, source_target_pairs={{0,2},{1,17},{2,0},{3,19},{4,6},{5,21},{6,4},{7,23},{8,10},{9,25},... | collective-permute-start | bytes 393224 | tf_op jit(solution)/shard_map/ppermute | solution.py:201
  8.7 5.0 %collective-permute-start.9 = (f32[2,128,128]{2,1,0:T(8,128)S(1)}, f32[2,128,128]{2,1,0:T(8,128)S(1)}, u32[]{:S(2)}, u32[]{:S(2)}) collective-permute-start(f32[2,128,128]{2,1,0:T(8,128)S(1)} %add.160), channel_id=1, source_target_pairs={{0,4},{1,17},{2,6},{3,19},{4,0},{5,21},{6,2},{7,23},{8,12},{9,25},... | collective-permute-start | bytes 393224 | tf_op jit(solution)/shard_map/ppermute | solution.py:201
  10.8 5.0 %collective-permute-start.2 = (f32[2,128,128]{2,1,0:T(8,128)S(1)}, f32[2,128,128]{2,1,0:T(8,128)S(1)}, u32[]{:S(2)}, u32[]{:S(2)}) collective-permute-start(f32[2,128,128]{2,1,0:T(8,128)S(1)} %get-tuple-element.27), channel_id=1, source_target_pairs={{0,4},{1,9},{2,6},{3,11},{4,0},{5,13},{6,2},{7,15},{8,12},{9,1},{1... | collective-permute-start | bytes 393224 | tf_op jit(solution)/shard_map/ppermute | solution.py:201
  13.8 2.3 %collective-permute-start.10 = (f32[4,128,128]{2,1,0:T(8,128)S(1)}, f32[4,128,128]{2,1,0:T(8,128)S(1)}, u32[]{:S(2)}, u32[]{:S(2)}) collective-permute-start(f32[4,128,128]{2,1,0:T(8,128)S(1)} %pad_maximum_fusion.1), channel_id=1, source_target_pairs={{0,1},{1,0},{2,3},{3,2},{4,5},{5,4},{6,7},{7,6},{8,9},{9,8},{10,11... | collective-permute-start | bytes 786440 | tf_op jit(solution)/shard_map/ppermute | solution.py:179
  15.9 1.8 %collective-permute-start.3 = (f32[4,128,128]{2,1,0:T(8,128)S(1)}, f32[4,128,128]{2,1,0:T(8,128)S(1)}, u32[]{:S(2)}, u32[]{:S(2)}) collective-permute-start(f32[4,128,128]{2,1,0:T(8,128)S(1)} %pad_maximum_fusion), channel_id=1, source_target_pairs={{0,1},{1,0},{2,3},{3,2},{4,5},{5,4},{6,7},{7,6},{8,9},{9,8},{10,11... | collective-permute-start | bytes 786440 | tf_op jit(solution)/shard_map/ppermute | solution.py:179
  16.2 5.0 %collective-permute-start.11 = (f32[2,128,128]{2,1,0:T(8,128)S(1)}, f32[2,128,128]{2,1,0:T(8,128)S(1)}, u32[]{:S(2)}, u32[]{:S(2)}) collective-permute-start(f32[2,128,128]{2,1,0:T(8,128)S(1)} %add_select_fusion.1), channel_id=1, source_target_pairs={{0,4},{1,9},{2,6},{3,11},{4,0},{5,13},{6,2},{7,15},{8,12},{9,1},{1... | collective-permute-start | bytes 393224 | tf_op jit(solution)/shard_map/ppermute | solution.py:201
  17.8 5.0 %collective-permute-start.4 = (f32[2,128,128]{2,1,0:T(8,128)S(1)}, f32[2,128,128]{2,1,0:T(8,128)S(1)}, u32[]{:S(2)}, u32[]{:S(2)}) collective-permute-start(f32[2,128,128]{2,1,0:T(8,128)S(1)} %add_select_fusion.5), channel_id=1, source_target_pairs={{0,4},{1,17},{2,6},{3,19},{4,0},{5,21},{6,2},{7,23},{8,12},{9,25},... | collective-permute-start | bytes 393224 | tf_op jit(solution)/shard_map/ppermute | solution.py:201
  21.2 3.0 %copy-start = (bf16[128,1024]{1,0:T(8,128)(2,1)S(1)}, bf16[128,1024]{1,0:T(8,128)(2,1)}, u32[]{:S(2)}) copy-start(bf16[128,1024]{1,0:T(8,128)(2,1)} %q_ref.1) | copy-start | bytes 786436
  21.3 5.0 %collective-permute-start.12 = (f32[2,128,128]{2,1,0:T(8,128)S(1)}, f32[2,128,128]{2,1,0:T(8,128)S(1)}, u32[]{:S(2)}, u32[]{:S(2)}) collective-permute-start(f32[2,128,128]{2,1,0:T(8,128)S(1)} %add_select_fusion), channel_id=1, source_target_pairs={{0,2},{1,17},{2,0},{3,19},{4,6},{5,21},{6,4},{7,23},{8,10},{9,25},... | collective-permute-start | bytes 393224 | tf_op jit(solution)/shard_map/ppermute | solution.py:201
  22.8 1.4 %copy-start.1 = (f32[1024]{0:T(1024)S(1)}, f32[1024]{0:T(1024)}, u32[]{:S(2)}) copy-start(f32[1024]{0:T(1024)} %param.7) | copy-start | bytes 12292
  22.9 5.0 %collective-permute-start.5 = (f32[2,128,128]{2,1,0:T(8,128)S(1)}, f32[2,128,128]{2,1,0:T(8,128)S(1)}, u32[]{:S(2)}, u32[]{:S(2)}) collective-permute-start(f32[2,128,128]{2,1,0:T(8,128)S(1)} %add_select_fusion.4.late_ref), channel_id=1, source_target_pairs={{0,2},{1,9},{2,0},{3,11},{4,6},{5,13},{6,4},{7,15},{8,10},{9,1},{1... | collective-permute-start | bytes 393224 | tf_op jit(solution)/shard_map/ppermute | solution.py:201
  26.3 2.2 %collective-permute-start.13 = (f32[2,128,128]{2,1,0:T(8,128)S(1)}, f32[2,128,128]{2,1,0:T(8,128)S(1)}, u32[]{:S(2)}, u32[]{:S(2)}) collective-permute-start(f32[2,128,128]{2,1,0:T(8,128)S(1)} %get-tuple-element.26), channel_id=1, source_target_pairs={{0,1},{1,0},{2,3},{3,2},{4,5},{5,4},{6,7},{7,6},{8,9},{9,8},{10,11... | collective-permute-start | bytes 393224 | tf_op jit(solution)/shard_map/ppermute | solution.py:179
  27.9 1.5 %collective-permute-start.6 = (f32[2,128,128]{2,1,0:T(8,128)S(1)}, f32[2,128,128]{2,1,0:T(8,128)S(1)}, u32[]{:S(2)}, u32[]{:S(2)}) collective-permute-start(f32[2,128,128]{2,1,0:T(8,128)S(1)} %get-tuple-element.24), channel_id=1, source_target_pairs={{0,1},{1,0},{2,3},{3,2},{4,5},{5,4},{6,7},{7,6},{8,9},{9,8},{10,11... | collective-permute-start | bytes 393224 | tf_op jit(solution)/shard_map/ppermute | solution.py:179

commit v9 on v8

--- a/solution.py
+++ b/solution.py
@@ -85,7 +85,7 @@
 
 
 def last_kernel(jobs, early, core_ref, fq_ref, intra_ref, gain_ref, *refs):
-    carried, (early_ref, out_hbm, buf_ref, sems) = refs[: len(jobs)], refs[len(jobs) :]
+    swapped_ref, kept_ref, early_ref, out_hbm, buf_ref, sems = refs
     core = core_ref[0]
     width = PER * HEAD_DIM
 
@@ -98,6 +98,7 @@
         return copy
 
     copies = [copy_out(job, early_ref.at[slot], slot) for slot, job in enumerate(early)]
+    carried = [[swapped_ref[i] + kept_ref[i] for i in range(PER)]]
     attend_heads(jobs, core, fq_ref, intra_ref, gain_ref, carried, buf_ref)
     copies += [copy_out(job, buf_ref.at[slot], len(early) + slot) for slot, job in enumerate(jobs)]
     for copy in copies:
@@ -219,7 +220,11 @@
         )
         if c == LATE_CHUNK:
             late = sent[LATE_STEP]
-        mine_parts.append(to_swap(after) + jnp.where(even, before, partner[c]))
+        swapped_back, kept_here = to_swap(after), jnp.where(even, before, partner[c])
+        if c == LAST_CHUNK:
+            last_parts = [swapped_back, kept_here]
+        else:
+            mine_parts.append(swapped_back + kept_here)
         their_parts.append(after + jnp.where(even, zero, more))
 
     fq, intra, gain = pl.pallas_call(
@@ -240,7 +245,7 @@
 
     early = [(1, c) for c in range(CHUNKS)] + [(0, c) for c in range(CHUNKS) if c != LAST_CHUNK]
     jobs = [(0, LAST_CHUNK)]
-    early_parts = their_parts + [x for c, x in enumerate(mine_parts) if c != LAST_CHUNK]
+    early_parts = their_parts + mine_parts
 
     def cost(n_jobs):
         return pl.CostEstimate(
@@ -259,7 +264,7 @@
     return pl.pallas_call(
         functools.partial(last_kernel, jobs, early),
         out_shape=jax.ShapeDtypeStruct(queries.shape, jnp.bfloat16),
-        in_specs=[SMEM] + [VMEM] * (3 + len(jobs) + 1),
+        in_specs=[SMEM] + [VMEM] * 6,
         out_specs=HBM,
         scratch_shapes=[
             pltpu.VMEM((len(jobs), rows, PER * HEAD_DIM), jnp.bfloat16),
@@ -268,7 +273,7 @@
         compiler_params=PARAMS,
         cost_estimate=cost(len(jobs)),
         name="attend_last",
-    )(core_arr, fq, intra, gain, mine_parts[LAST_CHUNK], done)
+    )(core_arr, fq, intra, gain, *last_parts, done)
 
 
 def solution(mesh):

time: 30.6 us -> 30.5 us (level)
  transfers between devices with their start and end apart: 14 -> 14, of which waited for: 8 -> 8; matrix products, arithmetic and copies ran while one was open for 1% -> 2% of each run, Pallas kernels for 6% -> 6%
where the time goes in v9:
time: 30.5 us; the launch traced here: 30.4 us
  starting transfers between devices  14.9 us (49%)
  waiting for transfers between devices  10.8 us (35%)
  Pallas kernels  4.15 us (14%)
  other arithmetic  0.46 us (2%)
    ppermute x8, starting transfers between devices, scan(): got = lax.ppermute(sent[-1], AXES, perm)  12.6 us
    ppermute x8, waiting for transfers between devices, scan(): got = lax.ppermute(sent[-1], AXES, perm)  9.53 us
    ppermute x6, starting transfers between devices, to_swap(): return lax.ppermute(x, AXES, swap)  2.26 us
    pallas_call x1, Pallas kernels, per_device(): pl.pallas_call(intra_kernel, out_shape=[jax.ShapeDtypeStruct(queries.shap...  1.36 us
    pallas_call x1, Pallas kernels, per_device(): pl.pallas_call(theirs_kernel, out_shape=[part] * CHUNKS + [jax.ShapeDtype...  1.28 us
    ppermute x6, waiting for transfers between devices, to_swap(): return lax.ppermute(x, AXES, swap)  1.27 us
    pallas_call x1, Pallas kernels, per_device(): pl.pallas_call(functools.partial(last_kernel, jobs, early), out_shape=jax...  0.93 us
  transfers between devices with their start and end apart: 14, of which 8 were waited for; matrix products, arithmetic and copies ran while one was open for 2% of the time, Pallas kernels for 6%

profile of v9, /device:TPU:0, one launch (start us, length us, event | category | flops | bytes accessed | tf_op | source)
XLA Modules:
  0.0 30.4 jit_solution(16990919100677946226)
XLA Ops:
  0.0 1.3 %theirs.1 = (f32[2,128,128]{2,1,0:T(8,128)S(1)}, f32[2,128,128]{2,1,0:T(8,128)S(1)}, bf16[128,1024]{1,0:T(8,128)(2,1)S(1)}, bf16[128,1024]{1,0:T(8,128)(2,1)S(1)}) custom-call(s32[1]{0:T(128)} %bitcast.core_ref, bf16[128,1024]{1,0:T(8,128)(2,1)} %k_hbm.1, bf16[128,1024]{1,0:T(8,128)(2,1)} %v_hbm.1), custom_call_target="tpu_custom_call" | custom-call | tf_op jit(solution)/shard_map/theirs/pallas_call | solution.py:143
  1.3 0.5 %collective-permute-start.7 = (f32[2,128,128]{2,1,0:T(8,128)S(1)}, f32[2,128,128]{2,1,0:T(8,128)S(1)}, u32[]{:S(2)}, u32[]{:S(2)}) collective-permute-start(f32[2,128,128]{2,1,0:T(8,128)S(1)} %get-tuple-element.22), channel_id=1, source_target_pairs={{0,1},{1,0},{2,3},{3,2},{4,5},{5,4},{6,7},{7,6},{8,9},{9,8},{10,11... | collective-permute-start | bytes 393224 | tf_op jit(solution)/shard_map/ppermute | solution.py:180
  1.9 0.2 mine.1
  2.1 0.7 %collective-permute-done.7 = f32[2,128,128]{2,1,0:T(8,128)S(1)} collective-permute-done((f32[2,128,128]{2,1,0:T(8,128)S(1)}, f32[2,128,128]{2,1,0:T(8,128)S(1)}, u32[]{:S(2)}, u32[]{:S(2)}) %collective-permute-start.7) | collective-permute-done | bytes 131104 | tf_op jit(solution)/shard_map/ppermute | solution.py:180
  2.8 2.9 %collective-permute-start.8 = (f32[2,128,128]{2,1,0:T(8,128)S(1)}, f32[2,128,128]{2,1,0:T(8,128)S(1)}, u32[]{:S(2)}, u32[]{:S(2)}) collective-permute-start(f32[2,128,128]{2,1,0:T(8,128)S(1)} %add.155), channel_id=1, source_target_pairs={{0,2},{1,9},{2,0},{3,11},{4,6},{5,13},{6,4},{7,15},{8,10},{9,1},{1... | collective-permute-start | bytes 393224 | tf_op jit(solution)/shard_map/ppermute | solution.py:202
  6.0 2.7 %collective-permute-done.8 = f32[2,128,128]{2,1,0:T(8,128)S(1)} collective-permute-done((f32[2,128,128]{2,1,0:T(8,128)S(1)}, f32[2,128,128]{2,1,0:T(8,128)S(1)}, u32[]{:S(2)}, u32[]{:S(2)}) %collective-permute-start.8) | collective-permute-done | bytes 131104 | tf_op jit(solution)/shard_map/ppermute | solution.py:202
  8.7 2.1 %collective-permute-start.9 = (f32[2,128,128]{2,1,0:T(8,128)S(1)}, f32[2,128,128]{2,1,0:T(8,128)S(1)}, u32[]{:S(2)}, u32[]{:S(2)}) collective-permute-start(f32[2,128,128]{2,1,0:T(8,128)S(1)} %add.156), channel_id=1, source_target_pairs={{0,4},{1,17},{2,6},{3,19},{4,0},{5,21},{6,2},{7,23},{8,12},{9,25},... | collective-permute-start | bytes 393224 | tf_op jit(solution)/shard_map/ppermute | solution.py:202
  10.8 1.6 %collective-permute-start.2 = (f32[2,128,128]{2,1,0:T(8,128)S(1)}, f32[2,128,128]{2,1,0:T(8,128)S(1)}, u32[]{:S(2)}, u32[]{:S(2)}) collective-permute-start(f32[2,128,128]{2,1,0:T(8,128)S(1)} %get-tuple-element.27), channel_id=1, source_target_pairs={{0,4},{1,9},{2,6},{3,11},{4,0},{5,13},{6,2},{7,15},{8,12},{9,1},{1... | collective-permute-start | bytes 393224 | tf_op jit(solution)/shard_map/ppermute | solution.py:202
  12.4 1.4 %collective-permute-done.9 = f32[2,128,128]{2,1,0:T(8,128)S(1)} collective-permute-done((f32[2,128,128]{2,1,0:T(8,128)S(1)}, f32[2,128,128]{2,1,0:T(8,128)S(1)}, u32[]{:S(2)}, u32[]{:S(2)}) %collective-permute-start.9) | collective-permute-done | bytes 131104 | tf_op jit(solution)/shard_map/ppermute | solution.py:202
  13.9 2.0 %collective-permute-done.2 = f32[2,128,128]{2,1,0:T(8,128)S(1)} collective-permute-done((f32[2,128,128]{2,1,0:T(8,128)S(1)}, f32[2,128,128]{2,1,0:T(8,128)S(1)}, u32[]{:S(2)}, u32[]{:S(2)}) %collective-permute-start.2) | collective-permute-done | bytes 131104 | tf_op jit(solution)/shard_map/ppermute | solution.py:202
  16.0 0.2 collective-permute-start.3
  16.2 1.6 %collective-permute-start.11 = (f32[2,128,128]{2,1,0:T(8,128)S(1)}, f32[2,128,128]{2,1,0:T(8,128)S(1)}, u32[]{:S(2)}, u32[]{:S(2)}) collective-permute-start(f32[2,128,128]{2,1,0:T(8,128)S(1)} %add_select_fusion.1), channel_id=1, source_target_pairs={{0,4},{1,9},{2,6},{3,11},{4,0},{5,13},{6,2},{7,15},{8,12},{9,1},{1... | collective-permute-start | bytes 393224 | tf_op jit(solution)/shard_map/ppermute | solution.py:202
  17.8 1.4 %collective-permute-start.4 = (f32[2,128,128]{2,1,0:T(8,128)S(1)}, f32[2,128,128]{2,1,0:T(8,128)S(1)}, u32[]{:S(2)}, u32[]{:S(2)}) collective-permute-start(f32[2,128,128]{2,1,0:T(8,128)S(1)} %add_select_fusion.5), channel_id=1, source_target_pairs={{0,4},{1,17},{2,6},{3,19},{4,0},{5,21},{6,2},{7,23},{8,12},{9,25},... | collective-permute-start | bytes 393224 | tf_op jit(solution)/shard_map/ppermute | solution.py:202
  19.2 2.1 %collective-permute-done.11 = f32[2,128,128]{2,1,0:T(8,128)S(1)} collective-permute-done((f32[2,128,128]{2,1,0:T(8,128)S(1)}, f32[2,128,128]{2,1,0:T(8,128)S(1)}, u32[]{:S(2)}, u32[]{:S(2)}) %collective-permute-start.11) | collective-permute-done | bytes 131104 | tf_op jit(solution)/shard_map/ppermute | solution.py:202
  21.3 1.6 %collective-permute-start.12 = (f32[2,128,128]{2,1,0:T(8,128)S(1)}, f32[2,128,128]{2,1,0:T(8,128)S(1)}, u32[]{:S(2)}, u32[]{:S(2)}) collective-permute-start(f32[2,128,128]{2,1,0:T(8,128)S(1)} %add_select_fusion), channel_id=1, source_target_pairs={{0,2},{1,17},{2,0},{3,19},{4,6},{5,21},{6,4},{7,23},{8,10},{9,25},... | collective-permute-start | bytes 393224 | tf_op jit(solution)/shard_map/ppermute | solution.py:202
  22.9 1.4 %collective-permute-start.5 = (f32[2,128,128]{2,1,0:T(8,128)S(1)}, f32[2,128,128]{2,1,0:T(8,128)S(1)}, u32[]{:S(2)}, u32[]{:S(2)}) collective-permute-start(f32[2,128,128]{2,1,0:T(8,128)S(1)} %add_select_fusion.4.late_ref), channel_id=1, source_target_pairs={{0,2},{1,9},{2,0},{3,11},{4,6},{5,13},{6,4},{7,15},{8,10},{9,1},{1... | collective-permute-start | bytes 393224 | tf_op jit(solution)/shard_map/ppermute | solution.py:202
  24.3 1.4 %intra.1 = (bf16[128,1024]{1,0:T(8,128)(2,1)S(1)}, f32[128,1024]{1,0:T(8,128)S(1)}, f32[1,1024]{1,0:T(1,128)S(1)}) custom-call(bf16[128,1024]{1,0:T(8,128)(2,1)S(1)} %copy-done, bf16[128,1024]{1,0:T(8,128)(2,1)S(1)} %get-tuple-element.14.k_ref, bf16[128,1024]{1,0:T(8,128)(2,1)S(1)} %get-tuple-element.15.v_ref, f32[1,1024]{1,0:T(1,128)S(1)} %bitcast.2, ...), custom_call_target="tpu_custom_call" | custom-call | flops 67108864 | bytes 1572864 | tf_op jit(solution)/shard_map/intra/pallas_call | solution.py:230
  25.6 0.7 %collective-permute-done.12 = f32[2,128,128]{2,1,0:T(8,128)S(1)} collective-permute-done((f32[2,128,128]{2,1,0:T(8,128)S(1)}, f32[2,128,128]{2,1,0:T(8,128)S(1)}, u32[]{:S(2)}, u32[]{:S(2)}) %collective-permute-start.12) | collective-permute-done | bytes 131104 | tf_op jit(solution)/shard_map/ppermute | solution.py:202
  26.3 0.9 %collective-permute-start.13 = (f32[2,128,128]{2,1,0:T(8,128)S(1)}, f32[2,128,128]{2,1,0:T(8,128)S(1)}, u32[]{:S(2)}, u32[]{:S(2)}) collective-permute-start(f32[2,128,128]{2,1,0:T(8,128)S(1)} %get-tuple-element.26), channel_id=1, source_target_pairs={{0,1},{1,0},{2,3},{3,2},{4,5},{5,4},{6,7},{7,6},{8,9},{9,8},{10,11... | collective-permute-start | bytes 393224 | tf_op jit(solution)/shard_map/ppermute | solution.py:180
  27.2 0.7 %collective-permute-done.5 = f32[2,128,128]{2,1,0:T(8,128)S(1)} collective-permute-done((f32[2,128,128]{2,1,0:T(8,128)S(1)}, f32[2,128,128]{2,1,0:T(8,128)S(1)}, u32[]{:S(2)}, u32[]{:S(2)}) %collective-permute-start.5) | collective-permute-done | bytes 131104 | tf_op jit(solution)/shard_map/ppermute | solution.py:202
  27.9 0.5 %collective-permute-start.6 = (f32[2,128,128]{2,1,0:T(8,128)S(1)}, f32[2,128,128]{2,1,0:T(8,128)S(1)}, u32[]{:S(2)}, u32[]{:S(2)}) collective-permute-start(f32[2,128,128]{2,1,0:T(8,128)S(1)} %get-tuple-element.24), channel_id=1, source_target_pairs={{0,1},{1,0},{2,3},{3,2},{4,5},{5,4},{6,7},{7,6},{8,9},{9,8},{10,11... | collective-permute-start | bytes 393224 | tf_op jit(solution)/shard_map/ppermute | solution.py:180
  28.5 0.3 %attend_early.1.refs_2_ = bf16[3,128,256]{2,1,0:T(8,128)(2,1)S(1)} custom-call(s32[1]{0:T(128)} %bitcast.core_ref, bf16[128,1024]{1,0:T(8,128)(2,1)S(1)} %get-tuple-element.18.fq_ref, f32[128,1024]{1,0:T(8,128)S(1)} %get-tuple-element.19.intra_ref, f32[1,1024]{1,0:T(1,128)S(1)} %get-tuple-element.20.gain_ref, f32[2,128,128]{2,1,0:T(8,128)S(1)} %get-tuple-element.25.refs_0_, ...), custom_call_target="tpu_custom_call" | custom-call | flops 25165824 | bytes 393216 | tf_op jit(solution)/shard_map/attend_early/pallas_call | solution.py:255
  28.9 0.6 %collective-permute-done.6.refs_0_ = f32[2,128,128]{2,1,0:T(8,128)S(1)} collective-permute-done((f32[2,128,128]{2,1,0:T(8,128)S(1)}, f32[2,128,128]{2,1,0:T(8,128)S(1)}, u32[]{:S(2)}, u32[]{:S(2)}) %collective-permute-start.6) | collective-permute-done | bytes 131104 | tf_op jit(solution)/shard_map/ppermute | solution.py:180
  29.5 0.9 %attend_last.1 = bf16[128,1024]{1,0:T(8,128)(2,1)} custom-call(s32[1]{0:T(128)} %bitcast.core_ref, bf16[128,1024]{1,0:T(8,128)(2,1)S(1)} %get-tuple-element.18.fq_ref, f32[128,1024]{1,0:T(8,128)S(1)} %get-tuple-element.19.intra_ref, f32[1,1024]{1,0:T(1,128)S(1)} %get-tuple-element.20.gain_ref, f32[2,128,128]{2,1,0:T(8,128)S(1)} %collective-permute-done.6.refs_0_, ...), custom_call_target="tpu_custom_call" | custom-call | flops 8388608 | bytes 131072 | tf_op jit(solution)/shard_map/attend_last/pallas_call | solution.py:264
  (28 shorter events, 0.8 us)
Async XLA Ops:
  1.3 1.5 %collective-permute-start.7 = (f32[2,128,128]{2,1,0:T(8,128)S(1)}, f32[2,128,128]{2,1,0:T(8,128)S(1)}, u32[]{:S(2)}, u32[]{:S(2)}) collective-permute-start(f32[2,128,128]{2,1,0:T(8,128)S(1)} %get-tuple-element.22), channel_id=1, source_target_pairs={{0,1},{1,0},{2,3},{3,2},{4,5},{5,4},{6,7},{7,6},{8,9},{9,8},{10,11... | collective-permute-start | bytes 393224 | tf_op jit(solution)/shard_map/ppermute | solution.py:180
  1.8 4.0 %collective-permute-start = (f32[2,128,128]{2,1,0:T(8,128)S(1)}, f32[2,128,128]{2,1,0:T(8,128)S(1)}, u32[]{:S(2)}, u32[]{:S(2)}) collective-permute-start(f32[2,128,128]{2,1,0:T(8,128)S(1)} %get-tuple-element.17), channel_id=1, source_target_pairs={{0,1},{1,0},{2,3},{3,2},{4,5},{5,4},{6,7},{7,6},{8,9},{9,8},{10,11... | collective-permute-start | bytes 393224 | tf_op jit(solution)/shard_map/ppermute | solution.py:180
  2.8 5.9 %collective-permute-start.8 = (f32[2,128,128]{2,1,0:T(8,128)S(1)}, f32[2,128,128]{2,1,0:T(8,128)S(1)}, u32[]{:S(2)}, u32[]{:S(2)}) collective-permute-start(f32[2,128,128]{2,1,0:T(8,128)S(1)} %add.155), channel_id=1, source_target_pairs={{0,2},{1,9},{2,0},{3,11},{4,6},{5,13},{6,4},{7,15},{8,10},{9,1},{1... | collective-permute-start | bytes 393224 | tf_op jit(solution)/shard_map/ppermute | solution.py:202
  5.8 5.0 %collective-permute-start.1 = (f32[2,128,128]{2,1,0:T(8,128)S(1)}, f32[2,128,128]{2,1,0:T(8,128)S(1)}, u32[]{:S(2)}, u32[]{:S(2)}) collective-permute-start(f32[2,128,128]{2,1,0:T(8,128)S(1)} %get-tuple-element.29), channel_id=1, source_target_pairs={{0,2},{1,17},{2,0},{3,19},{4,6},{5,21},{6,4},{7,23},{8,10},{9,25},... | collective-permute-start | bytes 393224 | tf_op jit(solution)/shard_map/ppermute | solution.py:202
  8.7 5.0 %collective-permute-start.9 = (f32[2,128,128]{2,1,0:T(8,128)S(1)}, f32[2,128,128]{2,1,0:T(8,128)S(1)}, u32[]{:S(2)}, u32[]{:S(2)}) collective-permute-start(f32[2,128,128]{2,1,0:T(8,128)S(1)} %add.156), channel_id=1, source_target_pairs={{0,4},{1,17},{2,6},{3,19},{4,0},{5,21},{6,2},{7,23},{8,12},{9,25},... | collective-permute-start | bytes 393224 | tf_op jit(solution)/shard_map/ppermute | solution.py:202
  10.8 5.0 %collective-permute-start.2 = (f32[2,128,128]{2,1,0:T(8,128)S(1)}, f32[2,128,128]{2,1,0:T(8,128)S(1)}, u32[]{:S(2)}, u32[]{:S(2)}) collective-permute-start(f32[2,128,128]{2,1,0:T(8,128)S(1)} %get-tuple-element.27), channel_id=1, source_target_pairs={{0,4},{1,9},{2,6},{3,11},{4,0},{5,13},{6,2},{7,15},{8,12},{9,1},{1... | collective-permute-start | bytes 393224 | tf_op jit(solution)/shard_map/ppermute | solution.py:202
  13.8 2.3 %collective-permute-start.10 = (f32[4,128,128]{2,1,0:T(8,128)S(1)}, f32[4,128,128]{2,1,0:T(8,128)S(1)}, u32[]{:S(2)}, u32[]{:S(2)}) collective-permute-start(f32[4,128,128]{2,1,0:T(8,128)S(1)} %pad_maximum_fusion.1), channel_id=1, source_target_pairs={{0,1},{1,0},{2,3},{3,2},{4,5},{5,4},{6,7},{7,6},{8,9},{9,8},{10,11... | collective-permute-start | bytes 786440 | tf_op jit(solution)/shard_map/ppermute | solution.py:180
  16.0 1.8 %collective-permute-start.3 = (f32[4,128,128]{2,1,0:T(8,128)S(1)}, f32[4,128,128]{2,1,0:T(8,128)S(1)}, u32[]{:S(2)}, u32[]{:S(2)}) collective-permute-start(f32[4,128,128]{2,1,0:T(8,128)S(1)} %pad_maximum_fusion), channel_id=1, source_target_pairs={{0,1},{1,0},{2,3},{3,2},{4,5},{5,4},{6,7},{7,6},{8,9},{9,8},{10,11... | collective-permute-start | bytes 786440 | tf_op jit(solution)/shard_map/ppermute | solution.py:180
  16.2 5.0 %collective-permute-start.11 = (f32[2,128,128]{2,1,0:T(8,128)S(1)}, f32[2,128,128]{2,1,0:T(8,128)S(1)}, u32[]{:S(2)}, u32[]{:S(2)}) collective-permute-start(f32[2,128,128]{2,1,0:T(8,128)S(1)} %add_select_fusion.1), channel_id=1, source_target_pairs={{0,4},{1,9},{2,6},{3,11},{4,0},{5,13},{6,2},{7,15},{8,12},{9,1},{1... | collective-permute-start | bytes 393224 | tf_op jit(solution)/shard_map/ppermute | solution.py:202
  17.8 5.0 %collective-permute-start.4 = (f32[2,128,128]{2,1,0:T(8,128)S(1)}, f32[2,128,128]{2,1,0:T(8,128)S(1)}, u32[]{:S(2)}, u32[]{:S(2)}) collective-permute-start(f32[2,128,128]{2,1,0:T(8,128)S(1)} %add_select_fusion.5), channel_id=1, source_target_pairs={{0,4},{1,17},{2,6},{3,19},{4,0},{5,21},{6,2},{7,23},{8,12},{9,25},... | collective-permute-start | bytes 393224 | tf_op jit(solution)/shard_map/ppermute | solution.py:202
  21.3 3.0 %copy-start = (bf16[128,1024]{1,0:T(8,128)(2,1)S(1)}, bf16[128,1024]{1,0:T(8,128)(2,1)}, u32[]{:S(2)}) copy-start(bf16[128,1024]{1,0:T(8,128)(2,1)} %q_ref.1) | copy-start | bytes 786436
  21.3 5.0 %collective-permute-start.12 = (f32[2,128,128]{2,1,0:T(8,128)S(1)}, f32[2,128,128]{2,1,0:T(8,128)S(1)}, u32[]{:S(2)}, u32[]{:S(2)}) collective-permute-start(f32[2,128,128]{2,1,0:T(8,128)S(1)} %add_select_fusion), channel_id=1, source_target_pairs={{0,2},{1,17},{2,0},{3,19},{4,6},{5,21},{6,4},{7,23},{8,10},{9,25},... | collective-permute-start | bytes 393224 | tf_op jit(solution)/shard_map/ppermute | solution.py:202
  22.8 1.4 %copy-start.1 = (f32[1024]{0:T(1024)S(1)}, f32[1024]{0:T(1024)}, u32[]{:S(2)}) copy-start(f32[1024]{0:T(1024)} %param.7) | copy-start | bytes 12292
  22.9 5.0 %collective-permute-start.5 = (f32[2,128,128]{2,1,0:T(8,128)S(1)}, f32[2,128,128]{2,1,0:T(8,128)S(1)}, u32[]{:S(2)}, u32[]{:S(2)}) collective-permute-start(f32[2,128,128]{2,1,0:T(8,128)S(1)} %add_select_fusion.4.late_ref), channel_id=1, source_target_pairs={{0,2},{1,9},{2,0},{3,11},{4,6},{5,13},{6,4},{7,15},{8,10},{9,1},{1... | collective-permute-start | bytes 393224 | tf_op jit(solution)/shard_map/ppermute | solution.py:202
  26.3 2.1 %collective-permute-start.13 = (f32[2,128,128]{2,1,0:T(8,128)S(1)}, f32[2,128,128]{2,1,0:T(8,128)S(1)}, u32[]{:S(2)}, u32[]{:S(2)}) collective-permute-start(f32[2,128,128]{2,1,0:T(8,128)S(1)} %get-tuple-element.26), channel_id=1, source_target_pairs={{0,1},{1,0},{2,3},{3,2},{4,5},{5,4},{6,7},{7,6},{8,9},{9,8},{10,11... | collective-permute-start | bytes 393224 | tf_op jit(solution)/shard_map/ppermute | solution.py:180
  27.9 1.5 %collective-permute-start.6 = (f32[2,128,128]{2,1,0:T(8,128)S(1)}, f32[2,128,128]{2,1,0:T(8,128)S(1)}, u32[]{:S(2)}, u32[]{:S(2)}) collective-permute-start(f32[2,128,128]{2,1,0:T(8,128)S(1)} %get-tuple-element.24), channel_id=1, source_target_pairs={{0,1},{1,0},{2,3},{3,2},{4,5},{5,4},{6,7},{7,6},{8,9},{9,8},{10,11... | collective-permute-start | bytes 393224 | tf_op jit(solution)/shard_map/ppermute | solution.py:180

commit v10 on v8

--- a/solution.py
+++ b/solution.py
@@ -69,7 +69,7 @@
         intra_ref[:, cols] = jnp.dot(weights, v_ref[:, cols], preferred_element_type=jnp.float32)
 
 
-def attend_heads(jobs, core, fq_ref, intra_ref, gain_ref, carried, buf_ref):
+def attend_heads(jobs, core, fq_ref, intra_ref, gain_ref, carried, buf_ref, finished=None):
     for slot, (half, c) in enumerate(jobs):
         for i in range(PER):
             cols = head_cols((core * HALF + half * HALF + c * PER + i) % HEADS)
@@ -78,6 +78,8 @@
             meansq = jnp.mean(total * total, axis=-1, keepdims=True)
             normed = total * lax.rsqrt(meansq + 1e-06) * gain_ref[:, cols]
             buf_ref[slot, :, i * HEAD_DIM : (i + 1) * HEAD_DIM] = normed.astype(jnp.bfloat16)
+            if finished is not None:
+                finished(slot, i, cols)
 
 
 def early_kernel(jobs, core_ref, fq_ref, intra_ref, gain_ref, *refs):
@@ -98,8 +100,14 @@
         return copy
 
     copies = [copy_out(job, early_ref.at[slot], slot) for slot, job in enumerate(early)]
-    attend_heads(jobs, core, fq_ref, intra_ref, gain_ref, carried, buf_ref)
-    copies += [copy_out(job, buf_ref.at[slot], len(early) + slot) for slot, job in enumerate(jobs)]
+
+    def finished(slot, i, cols):
+        source = buf_ref.at[slot, :, i * HEAD_DIM : (i + 1) * HEAD_DIM]
+        copy = pltpu.make_async_copy(source, out_hbm.at[:, cols], sems.at[len(early) + slot * PER + i])
+        copy.start()
+        copies.append(copy)
+
+    attend_heads(jobs, core, fq_ref, intra_ref, gain_ref, carried, buf_ref, finished)
     for copy in copies:
         copy.wait()
 
@@ -263,7 +271,7 @@
         out_specs=HBM,
         scratch_shapes=[
             pltpu.VMEM((len(jobs), rows, PER * HEAD_DIM), jnp.bfloat16),
-            pltpu.SemaphoreType.DMA((len(early) + len(jobs),)),
+            pltpu.SemaphoreType.DMA((len(early) + len(jobs) * PER,)),
         ],
         compiler_params=PARAMS,
         cost_estimate=cost(len(jobs)),

time: 30.6 us -> 30.6 us (level)
  no operation moved by 1% of the time
where the time goes in v10:
time: 30.6 us; the launch traced here: 30.4 us
  starting transfers between devices  14.9 us (49%)
  waiting for transfers between devices  10.8 us (35%)
  Pallas kernels  4.15 us (14%)
  other arithmetic  0.48 us (2%)
    ppermute x8, starting transfers between devices, scan(): got = lax.ppermute(sent[-1], AXES, perm)  12.6 us
    ppermute x8, waiting for transfers between devices, scan(): got = lax.ppermute(sent[-1], AXES, perm)  9.54 us
    ppermute x6, starting transfers between devices, to_swap(): return lax.ppermute(x, AXES, swap)  2.26 us
    pallas_call x1, Pallas kernels, per_device(): pl.pallas_call(intra_kernel, out_shape=[jax.ShapeDtypeStruct(queries.shap...  1.36 us
    pallas_call x1, Pallas kernels, per_device(): pl.pallas_call(theirs_kernel, out_shape=[part] * CHUNKS + [jax.ShapeDtype...  1.28 us
    ppermute x6, waiting for transfers between devices, to_swap(): return lax.ppermute(x, AXES, swap)  1.27 us
    pallas_call x1, Pallas kernels, per_device(): pl.pallas_call(functools.partial(last_kernel, jobs, early), out_shape=jax...  0.93 us
  transfers between devices with their start and end apart: 14, of which 8 were waited for; matrix products, arithmetic and copies ran while one was open for 1% of the time, Pallas kernels for 6%

profile of v10, /device:TPU:0, one launch (start us, length us, event | category | flops | bytes accessed | tf_op | source)
XLA Modules:
  0.0 30.4 jit_solution(3083188058228163312)
XLA Ops:
  0.0 1.3 %theirs.1 = (f32[2,128,128]{2,1,0:T(8,128)S(1)}, f32[2,128,128]{2,1,0:T(8,128)S(1)}, bf16[128,1024]{1,0:T(8,128)(2,1)S(1)}, bf16[128,1024]{1,0:T(8,128)(2,1)S(1)}) custom-call(s32[1]{0:T(128)} %bitcast.core_ref, bf16[128,1024]{1,0:T(8,128)(2,1)} %k_hbm.1, bf16[128,1024]{1,0:T(8,128)(2,1)} %v_hbm.1), custom_call_target="tpu_custom_call" | custom-call | tf_op jit(solution)/shard_map/theirs/pallas_call | solution.py:150
  1.3 0.5 %collective-permute-start.7 = (f32[2,128,128]{2,1,0:T(8,128)S(1)}, f32[2,128,128]{2,1,0:T(8,128)S(1)}, u32[]{:S(2)}, u32[]{:S(2)}) collective-permute-start(f32[2,128,128]{2,1,0:T(8,128)S(1)} %get-tuple-element.22), channel_id=1, source_target_pairs={{0,1},{1,0},{2,3},{3,2},{4,5},{5,4},{6,7},{7,6},{8,9},{9,8},{10,11... | collective-permute-start | bytes 393224 | tf_op jit(solution)/shard_map/ppermute | solution.py:187
  1.9 0.2 mine.1
  2.1 0.7 %collective-permute-done.7 = f32[2,128,128]{2,1,0:T(8,128)S(1)} collective-permute-done((f32[2,128,128]{2,1,0:T(8,128)S(1)}, f32[2,128,128]{2,1,0:T(8,128)S(1)}, u32[]{:S(2)}, u32[]{:S(2)}) %collective-permute-start.7) | collective-permute-done | bytes 131104 | tf_op jit(solution)/shard_map/ppermute | solution.py:187
  2.8 2.9 %collective-permute-start.8 = (f32[2,128,128]{2,1,0:T(8,128)S(1)}, f32[2,128,128]{2,1,0:T(8,128)S(1)}, u32[]{:S(2)}, u32[]{:S(2)}) collective-permute-start(f32[2,128,128]{2,1,0:T(8,128)S(1)} %add.159), channel_id=1, source_target_pairs={{0,2},{1,9},{2,0},{3,11},{4,6},{5,13},{6,4},{7,15},{8,10},{9,1},{1... | collective-permute-start | bytes 393224 | tf_op jit(solution)/shard_map/ppermute | solution.py:209
  6.0 2.7 %collective-permute-done.8 = f32[2,128,128]{2,1,0:T(8,128)S(1)} collective-permute-done((f32[2,128,128]{2,1,0:T(8,128)S(1)}, f32[2,128,128]{2,1,0:T(8,128)S(1)}, u32[]{:S(2)}, u32[]{:S(2)}) %collective-permute-start.8) | collective-permute-done | bytes 131104 | tf_op jit(solution)/shard_map/ppermute | solution.py:209
  8.7 2.1 %collective-permute-start.9 = (f32[2,128,128]{2,1,0:T(8,128)S(1)}, f32[2,128,128]{2,1,0:T(8,128)S(1)}, u32[]{:S(2)}, u32[]{:S(2)}) collective-permute-start(f32[2,128,128]{2,1,0:T(8,128)S(1)} %add.160), channel_id=1, source_target_pairs={{0,4},{1,17},{2,6},{3,19},{4,0},{5,21},{6,2},{7,23},{8,12},{9,25},... | collective-permute-start | bytes 393224 | tf_op jit(solution)/shard_map/ppermute | solution.py:209
  10.8 1.6 %collective-permute-start.2 = (f32[2,128,128]{2,1,0:T(8,128)S(1)}, f32[2,128,128]{2,1,0:T(8,128)S(1)}, u32[]{:S(2)}, u32[]{:S(2)}) collective-permute-start(f32[2,128,128]{2,1,0:T(8,128)S(1)} %get-tuple-element.27), channel_id=1, source_target_pairs={{0,4},{1,9},{2,6},{3,11},{4,0},{5,13},{6,2},{7,15},{8,12},{9,1},{1... | collective-permute-start | bytes 393224 | tf_op jit(solution)/shard_map/ppermute | solution.py:209
  12.4 1.4 %collective-permute-done.9 = f32[2,128,128]{2,1,0:T(8,128)S(1)} collective-permute-done((f32[2,128,128]{2,1,0:T(8,128)S(1)}, f32[2,128,128]{2,1,0:T(8,128)S(1)}, u32[]{:S(2)}, u32[]{:S(2)}) %collective-permute-start.9) | collective-permute-done | bytes 131104 | tf_op jit(solution)/shard_map/ppermute | solution.py:209
  13.9 2.0 %collective-permute-done.2 = f32[2,128,128]{2,1,0:T(8,128)S(1)} collective-permute-done((f32[2,128,128]{2,1,0:T(8,128)S(1)}, f32[2,128,128]{2,1,0:T(8,128)S(1)}, u32[]{:S(2)}, u32[]{:S(2)}) %collective-permute-start.2) | collective-permute-done | bytes 131104 | tf_op jit(solution)/shard_map/ppermute | solution.py:209
  15.9 0.2 collective-permute-start.3
  16.2 1.6 %collective-permute-start.11 = (f32[2,128,128]{2,1,0:T(8,128)S(1)}, f32[2,128,128]{2,1,0:T(8,128)S(1)}, u32[]{:S(2)}, u32[]{:S(2)}) collective-permute-start(f32[2,128,128]{2,1,0:T(8,128)S(1)} %add_select_fusion.1), channel_id=1, source_target_pairs={{0,4},{1,9},{2,6},{3,11},{4,0},{5,13},{6,2},{7,15},{8,12},{9,1},{1... | collective-permute-start | bytes 393224 | tf_op jit(solution)/shard_map/ppermute | solution.py:209
  17.8 1.4 %collective-permute-start.4 = (f32[2,128,128]{2,1,0:T(8,128)S(1)}, f32[2,128,128]{2,1,0:T(8,128)S(1)}, u32[]{:S(2)}, u32[]{:S(2)}) collective-permute-start(f32[2,128,128]{2,1,0:T(8,128)S(1)} %add_select_fusion.5), channel_id=1, source_target_pairs={{0,4},{1,17},{2,6},{3,19},{4,0},{5,21},{6,2},{7,23},{8,12},{9,25},... | collective-permute-start | bytes 393224 | tf_op jit(solution)/shard_map/ppermute | solution.py:209
  19.1 2.1 %collective-permute-done.11 = f32[2,128,128]{2,1,0:T(8,128)S(1)} collective-permute-done((f32[2,128,128]{2,1,0:T(8,128)S(1)}, f32[2,128,128]{2,1,0:T(8,128)S(1)}, u32[]{:S(2)}, u32[]{:S(2)}) %collective-permute-start.11) | collective-permute-done | bytes 131104 | tf_op jit(solution)/shard_map/ppermute | solution.py:209
  21.3 1.6 %collective-permute-start.12 = (f32[2,128,128]{2,1,0:T(8,128)S(1)}, f32[2,128,128]{2,1,0:T(8,128)S(1)}, u32[]{:S(2)}, u32[]{:S(2)}) collective-permute-start(f32[2,128,128]{2,1,0:T(8,128)S(1)} %add_select_fusion), channel_id=1, source_target_pairs={{0,2},{1,17},{2,0},{3,19},{4,6},{5,21},{6,4},{7,23},{8,10},{9,25},... | collective-permute-start | bytes 393224 | tf_op jit(solution)/shard_map/ppermute | solution.py:209
  22.9 1.4 %collective-permute-start.5 = (f32[2,128,128]{2,1,0:T(8,128)S(1)}, f32[2,128,128]{2,1,0:T(8,128)S(1)}, u32[]{:S(2)}, u32[]{:S(2)}) collective-permute-start(f32[2,128,128]{2,1,0:T(8,128)S(1)} %add_select_fusion.4.late_ref), channel_id=1, source_target_pairs={{0,2},{1,9},{2,0},{3,11},{4,6},{5,13},{6,4},{7,15},{8,10},{9,1},{1... | collective-permute-start | bytes 393224 | tf_op jit(solution)/shard_map/ppermute | solution.py:209
  24.3 1.4 %intra.1 = (bf16[128,1024]{1,0:T(8,128)(2,1)S(1)}, f32[128,1024]{1,0:T(8,128)S(1)}, f32[1,1024]{1,0:T(1,128)S(1)}) custom-call(bf16[128,1024]{1,0:T(8,128)(2,1)S(1)} %copy-done, bf16[128,1024]{1,0:T(8,128)(2,1)S(1)} %get-tuple-element.14.k_ref, bf16[128,1024]{1,0:T(8,128)(2,1)S(1)} %get-tuple-element.15.v_ref, f32[1,1024]{1,0:T(1,128)S(1)} %bitcast.2, ...), custom_call_target="tpu_custom_call" | custom-call | flops 67108864 | bytes 1572864 | tf_op jit(solution)/shard_map/intra/pallas_call | solution.py:233
  25.6 0.7 %collective-permute-done.12 = f32[2,128,128]{2,1,0:T(8,128)S(1)} collective-permute-done((f32[2,128,128]{2,1,0:T(8,128)S(1)}, f32[2,128,128]{2,1,0:T(8,128)S(1)}, u32[]{:S(2)}, u32[]{:S(2)}) %collective-permute-start.12) | collective-permute-done | bytes 131104 | tf_op jit(solution)/shard_map/ppermute | solution.py:209
  26.3 0.9 %collective-permute-start.13 = (f32[2,128,128]{2,1,0:T(8,128)S(1)}, f32[2,128,128]{2,1,0:T(8,128)S(1)}, u32[]{:S(2)}, u32[]{:S(2)}) collective-permute-start(f32[2,128,128]{2,1,0:T(8,128)S(1)} %get-tuple-element.26), channel_id=1, source_target_pairs={{0,1},{1,0},{2,3},{3,2},{4,5},{5,4},{6,7},{7,6},{8,9},{9,8},{10,11... | collective-permute-start | bytes 393224 | tf_op jit(solution)/shard_map/ppermute | solution.py:187
  27.2 0.7 %collective-permute-done.5 = f32[2,128,128]{2,1,0:T(8,128)S(1)} collective-permute-done((f32[2,128,128]{2,1,0:T(8,128)S(1)}, f32[2,128,128]{2,1,0:T(8,128)S(1)}, u32[]{:S(2)}, u32[]{:S(2)}) %collective-permute-start.5) | collective-permute-done | bytes 131104 | tf_op jit(solution)/shard_map/ppermute | solution.py:209
  27.9 0.5 %collective-permute-start.6 = (f32[2,128,128]{2,1,0:T(8,128)S(1)}, f32[2,128,128]{2,1,0:T(8,128)S(1)}, u32[]{:S(2)}, u32[]{:S(2)}) collective-permute-start(f32[2,128,128]{2,1,0:T(8,128)S(1)} %get-tuple-element.24), channel_id=1, source_target_pairs={{0,1},{1,0},{2,3},{3,2},{4,5},{5,4},{6,7},{7,6},{8,9},{9,8},{10,11... | collective-permute-start | bytes 393224 | tf_op jit(solution)/shard_map/ppermute | solution.py:187
  28.5 0.3 %attend_early.1.refs_1_ = bf16[3,128,256]{2,1,0:T(8,128)(2,1)S(1)} custom-call(s32[1]{0:T(128)} %bitcast.core_ref, bf16[128,1024]{1,0:T(8,128)(2,1)S(1)} %get-tuple-element.18.fq_ref, f32[128,1024]{1,0:T(8,128)S(1)} %get-tuple-element.19.intra_ref, f32[1,1024]{1,0:T(1,128)S(1)} %get-tuple-element.20.gain_ref, f32[2,128,128]{2,1,0:T(8,128)S(1)} %get-tuple-element.25.refs_0_, ...), custom_call_target="tpu_custom_call" | custom-call | flops 25165824 | bytes 393216 | tf_op jit(solution)/shard_map/attend_early/pallas_call | solution.py:258
  28.9 0.6 %collective-permute-done.6 = f32[2,128,128]{2,1,0:T(8,128)S(1)} collective-permute-done((f32[2,128,128]{2,1,0:T(8,128)S(1)}, f32[2,128,128]{2,1,0:T(8,128)S(1)}, u32[]{:S(2)}, u32[]{:S(2)}) %collective-permute-start.6) | collective-permute-done | bytes 131104 | tf_op jit(solution)/shard_map/ppermute | solution.py:187
  29.5 0.9 %attend_last.1 = bf16[128,1024]{1,0:T(8,128)(2,1)} custom-call(s32[1]{0:T(128)} %bitcast.core_ref, bf16[128,1024]{1,0:T(8,128)(2,1)S(1)} %get-tuple-element.18.fq_ref, f32[128,1024]{1,0:T(8,128)S(1)} %get-tuple-element.19.intra_ref, f32[1,1024]{1,0:T(1,128)S(1)} %get-tuple-element.20.gain_ref, f32[2,128,128]{2,1,0:T(8,128)S(1)} %select_add_fusion.7.refs_0_, ...), custom_call_target="tpu_custom_call" | custom-call | flops 8388608 | bytes 131072 | tf_op jit(solution)/shard_map/attend_last/pallas_call | solution.py:267
  (29 shorter events, 0.9 us)
Async XLA Ops:
  1.3 1.5 %collective-permute-start.7 = (f32[2,128,128]{2,1,0:T(8,128)S(1)}, f32[2,128,128]{2,1,0:T(8,128)S(1)}, u32[]{:S(2)}, u32[]{:S(2)}) collective-permute-start(f32[2,128,128]{2,1,0:T(8,128)S(1)} %get-tuple-element.22), channel_id=1, source_target_pairs={{0,1},{1,0},{2,3},{3,2},{4,5},{5,4},{6,7},{7,6},{8,9},{9,8},{10,11... | collective-permute-start | bytes 393224 | tf_op jit(solution)/shard_map/ppermute | solution.py:187
  1.8 4.0 %collective-permute-start = (f32[2,128,128]{2,1,0:T(8,128)S(1)}, f32[2,128,128]{2,1,0:T(8,128)S(1)}, u32[]{:S(2)}, u32[]{:S(2)}) collective-permute-start(f32[2,128,128]{2,1,0:T(8,128)S(1)} %get-tuple-element.17), channel_id=1, source_target_pairs={{0,1},{1,0},{2,3},{3,2},{4,5},{5,4},{6,7},{7,6},{8,9},{9,8},{10,11... | collective-permute-start | bytes 393224 | tf_op jit(solution)/shard_map/ppermute | solution.py:187
  2.8 5.9 %collective-permute-start.8 = (f32[2,128,128]{2,1,0:T(8,128)S(1)}, f32[2,128,128]{2,1,0:T(8,128)S(1)}, u32[]{:S(2)}, u32[]{:S(2)}) collective-permute-start(f32[2,128,128]{2,1,0:T(8,128)S(1)} %add.159), channel_id=1, source_target_pairs={{0,2},{1,9},{2,0},{3,11},{4,6},{5,13},{6,4},{7,15},{8,10},{9,1},{1... | collective-permute-start | bytes 393224 | tf_op jit(solution)/shard_map/ppermute | solution.py:209
  5.8 5.0 %collective-permute-start.1 = (f32[2,128,128]{2,1,0:T(8,128)S(1)}, f32[2,128,128]{2,1,0:T(8,128)S(1)}, u32[]{:S(2)}, u32[]{:S(2)}) collective-permute-start(f32[2,128,128]{2,1,0:T(8,128)S(1)} %get-tuple-element.29), channel_id=1, source_target_pairs={{0,2},{1,17},{2,0},{3,19},{4,6},{5,21},{6,4},{7,23},{8,10},{9,25},... | collective-permute-start | bytes 393224 | tf_op jit(solution)/shard_map/ppermute | solution.py:209
  8.7 5.0 %collective-permute-start.9 = (f32[2,128,128]{2,1,0:T(8,128)S(1)}, f32[2,128,128]{2,1,0:T(8,128)S(1)}, u32[]{:S(2)}, u32[]{:S(2)}) collective-permute-start(f32[2,128,128]{2,1,0:T(8,128)S(1)} %add.160), channel_id=1, source_target_pairs={{0,4},{1,17},{2,6},{3,19},{4,0},{5,21},{6,2},{7,23},{8,12},{9,25},... | collective-permute-start | bytes 393224 | tf_op jit(solution)/shard_map/ppermute | solution.py:209
  10.8 5.0 %collective-permute-start.2 = (f32[2,128,128]{2,1,0:T(8,128)S(1)}, f32[2,128,128]{2,1,0:T(8,128)S(1)}, u32[]{:S(2)}, u32[]{:S(2)}) collective-permute-start(f32[2,128,128]{2,1,0:T(8,128)S(1)} %get-tuple-element.27), channel_id=1, source_target_pairs={{0,4},{1,9},{2,6},{3,11},{4,0},{5,13},{6,2},{7,15},{8,12},{9,1},{1... | collective-permute-start | bytes 393224 | tf_op jit(solution)/shard_map/ppermute | solution.py:209
  13.8 2.3 %collective-permute-start.10 = (f32[4,128,128]{2,1,0:T(8,128)S(1)}, f32[4,128,128]{2,1,0:T(8,128)S(1)}, u32[]{:S(2)}, u32[]{:S(2)}) collective-permute-start(f32[4,128,128]{2,1,0:T(8,128)S(1)} %pad_maximum_fusion.1), channel_id=1, source_target_pairs={{0,1},{1,0},{2,3},{3,2},{4,5},{5,4},{6,7},{7,6},{8,9},{9,8},{10,11... | collective-permute-start | bytes 786440 | tf_op jit(solution)/shard_map/ppermute | solution.py:187
  15.9 1.8 %collective-permute-start.3 = (f32[4,128,128]{2,1,0:T(8,128)S(1)}, f32[4,128,128]{2,1,0:T(8,128)S(1)}, u32[]{:S(2)}, u32[]{:S(2)}) collective-permute-start(f32[4,128,128]{2,1,0:T(8,128)S(1)} %pad_maximum_fusion), channel_id=1, source_target_pairs={{0,1},{1,0},{2,3},{3,2},{4,5},{5,4},{6,7},{7,6},{8,9},{9,8},{10,11... | collective-permute-start | bytes 786440 | tf_op jit(solution)/shard_map/ppermute | solution.py:187
  16.2 5.0 %collective-permute-start.11 = (f32[2,128,128]{2,1,0:T(8,128)S(1)}, f32[2,128,128]{2,1,0:T(8,128)S(1)}, u32[]{:S(2)}, u32[]{:S(2)}) collective-permute-start(f32[2,128,128]{2,1,0:T(8,128)S(1)} %add_select_fusion.1), channel_id=1, source_target_pairs={{0,4},{1,9},{2,6},{3,11},{4,0},{5,13},{6,2},{7,15},{8,12},{9,1},{1... | collective-permute-start | bytes 393224 | tf_op jit(solution)/shard_map/ppermute | solution.py:209
  17.8 5.0 %collective-permute-start.4 = (f32[2,128,128]{2,1,0:T(8,128)S(1)}, f32[2,128,128]{2,1,0:T(8,128)S(1)}, u32[]{:S(2)}, u32[]{:S(2)}) collective-permute-start(f32[2,128,128]{2,1,0:T(8,128)S(1)} %add_select_fusion.5), channel_id=1, source_target_pairs={{0,4},{1,17},{2,6},{3,19},{4,0},{5,21},{6,2},{7,23},{8,12},{9,25},... | collective-permute-start | bytes 393224 | tf_op jit(solution)/shard_map/ppermute | solution.py:209
  21.2 3.0 %copy-start = (bf16[128,1024]{1,0:T(8,128)(2,1)S(1)}, bf16[128,1024]{1,0:T(8,128)(2,1)}, u32[]{:S(2)}) copy-start(bf16[128,1024]{1,0:T(8,128)(2,1)} %q_ref.1) | copy-start | bytes 786436
  21.3 5.0 %collective-permute-start.12 = (f32[2,128,128]{2,1,0:T(8,128)S(1)}, f32[2,128,128]{2,1,0:T(8,128)S(1)}, u32[]{:S(2)}, u32[]{:S(2)}) collective-permute-start(f32[2,128,128]{2,1,0:T(8,128)S(1)} %add_select_fusion), channel_id=1, source_target_pairs={{0,2},{1,17},{2,0},{3,19},{4,6},{5,21},{6,4},{7,23},{8,10},{9,25},... | collective-permute-start | bytes 393224 | tf_op jit(solution)/shard_map/ppermute | solution.py:209
  22.8 1.4 %copy-start.1 = (f32[1024]{0:T(1024)S(1)}, f32[1024]{0:T(1024)}, u32[]{:S(2)}) copy-start(f32[1024]{0:T(1024)} %param.7) | copy-start | bytes 12292
  22.9 5.0 %collective-permute-start.5 = (f32[2,128,128]{2,1,0:T(8,128)S(1)}, f32[2,128,128]{2,1,0:T(8,128)S(1)}, u32[]{:S(2)}, u32[]{:S(2)}) collective-permute-start(f32[2,128,128]{2,1,0:T(8,128)S(1)} %add_select_fusion.4.late_ref), channel_id=1, source_target_pairs={{0,2},{1,9},{2,0},{3,11},{4,6},{5,13},{6,4},{7,15},{8,10},{9,1},{1... | collective-permute-start | bytes 393224 | tf_op jit(solution)/shard_map/ppermute | solution.py:209
  26.3 2.2 %collective-permute-start.13 = (f32[2,128,128]{2,1,0:T(8,128)S(1)}, f32[2,128,128]{2,1,0:T(8,128)S(1)}, u32[]{:S(2)}, u32[]{:S(2)}) collective-permute-start(f32[2,128,128]{2,1,0:T(8,128)S(1)} %get-tuple-element.26), channel_id=1, source_target_pairs={{0,1},{1,0},{2,3},{3,2},{4,5},{5,4},{6,7},{7,6},{8,9},{9,8},{10,11... | collective-permute-start | bytes 393224 | tf_op jit(solution)/shard_map/ppermute | solution.py:187
  27.9 1.5 %collective-permute-start.6 = (f32[2,128,128]{2,1,0:T(8,128)S(1)}, f32[2,128,128]{2,1,0:T(8,128)S(1)}, u32[]{:S(2)}, u32[]{:S(2)}) collective-permute-start(f32[2,128,128]{2,1,0:T(8,128)S(1)} %get-tuple-element.24), channel_id=1, source_target_pairs={{0,1},{1,0},{2,3},{3,2},{4,5},{5,4},{6,7},{7,6},{8,9},{9,8},{10,11... | collective-permute-start | bytes 393224 | tf_op jit(solution)/shard_map/ppermute | solution.py:187

commit v11 on v10

--- a/solution.py
+++ b/solution.py
@@ -70,16 +70,19 @@
 
 
 def attend_heads(jobs, core, fq_ref, intra_ref, gain_ref, carried, buf_ref, finished=None):
+    work = []
     for slot, (half, c) in enumerate(jobs):
         for i in range(PER):
             cols = head_cols((core * HALF + half * HALF + c * PER + i) % HEADS)
             state = carried[slot][i].astype(jnp.bfloat16)
             total = intra_ref[:, cols] + jnp.dot(fq_ref[:, cols], state, preferred_element_type=jnp.float32)
-            meansq = jnp.mean(total * total, axis=-1, keepdims=True)
-            normed = total * lax.rsqrt(meansq + 1e-06) * gain_ref[:, cols]
-            buf_ref[slot, :, i * HEAD_DIM : (i + 1) * HEAD_DIM] = normed.astype(jnp.bfloat16)
-            if finished is not None:
-                finished(slot, i, cols)
+            work.append((slot, i, cols, total))
+    for slot, i, cols, total in work:
+        meansq = jnp.mean(total * total, axis=-1, keepdims=True)
+        normed = total * lax.rsqrt(meansq + 1e-06) * gain_ref[:, cols]
+        buf_ref[slot, :, i * HEAD_DIM : (i + 1) * HEAD_DIM] = normed.astype(jnp.bfloat16)
+        if finished is not None:
+            finished(slot, i, cols)
 
 
 def early_kernel(jobs, core_ref, fq_ref, intra_ref, gain_ref, *refs):

time: 30.6 us -> 30.6 us (level)
  no operation moved by 1% of the time
where the time goes in v11:
time: 30.6 us; the launch traced here: 30.4 us
  starting transfers between devices  14.9 us (49%)
  waiting for transfers between devices  10.8 us (35%)
  Pallas kernels  4.15 us (14%)
  other arithmetic  0.48 us (2%)
    ppermute x8, starting transfers between devices, scan(): got = lax.ppermute(sent[-1], AXES, perm)  12.6 us
    ppermute x8, waiting for transfers between devices, scan(): got = lax.ppermute(sent[-1], AXES, perm)  9.54 us
    ppermute x6, starting transfers between devices, to_swap(): return lax.ppermute(x, AXES, swap)  2.26 us
    pallas_call x1, Pallas kernels, per_device(): pl.pallas_call(intra_kernel, out_shape=[jax.ShapeDtypeStruct(queries.shap...  1.36 us
    pallas_call x1, Pallas kernels, per_device(): pl.pallas_call(theirs_kernel, out_shape=[part] * CHUNKS + [jax.ShapeDtype...  1.28 us
    ppermute x6, waiting for transfers between devices, to_swap(): return lax.ppermute(x, AXES, swap)  1.27 us
    pallas_call x1, Pallas kernels, per_device(): pl.pallas_call(functools.partial(last_kernel, jobs, early), out_shape=jax...  0.93 us
  transfers between devices with their start and end apart: 14, of which 8 were waited for; matrix products, arithmetic and copies ran while one was open for 1% of the time, Pallas kernels for 6%

profile of v11, /device:TPU:0, one launch (start us, length us, event | category | flops | bytes accessed | tf_op | source)
XLA Modules:
  0.0 30.4 jit_solution(3083188058228163312)
XLA Ops:
  0.0 1.3 %theirs.1 = (f32[2,128,128]{2,1,0:T(8,128)S(1)}, f32[2,128,128]{2,1,0:T(8,128)S(1)}, bf16[128,1024]{1,0:T(8,128)(2,1)S(1)}, bf16[128,1024]{1,0:T(8,128)(2,1)S(1)}) custom-call(s32[1]{0:T(128)} %bitcast.core_ref, bf16[128,1024]{1,0:T(8,128)(2,1)} %k_hbm.1, bf16[128,1024]{1,0:T(8,128)(2,1)} %v_hbm.1), custom_call_target="tpu_custom_call" | custom-call | tf_op jit(solution)/shard_map/theirs/pallas_call | solution.py:153
  1.3 0.5 %collective-permute-start.7 = (f32[2,128,128]{2,1,0:T(8,128)S(1)}, f32[2,128,128]{2,1,0:T(8,128)S(1)}, u32[]{:S(2)}, u32[]{:S(2)}) collective-permute-start(f32[2,128,128]{2,1,0:T(8,128)S(1)} %get-tuple-element.22), channel_id=1, source_target_pairs={{0,1},{1,0},{2,3},{3,2},{4,5},{5,4},{6,7},{7,6},{8,9},{9,8},{10,11... | collective-permute-start | bytes 393224 | tf_op jit(solution)/shard_map/ppermute | solution.py:190
  1.9 0.2 mine.1
  2.1 0.7 %collective-permute-done.7 = f32[2,128,128]{2,1,0:T(8,128)S(1)} collective-permute-done((f32[2,128,128]{2,1,0:T(8,128)S(1)}, f32[2,128,128]{2,1,0:T(8,128)S(1)}, u32[]{:S(2)}, u32[]{:S(2)}) %collective-permute-start.7) | collective-permute-done | bytes 131104 | tf_op jit(solution)/shard_map/ppermute | solution.py:190
  2.8 2.9 %collective-permute-start.8 = (f32[2,128,128]{2,1,0:T(8,128)S(1)}, f32[2,128,128]{2,1,0:T(8,128)S(1)}, u32[]{:S(2)}, u32[]{:S(2)}) collective-permute-start(f32[2,128,128]{2,1,0:T(8,128)S(1)} %add.159), channel_id=1, source_target_pairs={{0,2},{1,9},{2,0},{3,11},{4,6},{5,13},{6,4},{7,15},{8,10},{9,1},{1... | collective-permute-start | bytes 393224 | tf_op jit(solution)/shard_map/ppermute | solution.py:212
  6.0 2.7 %collective-permute-done.8 = f32[2,128,128]{2,1,0:T(8,128)S(1)} collective-permute-done((f32[2,128,128]{2,1,0:T(8,128)S(1)}, f32[2,128,128]{2,1,0:T(8,128)S(1)}, u32[]{:S(2)}, u32[]{:S(2)}) %collective-permute-start.8) | collective-permute-done | bytes 131104 | tf_op jit(solution)/shard_map/ppermute | solution.py:212
  8.7 2.1 %collective-permute-start.9 = (f32[2,128,128]{2,1,0:T(8,128)S(1)}, f32[2,128,128]{2,1,0:T(8,128)S(1)}, u32[]{:S(2)}, u32[]{:S(2)}) collective-permute-start(f32[2,128,128]{2,1,0:T(8,128)S(1)} %add.160), channel_id=1, source_target_pairs={{0,4},{1,17},{2,6},{3,19},{4,0},{5,21},{6,2},{7,23},{8,12},{9,25},... | collective-permute-start | bytes 393224 | tf_op jit(solution)/shard_map/ppermute | solution.py:212
  10.8 1.6 %collective-permute-start.2 = (f32[2,128,128]{2,1,0:T(8,128)S(1)}, f32[2,128,128]{2,1,0:T(8,128)S(1)}, u32[]{:S(2)}, u32[]{:S(2)}) collective-permute-start(f32[2,128,128]{2,1,0:T(8,128)S(1)} %get-tuple-element.27), channel_id=1, source_target_pairs={{0,4},{1,9},{2,6},{3,11},{4,0},{5,13},{6,2},{7,15},{8,12},{9,1},{1... | collective-permute-start | bytes 393224 | tf_op jit(solution)/shard_map/ppermute | solution.py:212
  12.4 1.4 %collective-permute-done.9 = f32[2,128,128]{2,1,0:T(8,128)S(1)} collective-permute-done((f32[2,128,128]{2,1,0:T(8,128)S(1)}, f32[2,128,128]{2,1,0:T(8,128)S(1)}, u32[]{:S(2)}, u32[]{:S(2)}) %collective-permute-start.9) | collective-permute-done | bytes 131104 | tf_op jit(solution)/shard_map/ppermute | solution.py:212
  13.9 2.0 %collective-permute-done.2 = f32[2,128,128]{2,1,0:T(8,128)S(1)} collective-permute-done((f32[2,128,128]{2,1,0:T(8,128)S(1)}, f32[2,128,128]{2,1,0:T(8,128)S(1)}, u32[]{:S(2)}, u32[]{:S(2)}) %collective-permute-start.2) | collective-permute-done | bytes 131104 | tf_op jit(solution)/shard_map/ppermute | solution.py:212
  15.9 0.2 collective-permute-start.3
  16.2 1.6 %collective-permute-start.11 = (f32[2,128,128]{2,1,0:T(8,128)S(1)}, f32[2,128,128]{2,1,0:T(8,128)S(1)}, u32[]{:S(2)}, u32[]{:S(2)}) collective-permute-start(f32[2,128,128]{2,1,0:T(8,128)S(1)} %add_select_fusion.1), channel_id=1, source_target_pairs={{0,4},{1,9},{2,6},{3,11},{4,0},{5,13},{6,2},{7,15},{8,12},{9,1},{1... | collective-permute-start | bytes 393224 | tf_op jit(solution)/shard_map/ppermute | solution.py:212
  17.8 1.4 %collective-permute-start.4 = (f32[2,128,128]{2,1,0:T(8,128)S(1)}, f32[2,128,128]{2,1,0:T(8,128)S(1)}, u32[]{:S(2)}, u32[]{:S(2)}) collective-permute-start(f32[2,128,128]{2,1,0:T(8,128)S(1)} %add_select_fusion.5), channel_id=1, source_target_pairs={{0,4},{1,17},{2,6},{3,19},{4,0},{5,21},{6,2},{7,23},{8,12},{9,25},... | collective-permute-start | bytes 393224 | tf_op jit(solution)/shard_map/ppermute | solution.py:212
  19.1 2.1 %collective-permute-done.11 = f32[2,128,128]{2,1,0:T(8,128)S(1)} collective-permute-done((f32[2,128,128]{2,1,0:T(8,128)S(1)}, f32[2,128,128]{2,1,0:T(8,128)S(1)}, u32[]{:S(2)}, u32[]{:S(2)}) %collective-permute-start.11) | collective-permute-done | bytes 131104 | tf_op jit(solution)/shard_map/ppermute | solution.py:212
  21.3 1.6 %collective-permute-start.12 = (f32[2,128,128]{2,1,0:T(8,128)S(1)}, f32[2,128,128]{2,1,0:T(8,128)S(1)}, u32[]{:S(2)}, u32[]{:S(2)}) collective-permute-start(f32[2,128,128]{2,1,0:T(8,128)S(1)} %add_select_fusion), channel_id=1, source_target_pairs={{0,2},{1,17},{2,0},{3,19},{4,6},{5,21},{6,4},{7,23},{8,10},{9,25},... | collective-permute-start | bytes 393224 | tf_op jit(solution)/shard_map/ppermute | solution.py:212
  22.9 1.4 %collective-permute-start.5 = (f32[2,128,128]{2,1,0:T(8,128)S(1)}, f32[2,128,128]{2,1,0:T(8,128)S(1)}, u32[]{:S(2)}, u32[]{:S(2)}) collective-permute-start(f32[2,128,128]{2,1,0:T(8,128)S(1)} %add_select_fusion.4.late_ref), channel_id=1, source_target_pairs={{0,2},{1,9},{2,0},{3,11},{4,6},{5,13},{6,4},{7,15},{8,10},{9,1},{1... | collective-permute-start | bytes 393224 | tf_op jit(solution)/shard_map/ppermute | solution.py:212
  24.3 1.4 %intra.1 = (bf16[128,1024]{1,0:T(8,128)(2,1)S(1)}, f32[128,1024]{1,0:T(8,128)S(1)}, f32[1,1024]{1,0:T(1,128)S(1)}) custom-call(bf16[128,1024]{1,0:T(8,128)(2,1)S(1)} %copy-done, bf16[128,1024]{1,0:T(8,128)(2,1)S(1)} %get-tuple-element.14.k_ref, bf16[128,1024]{1,0:T(8,128)(2,1)S(1)} %get-tuple-element.15.v_ref, f32[1,1024]{1,0:T(1,128)S(1)} %bitcast.2, ...), custom_call_target="tpu_custom_call" | custom-call | flops 67108864 | bytes 1572864 | tf_op jit(solution)/shard_map/intra/pallas_call | solution.py:236
  25.6 0.7 %collective-permute-done.12 = f32[2,128,128]{2,1,0:T(8,128)S(1)} collective-permute-done((f32[2,128,128]{2,1,0:T(8,128)S(1)}, f32[2,128,128]{2,1,0:T(8,128)S(1)}, u32[]{:S(2)}, u32[]{:S(2)}) %collective-permute-start.12) | collective-permute-done | bytes 131104 | tf_op jit(solution)/shard_map/ppermute | solution.py:212
  26.3 0.9 %collective-permute-start.13 = (f32[2,128,128]{2,1,0:T(8,128)S(1)}, f32[2,128,128]{2,1,0:T(8,128)S(1)}, u32[]{:S(2)}, u32[]{:S(2)}) collective-permute-start(f32[2,128,128]{2,1,0:T(8,128)S(1)} %get-tuple-element.26), channel_id=1, source_target_pairs={{0,1},{1,0},{2,3},{3,2},{4,5},{5,4},{6,7},{7,6},{8,9},{9,8},{10,11... | collective-permute-start | bytes 393224 | tf_op jit(solution)/shard_map/ppermute | solution.py:190
  27.2 0.7 %collective-permute-done.5 = f32[2,128,128]{2,1,0:T(8,128)S(1)} collective-permute-done((f32[2,128,128]{2,1,0:T(8,128)S(1)}, f32[2,128,128]{2,1,0:T(8,128)S(1)}, u32[]{:S(2)}, u32[]{:S(2)}) %collective-permute-start.5) | collective-permute-done | bytes 131104 | tf_op jit(solution)/shard_map/ppermute | solution.py:212
  27.9 0.5 %collective-permute-start.6 = (f32[2,128,128]{2,1,0:T(8,128)S(1)}, f32[2,128,128]{2,1,0:T(8,128)S(1)}, u32[]{:S(2)}, u32[]{:S(2)}) collective-permute-start(f32[2,128,128]{2,1,0:T(8,128)S(1)} %get-tuple-element.24), channel_id=1, source_target_pairs={{0,1},{1,0},{2,3},{3,2},{4,5},{5,4},{6,7},{7,6},{8,9},{9,8},{10,11... | collective-permute-start | bytes 393224 | tf_op jit(solution)/shard_map/ppermute | solution.py:190
  28.5 0.3 %attend_early.1.refs_1_ = bf16[3,128,256]{2,1,0:T(8,128)(2,1)S(1)} custom-call(s32[1]{0:T(128)} %bitcast.core_ref, bf16[128,1024]{1,0:T(8,128)(2,1)S(1)} %get-tuple-element.18.fq_ref, f32[128,1024]{1,0:T(8,128)S(1)} %get-tuple-element.19.intra_ref, f32[1,1024]{1,0:T(1,128)S(1)} %get-tuple-element.20.gain_ref, f32[2,128,128]{2,1,0:T(8,128)S(1)} %get-tuple-element.25.refs_0_, ...), custom_call_target="tpu_custom_call" | custom-call | flops 25165824 | bytes 393216 | tf_op jit(solution)/shard_map/attend_early/pallas_call | solution.py:261
  28.9 0.6 %collective-permute-done.6 = f32[2,128,128]{2,1,0:T(8,128)S(1)} collective-permute-done((f32[2,128,128]{2,1,0:T(8,128)S(1)}, f32[2,128,128]{2,1,0:T(8,128)S(1)}, u32[]{:S(2)}, u32[]{:S(2)}) %collective-permute-start.6) | collective-permute-done | bytes 131104 | tf_op jit(solution)/shard_map/ppermute | solution.py:190
  29.5 0.9 %attend_last.1 = bf16[128,1024]{1,0:T(8,128)(2,1)} custom-call(s32[1]{0:T(128)} %bitcast.core_ref, bf16[128,1024]{1,0:T(8,128)(2,1)S(1)} %get-tuple-element.18.fq_ref, f32[128,1024]{1,0:T(8,128)S(1)} %get-tuple-element.19.intra_ref, f32[1,1024]{1,0:T(1,128)S(1)} %get-tuple-element.20.gain_ref, f32[2,128,128]{2,1,0:T(8,128)S(1)} %select_add_fusion.7.refs_0_, ...), custom_call_target="tpu_custom_call" | custom-call | flops 8388608 | bytes 131072 | tf_op jit(solution)/shard_map/attend_last/pallas_call | solution.py:270
  (29 shorter events, 0.9 us)
Async XLA Ops:
  1.3 1.5 %collective-permute-start.7 = (f32[2,128,128]{2,1,0:T(8,128)S(1)}, f32[2,128,128]{2,1,0:T(8,128)S(1)}, u32[]{:S(2)}, u32[]{:S(2)}) collective-permute-start(f32[2,128,128]{2,1,0:T(8,128)S(1)} %get-tuple-element.22), channel_id=1, source_target_pairs={{0,1},{1,0},{2,3},{3,2},{4,5},{5,4},{6,7},{7,6},{8,9},{9,8},{10,11... | collective-permute-start | bytes 393224 | tf_op jit(solution)/shard_map/ppermute | solution.py:190
  1.8 4.0 %collective-permute-start = (f32[2,128,128]{2,1,0:T(8,128)S(1)}, f32[2,128,128]{2,1,0:T(8,128)S(1)}, u32[]{:S(2)}, u32[]{:S(2)}) collective-permute-start(f32[2,128,128]{2,1,0:T(8,128)S(1)} %get-tuple-element.17), channel_id=1, source_target_pairs={{0,1},{1,0},{2,3},{3,2},{4,5},{5,4},{6,7},{7,6},{8,9},{9,8},{10,11... | collective-permute-start | bytes 393224 | tf_op jit(solution)/shard_map/ppermute | solution.py:190
  2.8 5.9 %collective-permute-start.8 = (f32[2,128,128]{2,1,0:T(8,128)S(1)}, f32[2,128,128]{2,1,0:T(8,128)S(1)}, u32[]{:S(2)}, u32[]{:S(2)}) collective-permute-start(f32[2,128,128]{2,1,0:T(8,128)S(1)} %add.159), channel_id=1, source_target_pairs={{0,2},{1,9},{2,0},{3,11},{4,6},{5,13},{6,4},{7,15},{8,10},{9,1},{1... | collective-permute-start | bytes 393224 | tf_op jit(solution)/shard_map/ppermute | solution.py:212
  5.8 5.0 %collective-permute-start.1 = (f32[2,128,128]{2,1,0:T(8,128)S(1)}, f32[2,128,128]{2,1,0:T(8,128)S(1)}, u32[]{:S(2)}, u32[]{:S(2)}) collective-permute-start(f32[2,128,128]{2,1,0:T(8,128)S(1)} %get-tuple-element.29), channel_id=1, source_target_pairs={{0,2},{1,17},{2,0},{3,19},{4,6},{5,21},{6,4},{7,23},{8,10},{9,25},... | collective-permute-start | bytes 393224 | tf_op jit(solution)/shard_map/ppermute | solution.py:212
  8.7 5.0 %collective-permute-start.9 = (f32[2,128,128]{2,1,0:T(8,128)S(1)}, f32[2,128,128]{2,1,0:T(8,128)S(1)}, u32[]{:S(2)}, u32[]{:S(2)}) collective-permute-start(f32[2,128,128]{2,1,0:T(8,128)S(1)} %add.160), channel_id=1, source_target_pairs={{0,4},{1,17},{2,6},{3,19},{4,0},{5,21},{6,2},{7,23},{8,12},{9,25},... | collective-permute-start | bytes 393224 | tf_op jit(solution)/shard_map/ppermute | solution.py:212
  10.8 5.0 %collective-permute-start.2 = (f32[2,128,128]{2,1,0:T(8,128)S(1)}, f32[2,128,128]{2,1,0:T(8,128)S(1)}, u32[]{:S(2)}, u32[]{:S(2)}) collective-permute-start(f32[2,128,128]{2,1,0:T(8,128)S(1)} %get-tuple-element.27), channel_id=1, source_target_pairs={{0,4},{1,9},{2,6},{3,11},{4,0},{5,13},{6,2},{7,15},{8,12},{9,1},{1... | collective-permute-start | bytes 393224 | tf_op jit(solution)/shard_map/ppermute | solution.py:212
  13.8 2.3 %collective-permute-start.10 = (f32[4,128,128]{2,1,0:T(8,128)S(1)}, f32[4,128,128]{2,1,0:T(8,128)S(1)}, u32[]{:S(2)}, u32[]{:S(2)}) collective-permute-start(f32[4,128,128]{2,1,0:T(8,128)S(1)} %pad_maximum_fusion.1), channel_id=1, source_target_pairs={{0,1},{1,0},{2,3},{3,2},{4,5},{5,4},{6,7},{7,6},{8,9},{9,8},{10,11... | collective-permute-start | bytes 786440 | tf_op jit(solution)/shard_map/ppermute | solution.py:190
  15.9 1.8 %collective-permute-start.3 = (f32[4,128,128]{2,1,0:T(8,128)S(1)}, f32[4,128,128]{2,1,0:T(8,128)S(1)}, u32[]{:S(2)}, u32[]{:S(2)}) collective-permute-start(f32[4,128,128]{2,1,0:T(8,128)S(1)} %pad_maximum_fusion), channel_id=1, source_target_pairs={{0,1},{1,0},{2,3},{3,2},{4,5},{5,4},{6,7},{7,6},{8,9},{9,8},{10,11... | collective-permute-start | bytes 786440 | tf_op jit(solution)/shard_map/ppermute | solution.py:190
  16.2 5.0 %collective-permute-start.11 = (f32[2,128,128]{2,1,0:T(8,128)S(1)}, f32[2,128,128]{2,1,0:T(8,128)S(1)}, u32[]{:S(2)}, u32[]{:S(2)}) collective-permute-start(f32[2,128,128]{2,1,0:T(8,128)S(1)} %add_select_fusion.1), channel_id=1, source_target_pairs={{0,4},{1,9},{2,6},{3,11},{4,0},{5,13},{6,2},{7,15},{8,12},{9,1},{1... | collective-permute-start | bytes 393224 | tf_op jit(solution)/shard_map/ppermute | solution.py:212
  17.8 5.0 %collective-permute-start.4 = (f32[2,128,128]{2,1,0:T(8,128)S(1)}, f32[2,128,128]{2,1,0:T(8,128)S(1)}, u32[]{:S(2)}, u32[]{:S(2)}) collective-permute-start(f32[2,128,128]{2,1,0:T(8,128)S(1)} %add_select_fusion.5), channel_id=1, source_target_pairs={{0,4},{1,17},{2,6},{3,19},{4,0},{5,21},{6,2},{7,23},{8,12},{9,25},... | collective-permute-start | bytes 393224 | tf_op jit(solution)/shard_map/ppermute | solution.py:212
  21.2 3.0 %copy-start = (bf16[128,1024]{1,0:T(8,128)(2,1)S(1)}, bf16[128,1024]{1,0:T(8,128)(2,1)}, u32[]{:S(2)}) copy-start(bf16[128,1024]{1,0:T(8,128)(2,1)} %q_ref.1) | copy-start | bytes 786436
  21.3 5.0 %collective-permute-start.12 = (f32[2,128,128]{2,1,0:T(8,128)S(1)}, f32[2,128,128]{2,1,0:T(8,128)S(1)}, u32[]{:S(2)}, u32[]{:S(2)}) collective-permute-start(f32[2,128,128]{2,1,0:T(8,128)S(1)} %add_select_fusion), channel_id=1, source_target_pairs={{0,2},{1,17},{2,0},{3,19},{4,6},{5,21},{6,4},{7,23},{8,10},{9,25},... | collective-permute-start | bytes 393224 | tf_op jit(solution)/shard_map/ppermute | solution.py:212
  22.8 1.4 %copy-start.1 = (f32[1024]{0:T(1024)S(1)}, f32[1024]{0:T(1024)}, u32[]{:S(2)}) copy-start(f32[1024]{0:T(1024)} %param.7) | copy-start | bytes 12292
  22.9 5.0 %collective-permute-start.5 = (f32[2,128,128]{2,1,0:T(8,128)S(1)}, f32[2,128,128]{2,1,0:T(8,128)S(1)}, u32[]{:S(2)}, u32[]{:S(2)}) collective-permute-start(f32[2,128,128]{2,1,0:T(8,128)S(1)} %add_select_fusion.4.late_ref), channel_id=1, source_target_pairs={{0,2},{1,9},{2,0},{3,11},{4,6},{5,13},{6,4},{7,15},{8,10},{9,1},{1... | collective-permute-start | bytes 393224 | tf_op jit(solution)/shard_map/ppermute | solution.py:212
  26.3 2.2 %collective-permute-start.13 = (f32[2,128,128]{2,1,0:T(8,128)S(1)}, f32[2,128,128]{2,1,0:T(8,128)S(1)}, u32[]{:S(2)}, u32[]{:S(2)}) collective-permute-start(f32[2,128,128]{2,1,0:T(8,128)S(1)} %get-tuple-element.26), channel_id=1, source_target_pairs={{0,1},{1,0},{2,3},{3,2},{4,5},{5,4},{6,7},{7,6},{8,9},{9,8},{10,11... | collective-permute-start | bytes 393224 | tf_op jit(solution)/shard_map/ppermute | solution.py:190
  27.9 1.5 %collective-permute-start.6 = (f32[2,128,128]{2,1,0:T(8,128)S(1)}, f32[2,128,128]{2,1,0:T(8,128)S(1)}, u32[]{:S(2)}, u32[]{:S(2)}) collective-permute-start(f32[2,128,128]{2,1,0:T(8,128)S(1)} %get-tuple-element.24), channel_id=1, source_target_pairs={{0,1},{1,0},{2,3},{3,2},{4,5},{5,4},{6,7},{7,6},{8,9},{9,8},{10,11... | collective-permute-start | bytes 393224 | tf_op jit(solution)/shard_map/ppermute | solution.py:190

commit v12 on v10

--- a/solution.py
+++ b/solution.py
@@ -14,7 +14,7 @@
 CHUNKS = 2
 PER = HALF // CHUNKS
 LAST_CHUNK = 1
-LATE_CHUNK = 1
+LATE_CHUNK = 0
 LATE_STEP = -1
 AXES = ("outer", "inner")
 

time: 30.6 us -> 30.6 us (level)
  no operation moved by 1% of the time
where the time goes in v12:
time: 30.6 us; the launch traced here: 30.4 us
  starting transfers between devices  14.9 us (49%)
  waiting for transfers between devices  10.8 us (35%)
  Pallas kernels  4.15 us (14%)
  other arithmetic  0.48 us (2%)
    ppermute x8, starting transfers between devices, scan(): got = lax.ppermute(sent[-1], AXES, perm)  12.6 us
    ppermute x8, waiting for transfers between devices, scan(): got = lax.ppermute(sent[-1], AXES, perm)  9.54 us
    ppermute x6, starting transfers between devices, to_swap(): return lax.ppermute(x, AXES, swap)  2.26 us
    pallas_call x1, Pallas kernels, per_device(): pl.pallas_call(intra_kernel, out_shape=[jax.ShapeDtypeStruct(queries.shap...  1.36 us
    pallas_call x1, Pallas kernels, per_device(): pl.pallas_call(theirs_kernel, out_shape=[part] * CHUNKS + [jax.ShapeDtype...  1.28 us
    ppermute x6, waiting for transfers between devices, to_swap(): return lax.ppermute(x, AXES, swap)  1.27 us
    pallas_call x1, Pallas kernels, per_device(): pl.pallas_call(functools.partial(last_kernel, jobs, early), out_shape=jax...  0.93 us
  transfers between devices with their start and end apart: 14, of which 8 were waited for; matrix products, arithmetic and copies ran while one was open for 1% of the time, Pallas kernels for 6%

profile of v12, /device:TPU:0, one launch (start us, length us, event | category | flops | bytes accessed | tf_op | source)
XLA Modules:
  0.0 30.4 jit_solution(1084193761504924505)
XLA Ops:
  0.0 1.3 %theirs.1 = (f32[2,128,128]{2,1,0:T(8,128)S(1)}, f32[2,128,128]{2,1,0:T(8,128)S(1)}, bf16[128,1024]{1,0:T(8,128)(2,1)S(1)}, bf16[128,1024]{1,0:T(8,128)(2,1)S(1)}) custom-call(s32[1]{0:T(128)} %bitcast.core_ref, bf16[128,1024]{1,0:T(8,128)(2,1)} %k_hbm.1, bf16[128,1024]{1,0:T(8,128)(2,1)} %v_hbm.1), custom_call_target="tpu_custom_call" | custom-call | tf_op jit(solution)/shard_map/theirs/pallas_call | solution.py:150
  1.3 0.5 %collective-permute-start = (f32[2,128,128]{2,1,0:T(8,128)S(1)}, f32[2,128,128]{2,1,0:T(8,128)S(1)}, u32[]{:S(2)}, u32[]{:S(2)}) collective-permute-start(f32[2,128,128]{2,1,0:T(8,128)S(1)} %get-tuple-element.17), channel_id=1, source_target_pairs={{0,1},{1,0},{2,3},{3,2},{4,5},{5,4},{6,7},{7,6},{8,9},{9,8},{10,11... | collective-permute-start | bytes 393224 | tf_op jit(solution)/shard_map/ppermute | solution.py:187
  1.9 0.2 mine.1
  2.1 0.7 %collective-permute-done = f32[2,128,128]{2,1,0:T(8,128)S(1)} collective-permute-done((f32[2,128,128]{2,1,0:T(8,128)S(1)}, f32[2,128,128]{2,1,0:T(8,128)S(1)}, u32[]{:S(2)}, u32[]{:S(2)}) %collective-permute-start) | collective-permute-done | bytes 131104 | tf_op jit(solution)/shard_map/ppermute | solution.py:187
  2.8 2.9 %collective-permute-start.1 = (f32[2,128,128]{2,1,0:T(8,128)S(1)}, f32[2,128,128]{2,1,0:T(8,128)S(1)}, u32[]{:S(2)}, u32[]{:S(2)}) collective-permute-start(f32[2,128,128]{2,1,0:T(8,128)S(1)} %add.137), channel_id=1, source_target_pairs={{0,2},{1,9},{2,0},{3,11},{4,6},{5,13},{6,4},{7,15},{8,10},{9,1},{1... | collective-permute-start | bytes 393224 | tf_op jit(solution)/shard_map/ppermute | solution.py:209
  6.0 2.7 %collective-permute-done.1 = f32[2,128,128]{2,1,0:T(8,128)S(1)} collective-permute-done((f32[2,128,128]{2,1,0:T(8,128)S(1)}, f32[2,128,128]{2,1,0:T(8,128)S(1)}, u32[]{:S(2)}, u32[]{:S(2)}) %collective-permute-start.1) | collective-permute-done | bytes 131104 | tf_op jit(solution)/shard_map/ppermute | solution.py:209
  8.7 2.1 %collective-permute-start.2 = (f32[2,128,128]{2,1,0:T(8,128)S(1)}, f32[2,128,128]{2,1,0:T(8,128)S(1)}, u32[]{:S(2)}, u32[]{:S(2)}) collective-permute-start(f32[2,128,128]{2,1,0:T(8,128)S(1)} %add.138), channel_id=1, source_target_pairs={{0,4},{1,17},{2,6},{3,19},{4,0},{5,21},{6,2},{7,23},{8,12},{9,25},... | collective-permute-start | bytes 393224 | tf_op jit(solution)/shard_map/ppermute | solution.py:209
  10.8 1.6 %collective-permute-start.7 = (f32[2,128,128]{2,1,0:T(8,128)S(1)}, f32[2,128,128]{2,1,0:T(8,128)S(1)}, u32[]{:S(2)}, u32[]{:S(2)}) collective-permute-start(f32[2,128,128]{2,1,0:T(8,128)S(1)} %get-tuple-element.27), channel_id=1, source_target_pairs={{0,4},{1,9},{2,6},{3,11},{4,0},{5,13},{6,2},{7,15},{8,12},{9,1},{1... | collective-permute-start | bytes 393224 | tf_op jit(solution)/shard_map/ppermute | solution.py:209
  12.4 1.4 %collective-permute-done.2 = f32[2,128,128]{2,1,0:T(8,128)S(1)} collective-permute-done((f32[2,128,128]{2,1,0:T(8,128)S(1)}, f32[2,128,128]{2,1,0:T(8,128)S(1)}, u32[]{:S(2)}, u32[]{:S(2)}) %collective-permute-start.2) | collective-permute-done | bytes 131104 | tf_op jit(solution)/shard_map/ppermute | solution.py:209
  13.9 2.0 %collective-permute-done.7 = f32[2,128,128]{2,1,0:T(8,128)S(1)} collective-permute-done((f32[2,128,128]{2,1,0:T(8,128)S(1)}, f32[2,128,128]{2,1,0:T(8,128)S(1)}, u32[]{:S(2)}, u32[]{:S(2)}) %collective-permute-start.7) | collective-permute-done | bytes 131104 | tf_op jit(solution)/shard_map/ppermute | solution.py:209
  15.9 0.2 collective-permute-start.8
  16.2 1.6 %collective-permute-start.4 = (f32[2,128,128]{2,1,0:T(8,128)S(1)}, f32[2,128,128]{2,1,0:T(8,128)S(1)}, u32[]{:S(2)}, u32[]{:S(2)}) collective-permute-start(f32[2,128,128]{2,1,0:T(8,128)S(1)} %add_select_fusion.6), channel_id=1, source_target_pairs={{0,4},{1,9},{2,6},{3,11},{4,0},{5,13},{6,2},{7,15},{8,12},{9,1},{1... | collective-permute-start | bytes 393224 | tf_op jit(solution)/shard_map/ppermute | solution.py:209
  17.8 1.4 %collective-permute-start.9 = (f32[2,128,128]{2,1,0:T(8,128)S(1)}, f32[2,128,128]{2,1,0:T(8,128)S(1)}, u32[]{:S(2)}, u32[]{:S(2)}) collective-permute-start(f32[2,128,128]{2,1,0:T(8,128)S(1)} %add_select_fusion.1), channel_id=1, source_target_pairs={{0,4},{1,17},{2,6},{3,19},{4,0},{5,21},{6,2},{7,23},{8,12},{9,25},... | collective-permute-start | bytes 393224 | tf_op jit(solution)/shard_map/ppermute | solution.py:209
  19.1 2.1 %collective-permute-done.4 = f32[2,128,128]{2,1,0:T(8,128)S(1)} collective-permute-done((f32[2,128,128]{2,1,0:T(8,128)S(1)}, f32[2,128,128]{2,1,0:T(8,128)S(1)}, u32[]{:S(2)}, u32[]{:S(2)}) %collective-permute-start.4) | collective-permute-done | bytes 131104 | tf_op jit(solution)/shard_map/ppermute | solution.py:209
  21.3 1.6 %collective-permute-start.12 = (f32[2,128,128]{2,1,0:T(8,128)S(1)}, f32[2,128,128]{2,1,0:T(8,128)S(1)}, u32[]{:S(2)}, u32[]{:S(2)}) collective-permute-start(f32[2,128,128]{2,1,0:T(8,128)S(1)} %add_select_fusion.5.late_ref), channel_id=1, source_target_pairs={{0,2},{1,17},{2,0},{3,19},{4,6},{5,21},{6,4},{7,23},{8,10},{9,25},... | collective-permute-start | bytes 393224 | tf_op jit(solution)/shard_map/ppermute | solution.py:209
  22.9 1.4 %collective-permute-start.10 = (f32[2,128,128]{2,1,0:T(8,128)S(1)}, f32[2,128,128]{2,1,0:T(8,128)S(1)}, u32[]{:S(2)}, u32[]{:S(2)}) collective-permute-start(f32[2,128,128]{2,1,0:T(8,128)S(1)} %add_select_fusion), channel_id=1, source_target_pairs={{0,2},{1,9},{2,0},{3,11},{4,6},{5,13},{6,4},{7,15},{8,10},{9,1},{1... | collective-permute-start | bytes 393224 | tf_op jit(solution)/shard_map/ppermute | solution.py:209
  24.3 1.4 %intra.1 = (bf16[128,1024]{1,0:T(8,128)(2,1)S(1)}, f32[128,1024]{1,0:T(8,128)S(1)}, f32[1,1024]{1,0:T(1,128)S(1)}) custom-call(bf16[128,1024]{1,0:T(8,128)(2,1)S(1)} %copy-done, bf16[128,1024]{1,0:T(8,128)(2,1)S(1)} %get-tuple-element.14.k_ref, bf16[128,1024]{1,0:T(8,128)(2,1)S(1)} %get-tuple-element.15.v_ref, f32[1,1024]{1,0:T(1,128)S(1)} %bitcast.2, ...), custom_call_target="tpu_custom_call" | custom-call | flops 67108864 | bytes 1572864 | tf_op jit(solution)/shard_map/intra/pallas_call | solution.py:233
  25.6 0.7 %collective-permute-done.12 = f32[2,128,128]{2,1,0:T(8,128)S(1)} collective-permute-done((f32[2,128,128]{2,1,0:T(8,128)S(1)}, f32[2,128,128]{2,1,0:T(8,128)S(1)}, u32[]{:S(2)}, u32[]{:S(2)}) %collective-permute-start.12) | collective-permute-done | bytes 131104 | tf_op jit(solution)/shard_map/ppermute | solution.py:209
  26.3 0.9 %collective-permute-start.13 = (f32[2,128,128]{2,1,0:T(8,128)S(1)}, f32[2,128,128]{2,1,0:T(8,128)S(1)}, u32[]{:S(2)}, u32[]{:S(2)}) collective-permute-start(f32[2,128,128]{2,1,0:T(8,128)S(1)} %get-tuple-element.26), channel_id=1, source_target_pairs={{0,1},{1,0},{2,3},{3,2},{4,5},{5,4},{6,7},{7,6},{8,9},{9,8},{10,11... | collective-permute-start | bytes 393224 | tf_op jit(solution)/shard_map/ppermute | solution.py:187
  27.2 0.7 %collective-permute-done.10 = f32[2,128,128]{2,1,0:T(8,128)S(1)} collective-permute-done((f32[2,128,128]{2,1,0:T(8,128)S(1)}, f32[2,128,128]{2,1,0:T(8,128)S(1)}, u32[]{:S(2)}, u32[]{:S(2)}) %collective-permute-start.10) | collective-permute-done | bytes 131104 | tf_op jit(solution)/shard_map/ppermute | solution.py:209
  27.9 0.5 %collective-permute-start.11 = (f32[2,128,128]{2,1,0:T(8,128)S(1)}, f32[2,128,128]{2,1,0:T(8,128)S(1)}, u32[]{:S(2)}, u32[]{:S(2)}) collective-permute-start(f32[2,128,128]{2,1,0:T(8,128)S(1)} %get-tuple-element.24), channel_id=1, source_target_pairs={{0,1},{1,0},{2,3},{3,2},{4,5},{5,4},{6,7},{7,6},{8,9},{9,8},{10,11... | collective-permute-start | bytes 393224 | tf_op jit(solution)/shard_map/ppermute | solution.py:187
  28.5 0.3 %attend_early.1.refs_1_ = bf16[3,128,256]{2,1,0:T(8,128)(2,1)S(1)} custom-call(s32[1]{0:T(128)} %bitcast.core_ref, bf16[128,1024]{1,0:T(8,128)(2,1)S(1)} %get-tuple-element.18.fq_ref, f32[128,1024]{1,0:T(8,128)S(1)} %get-tuple-element.19.intra_ref, f32[1,1024]{1,0:T(1,128)S(1)} %get-tuple-element.20.gain_ref, f32[2,128,128]{2,1,0:T(8,128)S(1)} %get-tuple-element.25.refs_0_, ...), custom_call_target="tpu_custom_call" | custom-call | flops 25165824 | bytes 393216 | tf_op jit(solution)/shard_map/attend_early/pallas_call | solution.py:258
  28.9 0.6 %collective-permute-done.11 = f32[2,128,128]{2,1,0:T(8,128)S(1)} collective-permute-done((f32[2,128,128]{2,1,0:T(8,128)S(1)}, f32[2,128,128]{2,1,0:T(8,128)S(1)}, u32[]{:S(2)}, u32[]{:S(2)}) %collective-permute-start.11) | collective-permute-done | bytes 131104 | tf_op jit(solution)/shard_map/ppermute | solution.py:187
  29.5 0.9 %attend_last.1 = bf16[128,1024]{1,0:T(8,128)(2,1)} custom-call(s32[1]{0:T(128)} %bitcast.core_ref, bf16[128,1024]{1,0:T(8,128)(2,1)S(1)} %get-tuple-element.18.fq_ref, f32[128,1024]{1,0:T(8,128)S(1)} %get-tuple-element.19.intra_ref, f32[1,1024]{1,0:T(1,128)S(1)} %get-tuple-element.20.gain_ref, f32[2,128,128]{2,1,0:T(8,128)S(1)} %select_add_fusion.4.refs_0_, ...), custom_call_target="tpu_custom_call" | custom-call | flops 8388608 | bytes 131072 | tf_op jit(solution)/shard_map/attend_last/pallas_call | solution.py:267
  (29 shorter events, 0.9 us)
Async XLA Ops:
  1.3 1.5 %collective-permute-start = (f32[2,128,128]{2,1,0:T(8,128)S(1)}, f32[2,128,128]{2,1,0:T(8,128)S(1)}, u32[]{:S(2)}, u32[]{:S(2)}) collective-permute-start(f32[2,128,128]{2,1,0:T(8,128)S(1)} %get-tuple-element.17), channel_id=1, source_target_pairs={{0,1},{1,0},{2,3},{3,2},{4,5},{5,4},{6,7},{7,6},{8,9},{9,8},{10,11... | collective-permute-start | bytes 393224 | tf_op jit(solution)/shard_map/ppermute | solution.py:187
  1.8 4.0 %collective-permute-start.5 = (f32[2,128,128]{2,1,0:T(8,128)S(1)}, f32[2,128,128]{2,1,0:T(8,128)S(1)}, u32[]{:S(2)}, u32[]{:S(2)}) collective-permute-start(f32[2,128,128]{2,1,0:T(8,128)S(1)} %get-tuple-element.22), channel_id=1, source_target_pairs={{0,1},{1,0},{2,3},{3,2},{4,5},{5,4},{6,7},{7,6},{8,9},{9,8},{10,11... | collective-permute-start | bytes 393224 | tf_op jit(solution)/shard_map/ppermute | solution.py:187
  2.8 5.9 %collective-permute-start.1 = (f32[2,128,128]{2,1,0:T(8,128)S(1)}, f32[2,128,128]{2,1,0:T(8,128)S(1)}, u32[]{:S(2)}, u32[]{:S(2)}) collective-permute-start(f32[2,128,128]{2,1,0:T(8,128)S(1)} %add.137), channel_id=1, source_target_pairs={{0,2},{1,9},{2,0},{3,11},{4,6},{5,13},{6,4},{7,15},{8,10},{9,1},{1... | collective-permute-start | bytes 393224 | tf_op jit(solution)/shard_map/ppermute | solution.py:209
  5.8 5.0 %collective-permute-start.6 = (f32[2,128,128]{2,1,0:T(8,128)S(1)}, f32[2,128,128]{2,1,0:T(8,128)S(1)}, u32[]{:S(2)}, u32[]{:S(2)}) collective-permute-start(f32[2,128,128]{2,1,0:T(8,128)S(1)} %get-tuple-element.29), channel_id=1, source_target_pairs={{0,2},{1,17},{2,0},{3,19},{4,6},{5,21},{6,4},{7,23},{8,10},{9,25},... | collective-permute-start | bytes 393224 | tf_op jit(solution)/shard_map/ppermute | solution.py:209
  8.7 5.0 %collective-permute-start.2 = (f32[2,128,128]{2,1,0:T(8,128)S(1)}, f32[2,128,128]{2,1,0:T(8,128)S(1)}, u32[]{:S(2)}, u32[]{:S(2)}) collective-permute-start(f32[2,128,128]{2,1,0:T(8,128)S(1)} %add.138), channel_id=1, source_target_pairs={{0,4},{1,17},{2,6},{3,19},{4,0},{5,21},{6,2},{7,23},{8,12},{9,25},... | collective-permute-start | bytes 393224 | tf_op jit(solution)/shard_map/ppermute | solution.py:209
  10.8 5.0 %collective-permute-start.7 = (f32[2,128,128]{2,1,0:T(8,128)S(1)}, f32[2,128,128]{2,1,0:T(8,128)S(1)}, u32[]{:S(2)}, u32[]{:S(2)}) collective-permute-start(f32[2,128,128]{2,1,0:T(8,128)S(1)} %get-tuple-element.27), channel_id=1, source_target_pairs={{0,4},{1,9},{2,6},{3,11},{4,0},{5,13},{6,2},{7,15},{8,12},{9,1},{1... | collective-permute-start | bytes 393224 | tf_op jit(solution)/shard_map/ppermute | solution.py:209
  13.8 2.3 %collective-permute-start.3 = (f32[4,128,128]{2,1,0:T(8,128)S(1)}, f32[4,128,128]{2,1,0:T(8,128)S(1)}, u32[]{:S(2)}, u32[]{:S(2)}) collective-permute-start(f32[4,128,128]{2,1,0:T(8,128)S(1)} %pad_maximum_fusion), channel_id=1, source_target_pairs={{0,1},{1,0},{2,3},{3,2},{4,5},{5,4},{6,7},{7,6},{8,9},{9,8},{10,11... | collective-permute-start | bytes 786440 | tf_op jit(solution)/shard_map/ppermute | solution.py:187
  15.9 1.8 %collective-permute-start.8 = (f32[4,128,128]{2,1,0:T(8,128)S(1)}, f32[4,128,128]{2,1,0:T(8,128)S(1)}, u32[]{:S(2)}, u32[]{:S(2)}) collective-permute-start(f32[4,128,128]{2,1,0:T(8,128)S(1)} %pad_maximum_fusion.1), channel_id=1, source_target_pairs={{0,1},{1,0},{2,3},{3,2},{4,5},{5,4},{6,7},{7,6},{8,9},{9,8},{10,11... | collective-permute-start | bytes 786440 | tf_op jit(solution)/shard_map/ppermute | solution.py:187
  16.2 5.0 %collective-permute-start.4 = (f32[2,128,128]{2,1,0:T(8,128)S(1)}, f32[2,128,128]{2,1,0:T(8,128)S(1)}, u32[]{:S(2)}, u32[]{:S(2)}) collective-permute-start(f32[2,128,128]{2,1,0:T(8,128)S(1)} %add_select_fusion.6), channel_id=1, source_target_pairs={{0,4},{1,9},{2,6},{3,11},{4,0},{5,13},{6,2},{7,15},{8,12},{9,1},{1... | collective-permute-start | bytes 393224 | tf_op jit(solution)/shard_map/ppermute | solution.py:209
  17.8 5.0 %collective-permute-start.9 = (f32[2,128,128]{2,1,0:T(8,128)S(1)}, f32[2,128,128]{2,1,0:T(8,128)S(1)}, u32[]{:S(2)}, u32[]{:S(2)}) collective-permute-start(f32[2,128,128]{2,1,0:T(8,128)S(1)} %add_select_fusion.1), channel_id=1, source_target_pairs={{0,4},{1,17},{2,6},{3,19},{4,0},{5,21},{6,2},{7,23},{8,12},{9,25},... | collective-permute-start | bytes 393224 | tf_op jit(solution)/shard_map/ppermute | solution.py:209
  21.2 3.0 %copy-start = (bf16[128,1024]{1,0:T(8,128)(2,1)S(1)}, bf16[128,1024]{1,0:T(8,128)(2,1)}, u32[]{:S(2)}) copy-start(bf16[128,1024]{1,0:T(8,128)(2,1)} %q_ref.1) | copy-start | bytes 786436
  21.3 5.0 %collective-permute-start.12 = (f32[2,128,128]{2,1,0:T(8,128)S(1)}, f32[2,128,128]{2,1,0:T(8,128)S(1)}, u32[]{:S(2)}, u32[]{:S(2)}) collective-permute-start(f32[2,128,128]{2,1,0:T(8,128)S(1)} %add_select_fusion.5.late_ref), channel_id=1, source_target_pairs={{0,2},{1,17},{2,0},{3,19},{4,6},{5,21},{6,4},{7,23},{8,10},{9,25},... | collective-permute-start | bytes 393224 | tf_op jit(solution)/shard_map/ppermute | solution.py:209
  22.8 1.4 %copy-start.1 = (f32[1024]{0:T(1024)S(1)}, f32[1024]{0:T(1024)}, u32[]{:S(2)}) copy-start(f32[1024]{0:T(1024)} %param.7) | copy-start | bytes 12292
  22.9 5.0 %collective-permute-start.10 = (f32[2,128,128]{2,1,0:T(8,128)S(1)}, f32[2,128,128]{2,1,0:T(8,128)S(1)}, u32[]{:S(2)}, u32[]{:S(2)}) collective-permute-start(f32[2,128,128]{2,1,0:T(8,128)S(1)} %add_select_fusion), channel_id=1, source_target_pairs={{0,2},{1,9},{2,0},{3,11},{4,6},{5,13},{6,4},{7,15},{8,10},{9,1},{1... | collective-permute-start | bytes 393224 | tf_op jit(solution)/shard_map/ppermute | solution.py:209
  26.3 2.2 %collective-permute-start.13 = (f32[2,128,128]{2,1,0:T(8,128)S(1)}, f32[2,128,128]{2,1,0:T(8,128)S(1)}, u32[]{:S(2)}, u32[]{:S(2)}) collective-permute-start(f32[2,128,128]{2,1,0:T(8,128)S(1)} %get-tuple-element.26), channel_id=1, source_target_pairs={{0,1},{1,0},{2,3},{3,2},{4,5},{5,4},{6,7},{7,6},{8,9},{9,8},{10,11... | collective-permute-start | bytes 393224 | tf_op jit(solution)/shard_map/ppermute | solution.py:187
  27.9 1.5 %collective-permute-start.11 = (f32[2,128,128]{2,1,0:T(8,128)S(1)}, f32[2,128,128]{2,1,0:T(8,128)S(1)}, u32[]{:S(2)}, u32[]{:S(2)}) collective-permute-start(f32[2,128,128]{2,1,0:T(8,128)S(1)} %get-tuple-element.24), channel_id=1, source_target_pairs={{0,1},{1,0},{2,3},{3,2},{4,5},{5,4},{6,7},{7,6},{8,9},{9,8},{10,11... | collective-permute-start | bytes 393224 | tf_op jit(solution)/shard_map/ppermute | solution.py:187
